TPU v7x, 32 devices: a whole 2x2x4 slice. The times are simulated.
32 devices in a mesh: group: 2 (over y), ctx: 8 (over z, x), tp: 2 (over core).
Axes of the slice: x: 2, y: 2, z: 4, core: 2. Of those that a mesh axis runs over, the one named last changes fastest.
Arguments:
- queries: bfloat16 [4096, 4096], P(('group', 'ctx', 'tp')), parts along dimension 0, may hold values from -100 to 100
- keys: bfloat16 [4096, 2048], P(('group', 'ctx', 'tp')), parts along dimension 0, may hold values from -6 to 6
- values: bfloat16 [4096, 2048], P(('group', 'ctx', 'tp')), parts along dimension 0, may hold values from -6 to 6
- output_gradient: bfloat16 [4096, 4096], P(('group', 'ctx', 'tp')), parts along dimension 0, may hold values from -6 to 6
Outputs:
- attended: bfloat16 [4096, 4096], P(('group', 'ctx', 'tp')), parts along dimension 0
- query_grad: bfloat16 [4096, 4096], P(('group', 'ctx', 'tp')), parts along dimension 0
- key_gradient: bfloat16 [4096, 2048], P(('group', 'ctx', 'tp')), parts along dimension 0
- value_gradient: bfloat16 [4096, 2048], P(('group', 'ctx', 'tp')), parts along dimension 0
There are 2 independent parts, one for each index of `group`. A program takes and returns all parts, laid end to end along the dimension named above; each array names one. Nothing has to cross between parts.
All inputs are finite; a program needn't handle non-finite values.
Results may differ from a plain program's by a relative error of at most 0.02.
Values may be sent and summed in bfloat16 or wider, within the bound.
No kernel may reach another device: no remote copies, remote signals or barrier semaphores. Data moves between devices by JAX's collectives and lax.ppermute only.
A program may use at most 64 MiB of HBM per device.

v0:
```python
import jax
import jax.numpy as jnp
from jax import lax
from jax.sharding import PartitionSpec as P

HEAD_SIZE = 128
WINDOW_TOKENS = 1024


score_scale = 1.0 / 12.0
softcap_value = 50.0


def shifted(array, axis, by):
    length = lax.axis_size(axis)
    pairs = [(i, i + by) for i in range(length) if 0 <= i + by < length]
    return lax.ppermute(array, axis, pairs)


def to_query_heads(block, kv_heads):
    block_rows = block.shape[0]
    return block.reshape(block_rows, kv_heads, -1, HEAD_SIZE).transpose(1, 2, 0, 3)


def to_key_heads(block, kv_heads):
    block_rows = block.shape[0]
    return block.reshape(block_rows, kv_heads, HEAD_SIZE).transpose(1, 0, 2)


def from_query_heads(heads):
    return heads.transpose(2, 0, 1, 3).reshape(heads.shape[2], -1)


def from_key_heads(heads):
    return heads.transpose(1, 0, 2).reshape(heads.shape[1], -1)


def band_mask(query_pos, key_pos, seq_total):
    return (
        (key_pos[None, :] <= query_pos[:, None])
        & (key_pos[None, :] > query_pos[:, None] - WINDOW_TOKENS)
        & (key_pos[None, :] >= 0)
        & (query_pos[:, None] < seq_total)
    )


def capped_scores(query_head, key_head):
    score = (
        jnp.einsum("gqd,kd->gqk", query_head, key_head, preferred_element_type=jnp.float32)
        * score_scale
    )
    return softcap_value * jnp.tanh(score / softcap_value)


def forward_head(query_head, key_head, value_head, allowed):
    capped = capped_scores(query_head, key_head)
    expo = jnp.where(allowed, jnp.exp(capped), 0.0)
    normalizer = jnp.sum(expo, axis=-1)
    probs = (expo / normalizer[..., None]).astype(jnp.bfloat16)
    attended = jnp.einsum(
        "gqk,kd->gqd", probs, value_head, preferred_element_type=jnp.float32
    ).astype(jnp.bfloat16)
    return (attended, normalizer)


def score_grads(query_head, grad_head, normalizer, grad_dot, key_head, value_head, allowed):
    capped = capped_scores(query_head, key_head)
    expo = jnp.where(allowed, jnp.exp(capped), 0.0)
    weights = expo / normalizer[..., None]
    dprob = jnp.einsum("gqd,kd->gqk", grad_head, value_head, preferred_element_type=jnp.float32)
    dscore = (
        weights
        * (dprob - grad_dot[..., None])
        * (1.0 - (capped / softcap_value) ** 2)
        * score_scale
    ).astype(jnp.bfloat16)
    return (weights.astype(jnp.bfloat16), dscore)


def join_blocks(pieces):
    return jax.tree.map(lambda *members: jnp.concatenate(members, axis=1), *pieces)


def reach_back(payload, reach_depth):
    pieces = []
    current = payload
    for hop_index in range(reach_depth):
        current = shifted(current, "ctx", 1)
        pieces.insert(0, current)
    joined = join_blocks(pieces)
    return joined


def send_back(partials, reach_depth):
    block_rows = partials.shape[1] // reach_depth
    carried = partials[:, :block_rows]
    for hop_index in range(reach_depth):
        carried = shifted(carried.astype(jnp.bfloat16), "ctx", -1).astype(carried.dtype)
        if hop_index + 1 < reach_depth:
            carried = (
                carried + partials[:, (hop_index + 1) * block_rows : (hop_index + 2) * block_rows]
            )
    return carried


def on_device(queries, keys, values, output_gradient):
    query_block, key_block, value_block, grad_block = (
        lax.all_to_all(queries, "tp", split_axis=1, concat_axis=0, tiled=True),
        lax.all_to_all(keys, "tp", split_axis=1, concat_axis=0, tiled=True),
        lax.all_to_all(values, "tp", split_axis=1, concat_axis=0, tiled=True),
        lax.all_to_all(output_gradient, "tp", split_axis=1, concat_axis=0, tiled=True),
    )
    block_rows = query_block.shape[0]
    kv_heads = key_block.shape[1] // HEAD_SIZE
    reach_depth = max(1, WINDOW_TOKENS // block_rows)
    seq_total = lax.axis_size("ctx") * block_rows
    first_row = lax.axis_index("ctx") * block_rows
    query_pos = first_row + jnp.arange(block_rows, dtype=jnp.int32)
    key_pos = first_row - WINDOW_TOKENS + jnp.arange(WINDOW_TOKENS + block_rows, dtype=jnp.int32)
    own_pair = jnp.stack([key_block, value_block])
    halo_pair = reach_back(own_pair, reach_depth)
    all_pair = jnp.concatenate([halo_pair, own_pair], axis=1)
    heads_of_keys = to_key_heads(all_pair[0], kv_heads)
    heads_of_values = to_key_heads(all_pair[1], kv_heads)
    heads_of_queries = to_query_heads(query_block, kv_heads)
    gradient_heads = to_query_heads(grad_block, kv_heads)
    allowed = band_mask(query_pos, key_pos, seq_total)
    attended_heads, normalizer = lax.map(
        lambda members: forward_head(members[0], members[1], members[2], allowed),
        (heads_of_queries, heads_of_keys, heads_of_values),
    )
    grad_dot = jnp.sum(
        gradient_heads.astype(jnp.float32) * attended_heads.astype(jnp.float32), axis=-1
    )

    def full_grads(members):
        weights, dscore = score_grads(
            members[0], members[1], members[2], members[3], members[4], members[5], allowed
        )
        query_part = jnp.einsum(
            "gqk,kd->gqd", dscore, members[4], preferred_element_type=jnp.float32
        ).astype(jnp.bfloat16)
        key_part = jnp.einsum("gqk,gqd->kd", dscore, members[0], preferred_element_type=jnp.float32)
        value_part = jnp.einsum(
            "gqk,gqd->kd", weights, members[1], preferred_element_type=jnp.float32
        )
        return (query_part, key_part, value_part)

    dquery_heads, dkey_heads, dvalue_heads = lax.map(
        full_grads,
        (heads_of_queries, gradient_heads, normalizer, grad_dot, heads_of_keys, heads_of_values),
    )
    pair_grads = jnp.stack([from_key_heads(dkey_heads), from_key_heads(dvalue_heads)])
    tail_grads = pair_grads[:, WINDOW_TOKENS:]
    summed = send_back(pair_grads[:, :WINDOW_TOKENS], reach_depth)
    keep_rows = block_rows - summed.shape[1]
    own_grads = jnp.concatenate([tail_grads[:, :keep_rows], tail_grads + summed], axis=1)
    key_grad_block = own_grads[0].astype(jnp.bfloat16)
    value_grad_block = own_grads[1].astype(jnp.bfloat16)
    attended_block = from_query_heads(attended_heads)
    dquery_block = from_query_heads(dquery_heads)
    attended, query_grad, key_gradient, value_gradient = (
        lax.all_to_all(attended_block, "tp", split_axis=0, concat_axis=1, tiled=True),
        lax.all_to_all(dquery_block, "tp", split_axis=0, concat_axis=1, tiled=True),
        lax.all_to_all(key_grad_block, "tp", split_axis=0, concat_axis=1, tiled=True),
        lax.all_to_all(value_grad_block, "tp", split_axis=0, concat_axis=1, tiled=True),
    )
    return (attended, query_grad, key_gradient, value_gradient)


def solution(mesh):
    placed = (
        P(("group", "ctx", "tp"), None),
        P(("group", "ctx", "tp"), None),
        P(("group", "ctx", "tp"), None),
        P(("group", "ctx", "tp"), None),
    )
    return jax.shard_map(
        on_device,
        mesh=mesh,
        in_specs=placed,
        out_specs=(
            P(("group", "ctx", "tp"), None),
            P(("group", "ctx", "tp"), None),
            P(("group", "ctx", "tp"), None),
            P(("group", "ctx", "tp"), None),
        ),
        check_vma=False,
    )
```

profile of v0, /device:TPU:0, one launch (start us, length us, event | category | flops | bytes accessed | tf_op | source)
XLA Modules:
  0.0 377.4 jit_solution(17163447129338836667)
XLA Ops:
  2.7 3.5 all-to-all-start.1
  8.2 3.6 all-to-all-start.2
  13.9 4.9 %collective-permute-start = (bf16[2,256,1024]{2,1,0:T(8,128)(2,1)S(1)}, bf16[2,256,1024]{2,1,0:T(8,128)(2,1)S(1)}, u32[]{:S(2)}, u32[]{:S(2)}) collective-permute-start(bf16[2,256,1024]{2,1,0:T(8,128)(2,1)S(1)} %pad_maximum_fusion.1), channel_id=1, source_target_pairs={{0,2},{2,4},{4,6},{6,8},{8,10},{10,12},{12,14},{1,3},{3,5},{5,7},{... | collective-permute-start | bytes 3145736 | tf_op jit(solution)/shard_map/ppermute | solution.py:17
  18.8 22.6 %collective-permute-done = bf16[2,256,1024]{2,1,0:T(8,128)(2,1)S(1)} collective-permute-done((bf16[2,256,1024]{2,1,0:T(8,128)(2,1)S(1)}, bf16[2,256,1024]{2,1,0:T(8,128)(2,1)S(1)}, u32[]{:S(2)}, u32[]{:S(2)}) %collective-permute-start) | collective-permute-done | bytes 1048608 | tf_op jit(solution)/shard_map/ppermute | solution.py:17
  42.4 4.4 %collective-permute-start.1 = (bf16[2,256,1024]{2,1,0:T(8,128)(2,1)S(1)}, bf16[2,256,1024]{2,1,0:T(8,128)(2,1)S(1)}, u32[]{:S(2)}, u32[]{:S(2)}) collective-permute-start(bf16[2,256,1024]{2,1,0:T(8,128)(2,1)S(1)} %collective-permute-done), channel_id=1, source_target_pairs={{0,2},{2,4},{4,6},{6,8},{8,10},{10,12},{12,14},{1,3},{3,5},{5,7},{... | collective-permute-start | bytes 3145736 | tf_op jit(solution)/shard_map/ppermute | solution.py:17
  46.9 21.8 %collective-permute-done.1 = bf16[2,256,1024]{2,1,0:T(8,128)(2,1)S(1)} collective-permute-done((bf16[2,256,1024]{2,1,0:T(8,128)(2,1)S(1)}, bf16[2,256,1024]{2,1,0:T(8,128)(2,1)S(1)}, u32[]{:S(2)}, u32[]{:S(2)}) %collective-permute-start.1) | collective-permute-done | bytes 1048608 | tf_op jit(solution)/shard_map/ppermute | solution.py:17
  69.7 5.4 %collective-permute-start.2 = (bf16[2,256,1024]{2,1,0:T(8,128)(2,1)S(1)}, bf16[2,256,1024]{2,1,0:T(8,128)(2,1)}, u32[]{:S(2)}, u32[]{:S(2)}) collective-permute-start(bf16[2,256,1024]{2,1,0:T(8,128)(2,1)S(1)} %collective-permute-done.1), channel_id=1, source_target_pairs={{0,2},{2,4},{4,6},{6,8},{8,10},{10,12},{12,14},{1,3},{3,5},{5,7},{... | collective-permute-start | bytes 3145736 | tf_op jit(solution)/shard_map/ppermute | solution.py:17
  75.1 19.9 %collective-permute-done.2 = bf16[2,256,1024]{2,1,0:T(8,128)(2,1)} collective-permute-done((bf16[2,256,1024]{2,1,0:T(8,128)(2,1)S(1)}, bf16[2,256,1024]{2,1,0:T(8,128)(2,1)}, u32[]{:S(2)}, u32[]{:S(2)}) %collective-permute-start.2) | collective-permute-done | bytes 1048608 | tf_op jit(solution)/shard_map/ppermute | solution.py:17
  95.0 6.2 %collective-permute-start.3 = (bf16[2,256,1024]{2,1,0:T(8,128)(2,1)}, bf16[2,256,1024]{2,1,0:T(8,128)(2,1)}, u32[]{:S(2)}, u32[]{:S(2)}) collective-permute-start(bf16[2,256,1024]{2,1,0:T(8,128)(2,1)} %collective-permute-done.2), channel_id=1, source_target_pairs={{0,2},{2,4},{4,6},{6,8},{8,10},{10,12},{12,14},{1,3},{3,5},{5,7},{... | collective-permute-start | bytes 3145736 | tf_op jit(solution)/shard_map/ppermute | solution.py:17
  102.3 3.6 all-to-all-start
  108.3 3.6 all-to-all-start.4
  125.8 4.4 %copy.103 = bf16[1,1280,1024]{1,2,0:T(8,128)(2,1)} copy(bf16[1,1280,1024]{2,1,0:T(8,128)(2,1)} %get-tuple-element.477) | data formatting | bytes 5242880 | tf_op jit(solution)/shard_map/slice | solution.py:124
  130.2 4.5 %copy.106 = bf16[8,1280,128]{2,1,0:T(8,128)(2,1)} copy(bf16[8,1280,128]{1,2,0:T(8,128)(2,1)} %bitcast.157) | data formatting | bytes 5242880
  137.4 3.2 copy.105
  141.8 37.3 %while.32 = (s32[]{:T(128)}, bf16[8,2,256,128]{3,2,1,0:T(8,128)(2,1)}, f32[8,2,256]{2,1,0:T(2,128)S(1)}, bf16[8,2,256,128]{3,2,1,0:T(8,128)(2,1)}, bf16[8,1280,1...) while((s32[]{:T(128)}, ...), condition=%wide.region_2.3_spmd.clone, body=%wide.region_0.2_spmd.clone.sunk | while | flops 341179904 | bytes 6834817 | solution.py:128
  182.4 82.3 %while.33 = (s32[]{:T(128)}, bf16[8,2,256,128]{3,2,1,0:T(8,128)(2,1)}, f32[8,1280,128]{1,2,0:T(8,128)}, f32[8,1280,128]{1,2,0:T(8,128)}, bf16[8,2,256,128]{3,2,1...) while((s32[]{:T(128)}, ...), condition=%wide.region_5.6_spmd.clone, body=%wide.region_4.5_spmd.clone.sunk | while | flops 850395136 | bytes 15756961 | solution.py:149
  268.1 24.6 %collective-permute-done.4 = bf16[2,256,1024]{1,2,0:T(8,128)(2,1)S(1)} collective-permute-done((bf16[2,256,1024]{1,2,0:T(8,128)(2,1)S(1)}, bf16[2,256,1024]{1,2,0:T(8,128)(2,1)S(1)}, u32[]{:S(2)}, u32[]{:S(2)}) %collective-permute-start.4) | collective-permute-done | bytes 1048608 | tf_op jit(solution)/shard_map/ppermute | solution.py:17
  294.3 22.7 %collective-permute-done.5 = bf16[2,256,1024]{1,2,0:T(8,128)(2,1)S(1)} collective-permute-done((bf16[2,256,1024]{1,2,0:T(8,128)(2,1)S(1)}, bf16[2,256,1024]{1,2,0:T(8,128)(2,1)S(1)}, u32[]{:S(2)}, u32[]{:S(2)}) %collective-permute-start.5) | collective-permute-done | bytes 1048608 | tf_op jit(solution)/shard_map/ppermute | solution.py:17
  318.8 21.5 %collective-permute-done.6 = bf16[2,256,1024]{1,2,0:T(8,128)(2,1)S(1)} collective-permute-done((bf16[2,256,1024]{1,2,0:T(8,128)(2,1)S(1)}, bf16[2,256,1024]{1,2,0:T(8,128)(2,1)S(1)}, u32[]{:S(2)}, u32[]{:S(2)}) %collective-permute-start.6) | collective-permute-done | bytes 1048608 | tf_op jit(solution)/shard_map/ppermute | solution.py:17
  345.0 4.6 %all_to_all.134 = bf16[2,128,2048]{2,1,0:T(8,128)(2,1)S(1)} all-to-all(bf16[2,128,2048]{2,1,0:T(8,128)(2,1)S(1)} %all_to_all.109), channel_id=1, replica_groups=mesh['group'=2,'ctx'=8,'tp'=2] {'tp'}, dimensions={0} | all-to-all | bytes 2097152 | tf_op jit(solution)/shard_map/all_to_all | solution.py:163
  353.5 4.6 %all_to_all.135 = bf16[2,128,2048]{2,1,0:T(8,128)(2,1)S(1)} all-to-all(bf16[2,128,2048]{2,1,0:T(8,128)(2,1)S(1)} %all_to_all.116), channel_id=1, replica_groups=mesh['group'=2,'ctx'=8,'tp'=2] {'tp'}, dimensions={0} | all-to-all | bytes 2097152 | tf_op jit(solution)/shard_map/all_to_all | solution.py:164
  360.0 3.8 %collective-permute-done.7 = bf16[2,256,1024]{1,2,0:T(8,128)(2,1)} collective-permute-done((bf16[2,256,1024]{1,2,0:T(8,128)(2,1)}, bf16[2,256,1024]{1,2,0:T(8,128)(2,1)}, u32[]{:S(2)}, u32[]{:S(2)}) %collective-permute-start.7) | collective-permute-done | bytes 1048608 | tf_op jit(solution)/shard_map/ppermute | solution.py:17
  366.3 4.2 %all_to_all.136 = bf16[2,128,1024]{2,1,0:T(8,128)(2,1)S(1)} all-to-all(bf16[2,128,1024]{2,1,0:T(8,128)(2,1)S(1)} %bitcast.174), channel_id=1, replica_groups=mesh['group'=2,'ctx'=8,'tp'=2] {'tp'}, dimensions={0} | all-to-all | bytes 1048576 | tf_op jit(solution)/shard_map/all_to_all | solution.py:166
  371.9 4.2 %all_to_all.137 = bf16[2,128,1024]{2,1,0:T(8,128)(2,1)S(1)} all-to-all(bf16[2,128,1024]{2,1,0:T(8,128)(2,1)S(1)} %bitcast.177), channel_id=1, replica_groups=mesh['group'=2,'ctx'=8,'tp'=2] {'tp'}, dimensions={0} | all-to-all | bytes 1048576 | tf_op jit(solution)/shard_map/all_to_all | solution.py:165
  (168 shorter events, 174.3 us)
Async XLA Ops:
  2.7 5.5 %all-to-all-start.1 = ((bf16[128,2,1024]{0,2,1:T(8,128)(2,1)}), bf16[128,2,1024]{0,2,1:T(8,128)(2,1)S(1)}, u32[]{:S(2)}, u32[]{:S(2)}) async-start(bf16[128,2,1024]{0,2,1:T(8,128)(2,1)} %bitcast.2), calls=%async_computation.1 | async-start | bytes 1048576 | tf_op jit(solution)/shard_map/all_to_all | solution.py:109
  8.2 93.1 %copy-start.4 = (bf16[128,4096]{1,0:T(8,128)(2,1)S(1)}, bf16[128,4096]{1,0:T(8,128)(2,1)}, u32[]{:S(2)}) copy-start(bf16[128,4096]{1,0:T(8,128)(2,1)} %param.8) | copy-start | bytes 3145732
  8.2 5.4 %all-to-all-start.2 = ((bf16[128,2,1024]{0,2,1:T(8,128)(2,1)}), bf16[128,2,1024]{0,2,1:T(8,128)(2,1)S(1)}, u32[]{:S(2)}, u32[]{:S(2)}) async-start(bf16[128,2,1024]{0,2,1:T(8,128)(2,1)} %bitcast.5), calls=%async_computation.2 | async-start | bytes 1048576 | tf_op jit(solution)/shard_map/all_to_all | solution.py:110
  13.9 27.6 %collective-permute-start = (bf16[2,256,1024]{2,1,0:T(8,128)(2,1)S(1)}, bf16[2,256,1024]{2,1,0:T(8,128)(2,1)S(1)}, u32[]{:S(2)}, u32[]{:S(2)}) collective-permute-start(bf16[2,256,1024]{2,1,0:T(8,128)(2,1)S(1)} %pad_maximum_fusion.1), channel_id=1, source_target_pairs={{0,2},{2,4},{4,6},{6,8},{8,10},{10,12},{12,14},{1,3},{3,5},{5,7},{... | collective-permute-start | bytes 3145736 | tf_op jit(solution)/shard_map/ppermute | solution.py:17
  41.5 1.0 copy-start.5
  42.4 26.3 %collective-permute-start.1 = (bf16[2,256,1024]{2,1,0:T(8,128)(2,1)S(1)}, bf16[2,256,1024]{2,1,0:T(8,128)(2,1)S(1)}, u32[]{:S(2)}, u32[]{:S(2)}) collective-permute-start(bf16[2,256,1024]{2,1,0:T(8,128)(2,1)S(1)} %collective-permute-done), channel_id=1, source_target_pairs={{0,2},{2,4},{4,6},{6,8},{8,10},{10,12},{12,14},{1,3},{3,5},{5,7},{... | collective-permute-start | bytes 3145736 | tf_op jit(solution)/shard_map/ppermute | solution.py:17
  68.7 1.0 copy-start.7
  69.7 25.3 %collective-permute-start.2 = (bf16[2,256,1024]{2,1,0:T(8,128)(2,1)S(1)}, bf16[2,256,1024]{2,1,0:T(8,128)(2,1)}, u32[]{:S(2)}, u32[]{:S(2)}) collective-permute-start(bf16[2,256,1024]{2,1,0:T(8,128)(2,1)S(1)} %collective-permute-done.1), channel_id=1, source_target_pairs={{0,2},{2,4},{4,6},{6,8},{8,10},{10,12},{12,14},{1,3},{3,5},{5,7},{... | collective-permute-start | bytes 3145736 | tf_op jit(solution)/shard_map/ppermute | solution.py:17
  95.0 25.6 %collective-permute-start.3 = (bf16[2,256,1024]{2,1,0:T(8,128)(2,1)}, bf16[2,256,1024]{2,1,0:T(8,128)(2,1)}, u32[]{:S(2)}, u32[]{:S(2)}) collective-permute-start(bf16[2,256,1024]{2,1,0:T(8,128)(2,1)} %collective-permute-done.2), channel_id=1, source_target_pairs={{0,2},{2,4},{4,6},{6,8},{8,10},{10,12},{12,14},{1,3},{3,5},{5,7},{... | collective-permute-start | bytes 3145736 | tf_op jit(solution)/shard_map/ppermute | solution.py:17
  102.3 6.0 %all-to-all-start = ((bf16[128,2,2048]{2,0,1:T(8,128)(2,1)}), bf16[128,2,2048]{2,0,1:T(8,128)(2,1)S(1)}, u32[]{:S(2)}, u32[]{:S(2)}) async-start(bf16[128,2,2048]{2,0,1:T(8,128)(2,1)} %bitcast.107), calls=%async_computation | async-start | bytes 2097152 | tf_op jit(solution)/shard_map/all_to_all | solution.py:108
  108.3 7.6 %all-to-all-start.4 = ((bf16[128,2,2048]{2,0,1:T(8,128)(2,1)}), bf16[128,2,2048]{2,0,1:T(8,128)(2,1)S(1)}, u32[]{:S(2)}, u32[]{:S(2)}) async-start(bf16[128,2,2048]{2,0,1:T(8,128)(2,1)} %bitcast.106), calls=%async_computation.4 | async-start | bytes 2097152 | tf_op jit(solution)/shard_map/all_to_all | solution.py:111
  116.7 6.7 %copy-start.1 = (bf16[256,8,2,128]{3,2,1,0:T(2,128)(2,1)}, bf16[256,8,2,128]{3,2,1,0:T(2,128)(2,1)S(1)}, u32[]{:S(2)}) copy-start(bf16[256,8,2,128]{3,2,1,0:T(2,128)(2,1)S(1)} %reshape.76) | copy-start | bytes 3145732
  118.0 5.3 %copy-start.8 = (bf16[2,256,1024]{2,1,0:T(8,128)(2,1)S(1)}, bf16[2,256,1024]{2,1,0:T(8,128)(2,1)}, u32[]{:S(2)}) copy-start(bf16[2,256,1024]{2,1,0:T(8,128)(2,1)} %copy-done.7) | copy-start | bytes 3145732
  121.9 1.5 copy-start.6
  264.7 28.0 %slice-start = ((s8[5242880]{0:T(1024)(128)(4,1)}), s8[4194304]{0:T(1024)(128)(4,1)S(1)}, s32[]{:S(2)}) async-start(s8[5242880]{0:T(1024)(128)(4,1)} %bitcast.147), calls=%async_computation.8 | async-start | bytes 8388608
  264.7 28.0 %slice-start.1 = ((s8[5242880]{0:T(1024)(128)(4,1)}), s8[1048576]{0:T(1024)(128)(4,1)S(1)}, s32[]{:S(2)}) async-start(s8[5242880]{0:T(1024)(128)(4,1)} %bitcast.147), calls=%async_computation.9 | async-start | bytes 2097152
  264.7 28.0 %copy-start = (f32[8,1280,128]{1,2,0:T(8,128)S(1)}, f32[8,1280,128]{1,2,0:T(8,128)}, u32[]{:S(2)}) copy-start(f32[8,1280,128]{1,2,0:T(8,128)} %get-tuple-element.237) | copy-start | bytes 15728644
  266.6 26.1 %collective-permute-start.4 = (bf16[2,256,1024]{1,2,0:T(8,128)(2,1)S(1)}, bf16[2,256,1024]{1,2,0:T(8,128)(2,1)S(1)}, u32[]{:S(2)}, u32[]{:S(2)}) collective-permute-start(bf16[2,256,1024]{1,2,0:T(8,128)(2,1)S(1)} %fusion.65), channel_id=1, source_target_pairs={{2,0},{4,2},{6,4},{8,6},{10,8},{12,10},{14,12},{3,1},{5,3},{7,5},{... | collective-permute-start | bytes 3145736 | tf_op jit(solution)/shard_map/ppermute | solution.py:17
  293.0 24.0 %collective-permute-start.5 = (bf16[2,256,1024]{1,2,0:T(8,128)(2,1)S(1)}, bf16[2,256,1024]{1,2,0:T(8,128)(2,1)S(1)}, u32[]{:S(2)}, u32[]{:S(2)}) collective-permute-start(bf16[2,256,1024]{1,2,0:T(8,128)(2,1)S(1)} %fusion.68), channel_id=1, source_target_pairs={{2,0},{4,2},{6,4},{8,6},{10,8},{12,10},{14,12},{3,1},{5,3},{7,5},{... | collective-permute-start | bytes 3145736 | tf_op jit(solution)/shard_map/ppermute | solution.py:17
  317.3 25.8 %copy-start.2 = (bf16[8,2,256,128]{3,2,1,0:T(8,128)(2,1)S(1)}, bf16[8,2,256,128]{3,2,1,0:T(8,128)(2,1)}, u32[]{:S(2)}) copy-start(bf16[8,2,256,128]{3,2,1,0:T(8,128)(2,1)} %get-tuple-element.234) | copy-start | bytes 3145732
  317.3 23.0 %collective-permute-start.6 = (bf16[2,256,1024]{1,2,0:T(8,128)(2,1)S(1)}, bf16[2,256,1024]{1,2,0:T(8,128)(2,1)S(1)}, u32[]{:S(2)}, u32[]{:S(2)}) collective-permute-start(bf16[2,256,1024]{1,2,0:T(8,128)(2,1)S(1)} %fusion.60), channel_id=1, source_target_pairs={{2,0},{4,2},{6,4},{8,6},{10,8},{12,10},{14,12},{3,1},{5,3},{7,5},{... | collective-permute-start | bytes 3145736 | tf_op jit(solution)/shard_map/ppermute | solution.py:17
  341.6 22.2 %collective-permute-start.7 = (bf16[2,256,1024]{1,2,0:T(8,128)(2,1)}, bf16[2,256,1024]{1,2,0:T(8,128)(2,1)}, u32[]{:S(2)}, u32[]{:S(2)}) collective-permute-start(bf16[2,256,1024]{1,2,0:T(8,128)(2,1)} %fusion.70), channel_id=1, source_target_pairs={{2,0},{4,2},{6,4},{8,6},{10,8},{12,10},{14,12},{3,1},{5,3},{7,5},{... | collective-permute-start | bytes 3145736 | tf_op jit(solution)/shard_map/ppermute | solution.py:17
  349.6 2.0 copy-start.3
where the time goes:
time: 380 us; the launch traced here: 377 us
  waiting for transfers between devices  141 us (37%)
  matrix products  112 us (29%)
  local copies, waits for them, and re-layouts  49 us (13%)
  starting transfers between devices  41 us (11%)
  blocking collectives  17.5 us (5%)
  other arithmetic  15.1 us (4%)
    ppermute x8, waiting for transfers between devices, shifted(): return lax.ppermute(array, axis, pairs)  140 us
    dot_general x16, matrix products, capped_scores(): jnp.einsum('gqd,kd->gqk', query_head, key_head, preferred_element_type=jn...  27.5 us
    ppermute x8, starting transfers between devices, shifted(): return lax.ppermute(array, axis, pairs)  26.7 us
    unnamed x35, local copies, waits for them, and re-layouts  23.8 us
    dot_general x8, matrix products, full_grads(): jnp.einsum('gqk,gqd->kd', weights, members[1], preferred_element_type=jnp...  21.6 us
    dot_general x8, matrix products, score_grads(): jnp.einsum('gqd,kd->gqk', grad_head, value_head, preferred_element_type=j...  19.2 us
    dot_general x8, matrix products, forward_head(): jnp.einsum('gqk,kd->gqd', probs, value_head, preferred_element_type=jnp.f...  17.6 us
    dot_general x8, matrix products, full_grads(): jnp.einsum('gqk,gqd->kd', dscore, members[0], preferred_element_type=jnp....  17.2 us
  transfers between devices with their start and end apart: 12, of which 9 were waited for; matrix products, arithmetic and copies ran while one was open for 5% of the time, Pallas kernels for 0%

commit v1 on v0

v1 whole, which is shorter than its diff:
```python
import functools
import math

import jax
import jax.numpy as jnp
from jax import lax
from jax.experimental import pallas as pl
from jax.experimental.pallas import tpu as pltpu
from jax.sharding import PartitionSpec as P

HEAD = 128
WINDOW = 1024
INNER = 2
CHUNKS = (2, 2)
SOFTCAP = 50.0
TANH_SCALE = 1.0 / (12.0 * SOFTCAP)
EXP2_SCALE = SOFTCAP * math.log2(math.e)
SCORE_SCALE = 1.0 / 12.0
F32 = jnp.float32
BF16 = jnp.bfloat16


def dot(a, b, ca, cb):
    return lax.dot_general(a, b, (((ca,), (cb,)), ((), ())), preferred_element_type=F32)


def vmem():
    return pl.BlockSpec(memory_space=pltpu.VMEM)


def smem():
    return pl.BlockSpec(memory_space=pltpu.SMEM)


def head_cols(index):
    return pl.ds(pl.multiple_of(index * HEAD, HEAD), HEAD)


def pack_kernel(chunks, members, group, heads_dev, info, a_ref, b_ref, *outs):
    me = info[0]
    first = 0
    for c, heads in enumerate(chunks):
        for m in range(members):
            out = outs[c * members + m]
            base = (me ^ m) * heads_dev + first
            for h in range(heads):
                for g in range(group):
                    source = head_cols((base + h) * group + g)
                    out[:, (2 * h * group + g) * HEAD : (2 * h * group + g + 1) * HEAD] = a_ref[:, source]
                    out[:, ((2 * h + 1) * group + g) * HEAD : ((2 * h + 1) * group + g + 1) * HEAD] = b_ref[:, source]
        first += heads


def pack(info, a, b, chunks, members, group, heads_dev):
    rows = a.shape[0]
    return pl.pallas_call(
        functools.partial(pack_kernel, chunks, members, group, heads_dev),
        out_shape=[
            jax.ShapeDtypeStruct((rows, 2 * h * group * HEAD), BF16) for h in chunks for _ in range(members)
        ],
        in_specs=[smem(), vmem(), vmem()],
        out_specs=[vmem()] * (len(chunks) * members),
        compiler_params=pltpu.CompilerParams(vmem_limit_bytes=40 * 2**20),
        name="pack",
    )(info, a, b)


def unpack_kernel(chunks, members, group, heads_dev, info, *refs):
    me = info[0]
    ins, (a_ref, b_ref) = refs[:-2], refs[-2:]
    first = 0
    for c, heads in enumerate(chunks):
        for m in range(members):
            src = ins[c * members + m]
            base = (me ^ m) * heads_dev + first
            for h in range(heads):
                for g in range(group):
                    target = head_cols((base + h) * group + g)
                    a_ref[:, target] = src[:, (2 * h * group + g) * HEAD : (2 * h * group + g + 1) * HEAD]
                    b_ref[:, target] = src[:, ((2 * h + 1) * group + g) * HEAD : ((2 * h + 1) * group + g + 1) * HEAD]
        first += heads


def unpack(info, pieces, chunks, members, group, heads_dev):
    rows = pieces[0].shape[0]
    width = members * heads_dev * group * HEAD
    return pl.pallas_call(
        functools.partial(unpack_kernel, chunks, members, group, heads_dev),
        out_shape=[jax.ShapeDtypeStruct((rows, width), BF16)] * 2,
        in_specs=[smem()] + [vmem()] * len(pieces),
        out_specs=[vmem()] * 2,
        compiler_params=pltpu.CompilerParams(vmem_limit_bytes=40 * 2**20),
        name="unpack",
    )(info, *pieces)


def attention_kernel(members, hops, group, rows, info, *refs):
    planes = hops + 1
    kv_refs = refs[:planes]
    q_refs = refs[planes : planes + members]
    o_refs = refs[planes + members : planes + 2 * members]
    dkv_refs = refs[planes + 2 * members : 2 * planes + 2 * members]
    k_s, v_s, kt_s, vt_s, dk_s, dv_s, p_s, eg_s, ds_s = refs[2 * planes + 2 * members :]
    me = info[0]
    plane = info[1]
    blocks = WINDOW // rows + 1
    wide = group * rows
    span = blocks * rows
    for k in range(planes):
        for s in range(members):
            at = (k * members + s) * rows
            piece = kv_refs[k][me ^ s]
            k_s[at : at + rows, :] = piece[:, :HEAD]
            v_s[at : at + rows, :] = piece[:, HEAD:]
            kt_s[:, at : at + rows] = piece[:, :HEAD].T
            vt_s[:, at : at + rows] = piece[:, HEAD:].T
    dk_s[...] = jnp.zeros_like(dk_s)
    dv_s[...] = jnp.zeros_like(dv_s)
    key_at = lax.broadcasted_iota(jnp.int32, (rows, wide), 0)
    query_at = lax.broadcasted_iota(jnp.int32, (rows, wide), 1) % rows
    after = key_at > query_at
    for m in range(members):
        s = me ^ m
        base = pl.multiple_of(s * rows, rows)
        q_all = q_refs[m]
        q = jnp.concatenate([q_all[:, g * HEAD : (g + 1) * HEAD] for g in range(group)], axis=0)
        go = jnp.concatenate([q_all[:, (group + g) * HEAD : (group + g + 1) * HEAD] for g in range(group)], axis=0)
        total = jnp.zeros((1, wide), F32)
        for b in range(blocks):
            score = dot(k_s[pl.ds(pl.multiple_of(base + b * rows, rows), rows), :], q, 1, 1)
            t = jnp.tanh(score * TANH_SCALE)
            e = jnp.exp2(t * EXP2_SCALE)
            if b == 0:
                e = jnp.where(after, e, 0.0)
            if b == blocks - 1:
                e = jnp.where(after, 0.0, e)
            seen = plane - hops + lax.div(s + b, members) >= 0
            total = total + jnp.where(seen, jnp.sum(e, axis=0, keepdims=True), 0.0)
            p_s[b * rows : (b + 1) * rows, :] = e.astype(BF16)
            eg_s[b * rows : (b + 1) * rows, :] = e * (1.0 - t * t)
        inverse = 1.0 / total
        band = pl.ds(base, span)
        p = p_s[...]
        ot = (dot(vt_s[:, band], p, 1, 0) * inverse).astype(BF16)
        got = (go.astype(F32).T * inverse).astype(BF16)
        gdot = jnp.sum(ot.astype(F32) * got.astype(F32), axis=0, keepdims=True)
        for b in range(blocks):
            part = slice(b * rows, (b + 1) * rows)
            dp = dot(v_s[pl.ds(pl.multiple_of(base + b * rows, rows), rows), :], got, 1, 0)
            ds_s[part, :] = ((dp - gdot) * eg_s[part, :]).astype(BF16)
        ds = ds_s[...]
        dqt = dot(kt_s[:, band], ds, 1, 0) * SCORE_SCALE
        dk_s[band, :] += dot(ds, q, 1, 0)
        dv_s[band, :] += dot(p, got, 1, 1)
        o = ot.astype(F32).T.astype(BF16)
        dq = dqt.T.astype(BF16)
        for g in range(group):
            o_refs[m][:, g * HEAD : (g + 1) * HEAD] = o[g * rows : (g + 1) * rows]
            o_refs[m][:, (group + g) * HEAD : (group + g + 1) * HEAD] = dq[g * rows : (g + 1) * rows]
    for k in range(planes):
        for s in range(members):
            at = (k * members + s) * rows
            dkv_refs[k][me ^ s, :, :HEAD] = (dk_s[at : at + rows, :] * SCORE_SCALE).astype(BF16)
            dkv_refs[k][me ^ s, :, HEAD:] = dv_s[at : at + rows, :].astype(BF16)


def attention(info, kvs, qs, group):
    planes, members = len(kvs), len(qs)
    rows = qs[0].shape[0]
    heads = kvs[0].shape[2] // (2 * HEAD)
    keys_all = planes * members * rows
    wide = group * rows
    span = WINDOW + rows
    kv_spec = pl.BlockSpec((members, rows, 2 * HEAD), lambda h: (0, 0, h))
    q_spec = pl.BlockSpec((rows, 2 * group * HEAD), lambda h: (0, h))
    return pl.pallas_call(
        functools.partial(attention_kernel, members, planes - 1, group, rows),
        grid=(heads,),
        out_shape=[jax.ShapeDtypeStruct(q.shape, BF16) for q in qs]
        + [jax.ShapeDtypeStruct(kv.shape, BF16) for kv in kvs],
        in_specs=[smem()] + [kv_spec] * planes + [q_spec] * members,
        out_specs=[q_spec] * members + [kv_spec] * planes,
        scratch_shapes=[
            pltpu.VMEM((keys_all, HEAD), BF16),
            pltpu.VMEM((keys_all, HEAD), BF16),
            pltpu.VMEM((HEAD, keys_all), BF16),
            pltpu.VMEM((HEAD, keys_all), BF16),
            pltpu.VMEM((keys_all, HEAD), F32),
            pltpu.VMEM((keys_all, HEAD), F32),
            pltpu.VMEM((span, wide), BF16),
            pltpu.VMEM((span, wide), F32),
            pltpu.VMEM((span, wide), BF16),
        ],
        compiler_params=pltpu.CompilerParams(vmem_limit_bytes=40 * 2**20),
        cost_estimate=pl.CostEstimate(
            flops=12 * heads * members * wide * span * HEAD,
            bytes_accessed=2 * (2 * planes * kvs[0].size + 2 * members * qs[0].size),
            transcendentals=2 * heads * members * wide * span,
        ),
        name="attention",
    )(info, *kvs, *qs)


def on_device(queries, keys, values, output_gradient):
    rows = queries.shape[0]
    tp = lax.axis_size("tp")
    ctx = lax.axis_size("ctx")
    members = INNER * tp
    planes = ctx // INNER
    heads_dev = keys.shape[1] // HEAD // members
    group = queries.shape[1] // keys.shape[1]
    hops = max(1, WINDOW // (members * rows))
    device = lax.axis_index("ctx") * tp + lax.axis_index("tp")
    me = device % members
    plane = device // members
    info = jnp.stack([me, plane]).astype(jnp.int32)
    axes = ("ctx", "tp")

    def swap(piece, m):
        if m == 0:
            return piece
        return lax.ppermute(piece, axes, [(i, i ^ m) for i in range(ctx * tp)])

    def hop(array, by):
        pairs = [(i, i + by * members) for i in range(ctx * tp) if 0 <= i + by * members < ctx * tp]
        return lax.ppermute(array, axes, pairs)

    kv_packed = pack(info, keys, values, CHUNKS, members, 1, heads_dev)
    q_packed = pack(info, queries, output_gradient, CHUNKS, members, group, heads_dev)
    kv_own = []
    for c in range(len(CHUNKS)):
        kv_own.append(jnp.stack([swap(kv_packed[c * members + m], m) for m in range(members)]))
    q_pieces = []
    kv_all = []
    for c in range(len(CHUNKS)):
        halo = [kv_own[c]]
        for _ in range(hops):
            halo.insert(0, hop(halo[0], 1))
        kv_all.append(halo)
        q_pieces.append([swap(q_packed[c * members + m], m) for m in range(members)])
    o_pieces, dkv_pieces = [], []
    for c in range(len(CHUNKS)):
        results = attention(info, kv_all[c], q_pieces[c], group)
        os, dkvs = results[:members], results[members:]
        o_pieces += [swap(os[m], m) for m in range(members)]
        carried = dkvs[0]
        for k in range(1, hops + 1):
            carried = (hop(carried, -1).astype(F32) + dkvs[k].astype(F32)).astype(BF16)
        dkv_pieces += [swap(carried[m], m) for m in range(members)]
    attended, query_grad = unpack(info, o_pieces, CHUNKS, members, group, heads_dev)
    key_grad, value_grad = unpack(info, dkv_pieces, CHUNKS, members, 1, heads_dev)
    return attended, query_grad, key_grad, value_grad


def solution(mesh):
    placed = P(("group", "ctx", "tp"), None)
    return jax.shard_map(
        on_device, mesh=mesh, in_specs=(placed,) * 4, out_specs=(placed,) * 4, check_vma=False
    )
```

time: 380 us -> 137 us (0.36)
  matrix products: 112 us -> 0 us
  waiting for transfers between devices: 141 us -> 66.1 us
  local copies, waits for them, and re-layouts: 49 us -> 2.16 us
  Pallas kernels: 0 us -> 28.2 us
  blocking collectives: 17.5 us -> 0 us
  other arithmetic: 15.1 us -> 0.78 us
    dot_general x56 -> x0, matrix products: 112 us -> none  [the longest x16 27.5 us: capped_scores(): jnp.einsum('gqd,kd->gqk', query_head, key_head, preferred_element_type=jn...]
    ppermute x8 -> x32, waiting for transfers between devices: 140 us -> 66.1 us  [the longest x8 40.6 us: hop(): return lax.ppermute(array, axes, pairs)]
    pallas_call x0 -> x6, Pallas kernels: none -> 28.2 us  [the longest x2 22.1 us: attention(): pl.pallas_call(functools.partial(attention_kernel, members, planes - 1, g...]
    unnamed x35 -> x8, local copies, waits for them, and re-layouts: 23.8 us -> 2.09 us
    all_to_all x4 -> x0, blocking collectives: 17.5 us -> none  [the longest x1 4.58 us: on_device(): lax.all_to_all(attended_block, 'tp', split_axis=0, concat_axis=1, tiled=T...]
    all_to_all x4 -> x0, starting transfers between devices: 14.3 us -> none  [the longest x1 3.62 us: on_device(): lax.all_to_all(values, 'tp', split_axis=1, concat_axis=0, tiled=True)]
    ppermute x8 -> x32, starting transfers between devices: 26.7 us -> 38.6 us  [the longest x8 21 us: hop(): return lax.ppermute(array, axes, pairs)]
    slice x6 -> x0, local copies, waits for them, and re-layouts: 9.76 us -> none  [the longest x2 6.57 us: on_device(): heads_of_values = to_key_heads(all_pair[1], kv_heads)]
  transfers between devices with their start and end apart: 12 -> 32, of which waited for: 9 -> 15; matrix products, arithmetic and copies ran while one was open for 5% -> 1% of each run, Pallas kernels for 0% -> 19%
where the time goes in v1:
time: 137 us
  waiting for transfers between devices  66.1 us (48%)
  starting transfers between devices  38.6 us (28%)
  Pallas kernels  28.2 us (21%)
  local copies, waits for them, and re-layouts  2.16 us (2%)
    ppermute x8, waiting for transfers between devices, hop(): return lax.ppermute(array, axes, pairs)  40.6 us
    ppermute x24, waiting for transfers between devices, swap(): return lax.ppermute(piece, axes, [(i, i ^ m) for i in range(ctx * tp)])  25.5 us
    pallas_call x2, Pallas kernels, attention(): pl.pallas_call(functools.partial(attention_kernel, members, planes - 1, g...  22.1 us
    ppermute x8, starting transfers between devices, hop(): return lax.ppermute(array, axes, pairs)  21 us
    ppermute x24, starting transfers between devices, swap(): return lax.ppermute(piece, axes, [(i, i ^ m) for i in range(ctx * tp)])  17.6 us
    pallas_call x2, Pallas kernels, unpack(): pl.pallas_call(functools.partial(unpack_kernel, chunks, members, group, h...  4.15 us
  transfers between devices with their start and end apart: 32, of which 15 were waited for; matrix products, arithmetic and copies ran while one was open for 1% of the time, Pallas kernels for 19%

profile of v1, /device:TPU:0, one launch (start us, length us, event | category | flops | bytes accessed | tf_op | source)
XLA Modules:
  0.0 136.8 jit_solution(5655360201200716778)
XLA Ops:
  4.2 2.6 %collective-permute-start.12 = (bf16[128,512]{1,0:T(8,128)(2,1)S(1)}, bf16[128,512]{1,0:T(8,128)(2,1)S(1)}, u32[]{:S(2)}, u32[]{:S(2)}) collective-permute-start(bf16[128,512]{1,0:T(8,128)(2,1)S(1)} %get-tuple-element.52), channel_id=1, source_target_pairs={{0,2},{1,3},{2,0},{3,1},{4,6},{5,7},{6,4},{7,5},{8,10},{9,11},{10,... | collective-permute-start | bytes 393224 | tf_op jit(solution)/shard_map/ppermute | solution.py:222
  6.8 4.3 %collective-permute-done.12 = bf16[128,512]{1,0:T(8,128)(2,1)S(1)} collective-permute-done((bf16[128,512]{1,0:T(8,128)(2,1)S(1)}, bf16[128,512]{1,0:T(8,128)(2,1)S(1)}, u32[]{:S(2)}, u32[]{:S(2)}) %collective-permute-start.12) | collective-permute-done | bytes 131104 | tf_op jit(solution)/shard_map/ppermute | solution.py:222
  11.1 2.3 %collective-permute-done.13 = bf16[128,512]{1,0:T(8,128)(2,1)S(1)} collective-permute-done((bf16[128,512]{1,0:T(8,128)(2,1)S(1)}, bf16[128,512]{1,0:T(8,128)(2,1)S(1)}, u32[]{:S(2)}, u32[]{:S(2)}) %collective-permute-start.13) | collective-permute-done | bytes 131104 | tf_op jit(solution)/shard_map/ppermute | solution.py:222
  13.4 3.7 %collective-permute-start.14 = (bf16[4,128,512]{2,1,0:T(8,128)(2,1)S(1)}, bf16[4,128,512]{2,1,0:T(8,128)(2,1)S(1)}, u32[]{:S(2)}, u32[]{:S(2)}) collective-permute-start(bf16[4,128,512]{2,1,0:T(8,128)(2,1)S(1)} %pad_maximum_fusion.1.refs_2_), channel_id=1, source_target_pairs={{0,4},{1,5},{2,6},{3,7},{4,8},{5,9},{6,10},{7,11},{8,12},{9,13},{1... | collective-permute-start | bytes 1572872 | tf_op jit(solution)/shard_map/ppermute | solution.py:226
  17.2 1.6 %collective-permute-start.1 = (bf16[128,512]{1,0:T(8,128)(2,1)S(1)}, bf16[128,512]{1,0:T(8,128)(2,1)S(1)}, u32[]{:S(2)}, u32[]{:S(2)}) collective-permute-start(bf16[128,512]{1,0:T(8,128)(2,1)S(1)} %get-tuple-element.40), channel_id=1, source_target_pairs={{0,2},{1,3},{2,0},{3,1},{4,6},{5,7},{6,4},{7,5},{8,10},{9,11},{10,... | collective-permute-start | bytes 393224 | tf_op jit(solution)/shard_map/ppermute | solution.py:222
  19.1 4.5 %collective-permute-done.1 = bf16[128,512]{1,0:T(8,128)(2,1)S(1)} collective-permute-done((bf16[128,512]{1,0:T(8,128)(2,1)S(1)}, bf16[128,512]{1,0:T(8,128)(2,1)S(1)}, u32[]{:S(2)}, u32[]{:S(2)}) %collective-permute-start.1) | collective-permute-done | bytes 131104 | tf_op jit(solution)/shard_map/ppermute | solution.py:222
  23.6 1.9 %collective-permute-done.2 = bf16[128,512]{1,0:T(8,128)(2,1)S(1)} collective-permute-done((bf16[128,512]{1,0:T(8,128)(2,1)S(1)}, bf16[128,512]{1,0:T(8,128)(2,1)S(1)}, u32[]{:S(2)}, u32[]{:S(2)}) %collective-permute-start.2) | collective-permute-done | bytes 131104 | tf_op jit(solution)/shard_map/ppermute | solution.py:222
  25.6 3.5 %collective-permute-start.3 = (bf16[4,128,512]{2,1,0:T(8,128)(2,1)S(1)}, bf16[4,128,512]{2,1,0:T(8,128)(2,1)S(1)}, u32[]{:S(2)}, u32[]{:S(2)}) collective-permute-start(bf16[4,128,512]{2,1,0:T(8,128)(2,1)S(1)} %pad_maximum_fusion.refs_2_), channel_id=1, source_target_pairs={{0,4},{1,5},{2,6},{3,7},{4,8},{5,9},{6,10},{7,11},{8,12},{9,13},{1... | collective-permute-start | bytes 1572872 | tf_op jit(solution)/shard_map/ppermute | solution.py:226
  29.1 4.1 %collective-permute-start.15 = (bf16[4,128,512]{2,1,0:T(8,128)(2,1)S(1)}, bf16[4,128,512]{2,1,0:T(8,128)(2,1)S(1)}, u32[]{:S(2)}, u32[]{:S(2)}) collective-permute-start(bf16[4,128,512]{2,1,0:T(8,128)(2,1)S(1)} %collective-permute-done.14.refs_1_), channel_id=1, source_target_pairs={{0,4},{1,5},{2,6},{3,7},{4,8},{5,9},{6,10},{7,11},{8,12},{9,13},{1... | collective-permute-start | bytes 1572872 | tf_op jit(solution)/shard_map/ppermute | solution.py:226
  36.2 5.0 %collective-permute-done.3.refs_1_ = bf16[4,128,512]{2,1,0:T(8,128)(2,1)S(1)} collective-permute-done((bf16[4,128,512]{2,1,0:T(8,128)(2,1)S(1)}, bf16[4,128,512]{2,1,0:T(8,128)(2,1)S(1)}, u32[]{:S(2)}, u32[]{:S(2)}) %collective-permute-start.3) | collective-permute-done | bytes 524320 | tf_op jit(solution)/shard_map/ppermute | solution.py:226
  41.2 4.4 %collective-permute-start.4 = (bf16[4,128,512]{2,1,0:T(8,128)(2,1)S(1)}, bf16[4,128,512]{2,1,0:T(8,128)(2,1)S(1)}, u32[]{:S(2)}, u32[]{:S(2)}) collective-permute-start(bf16[4,128,512]{2,1,0:T(8,128)(2,1)S(1)} %collective-permute-done.3.refs_1_), channel_id=1, source_target_pairs={{0,4},{1,5},{2,6},{3,7},{4,8},{5,9},{6,10},{7,11},{8,12},{9,13},{1... | collective-permute-start | bytes 1572872 | tf_op jit(solution)/shard_map/ppermute | solution.py:226
  49.6 2.9 %collective-permute-done.15.refs_0_ = bf16[4,128,512]{2,1,0:T(8,128)(2,1)S(1)} collective-permute-done((bf16[4,128,512]{2,1,0:T(8,128)(2,1)S(1)}, bf16[4,128,512]{2,1,0:T(8,128)(2,1)S(1)}, u32[]{:S(2)}, u32[]{:S(2)}) %collective-permute-start.15) | collective-permute-done | bytes 524320 | tf_op jit(solution)/shard_map/ppermute | solution.py:226
  52.5 11.0 %attention.3 = (bf16[128,1024]{1,0:T(8,128)(2,1)S(1)}, bf16[128,1024]{1,0:T(8,128)(2,1)S(1)}, bf16[128,1024]{1,0:T(8,128)(2,1)S(1)}, bf16[128,1024]{1,0:T(8,128)...) custom-call(s32[2]{0:T(128)S(1)} %pad_add_fusion.info, ...), custom_call_target="tpu_custom_call" | custom-call | flops 3623878656 | bytes 5242880 | tf_op jit(solution)/shard_map/attention/pallas_call | solution.py:176
  65.1 11.1 %attention.2 = (bf16[128,1024]{1,0:T(8,128)(2,1)S(1)}, bf16[128,1024]{1,0:T(8,128)(2,1)S(1)}, bf16[128,1024]{1,0:T(8,128)(2,1)S(1)}, bf16[128,1024]{1,0:T(8,128)...) custom-call(s32[2]{0:T(128)S(1)} %pad_add_fusion.info, ...), custom_call_target="tpu_custom_call" | custom-call | flops 3623878656 | bytes 5242880 | tf_op jit(solution)/shard_map/attention/pallas_call | solution.py:176
  77.4 2.0 %collective-permute-done.27 = bf16[4,128,512]{2,1,0:T(8,128)(2,1)S(1)} collective-permute-done((bf16[4,128,512]{2,1,0:T(8,128)(2,1)S(1)}, bf16[4,128,512]{2,1,0:T(8,128)(2,1)S(1)}, u32[]{:S(2)}, u32[]{:S(2)}) %collective-permute-start.27) | collective-permute-done | bytes 524320 | tf_op jit(solution)/shard_map/ppermute | solution.py:226
  80.9 13.0 %collective-permute-done.22 = bf16[4,128,512]{2,1,0:T(8,128)(2,1)S(1)} collective-permute-done((bf16[4,128,512]{2,1,0:T(8,128)(2,1)S(1)}, bf16[4,128,512]{2,1,0:T(8,128)(2,1)S(1)}, u32[]{:S(2)}, u32[]{:S(2)}) %collective-permute-start.22) | collective-permute-done | bytes 524320 | tf_op jit(solution)/shard_map/ppermute | solution.py:226
  97.3 7.8 %collective-permute-done.28 = bf16[4,128,512]{2,1,0:T(8,128)(2,1)S(1)} collective-permute-done((bf16[4,128,512]{2,1,0:T(8,128)(2,1)S(1)}, bf16[4,128,512]{2,1,0:T(8,128)(2,1)S(1)}, u32[]{:S(2)}, u32[]{:S(2)}) %collective-permute-start.28) | collective-permute-done | bytes 524320 | tf_op jit(solution)/shard_map/ppermute | solution.py:226
  105.3 9.8 %collective-permute-done.23 = bf16[4,128,512]{2,1,0:T(8,128)(2,1)S(1)} collective-permute-done((bf16[4,128,512]{2,1,0:T(8,128)(2,1)S(1)}, bf16[4,128,512]{2,1,0:T(8,128)(2,1)S(1)}, u32[]{:S(2)}, u32[]{:S(2)}) %collective-permute-start.23) | collective-permute-done | bytes 524320 | tf_op jit(solution)/shard_map/ppermute | solution.py:226
  115.3 1.6 %collective-permute-start.9 = (bf16[128,1024]{1,0:T(8,128)(2,1)S(1)}, bf16[128,1024]{1,0:T(8,128)(2,1)S(1)}, u32[]{:S(2)}, u32[]{:S(2)}) collective-permute-start(bf16[128,1024]{1,0:T(8,128)(2,1)S(1)} %get-tuple-element.48), channel_id=1, source_target_pairs={{0,2},{1,3},{2,0},{3,1},{4,6},{5,7},{6,4},{7,5},{8,10},{9,11},{10,... | collective-permute-start | bytes 786440 | tf_op jit(solution)/shard_map/ppermute | solution.py:222
  119.5 5.0 %collective-permute-done.9.refs_2_ = bf16[128,1024]{1,0:T(8,128)(2,1)S(1)} collective-permute-done((bf16[128,1024]{1,0:T(8,128)(2,1)S(1)}, bf16[128,1024]{1,0:T(8,128)(2,1)S(1)}, u32[]{:S(2)}, u32[]{:S(2)}) %collective-permute-start.9) | collective-permute-done | bytes 262176 | tf_op jit(solution)/shard_map/ppermute | solution.py:222
  126.0 2.4 %unpack.2 = (bf16[128,4096]{1,0:T(8,128)(2,1)}, bf16[128,4096]{1,0:T(8,128)(2,1)}) custom-call(s32[2]{0:T(128)S(1)} %pad_add_fusion.info, bf16[128,1024]{1,0:T(8,128)(2,1)S(1)} %get-tuple-element.46.refs_0_, bf16[128,1024]{1,0:T(8,128)(2,1)S(1)} %collective-permute-done.8.refs_1_, bf16[128,1024]{1,0:T(8,128)(2,1)S(1)} %collective-permute-done.9.refs_2_, ...), custom_call_target="tpu_custom_call" | custom-call | tf_op jit(solution)/shard_map/unpack/pallas_call | solution.py:87
  129.4 3.6 %collective-permute-done.25.refs_2_ = bf16[128,512]{1,0:T(8,128)(2,1)S(1)} collective-permute-done((bf16[128,512]{1,0:T(8,128)(2,1)S(1)}, bf16[128,512]{1,0:T(8,128)(2,1)S(1)}, u32[]{:S(2)}, u32[]{:S(2)}) %collective-permute-start.25) | collective-permute-done | bytes 131104 | tf_op jit(solution)/shard_map/ppermute | solution.py:222
  132.9 2.0 %collective-permute-done.26.refs_3_ = bf16[128,512]{1,0:T(8,128)(2,1)S(1)} collective-permute-done((bf16[128,512]{1,0:T(8,128)(2,1)S(1)}, bf16[128,512]{1,0:T(8,128)(2,1)S(1)}, u32[]{:S(2)}, u32[]{:S(2)}) %collective-permute-start.26) | collective-permute-done | bytes 131104 | tf_op jit(solution)/shard_map/ppermute | solution.py:222
  135.0 1.8 %unpack.3 = (bf16[128,2048]{1,0:T(8,128)(2,1)}, bf16[128,2048]{1,0:T(8,128)(2,1)}) custom-call(s32[2]{0:T(128)S(1)} %pad_add_fusion.info, bf16[128,512]{1,0:T(8,128)(2,1)S(1)} %get-tuple-element.79.refs_0_, bf16[128,512]{1,0:T(8,128)(2,1)S(1)} %collective-permute-done.24.refs_1_, bf16[128,512]{1,0:T(8,128)(2,1)S(1)} %collective-permute-done.25.refs_2_, ...), custom_call_target="tpu_custom_call" | custom-call | tf_op jit(solution)/shard_map/unpack/pallas_call | solution.py:87
  (63 shorter events, 24.0 us)
Async XLA Ops:
  13.4 15.6 %collective-permute-start.14 = (bf16[4,128,512]{2,1,0:T(8,128)(2,1)S(1)}, bf16[4,128,512]{2,1,0:T(8,128)(2,1)S(1)}, u32[]{:S(2)}, u32[]{:S(2)}) collective-permute-start(bf16[4,128,512]{2,1,0:T(8,128)(2,1)S(1)} %pad_maximum_fusion.1.refs_2_), channel_id=1, source_target_pairs={{0,4},{1,5},{2,6},{3,7},{4,8},{5,9},{6,10},{7,11},{8,12},{9,13},{1... | collective-permute-start | bytes 1572872 | tf_op jit(solution)/shard_map/ppermute | solution.py:226
  25.6 15.7 %collective-permute-start.3 = (bf16[4,128,512]{2,1,0:T(8,128)(2,1)S(1)}, bf16[4,128,512]{2,1,0:T(8,128)(2,1)S(1)}, u32[]{:S(2)}, u32[]{:S(2)}) collective-permute-start(bf16[4,128,512]{2,1,0:T(8,128)(2,1)S(1)} %pad_maximum_fusion.refs_2_), channel_id=1, source_target_pairs={{0,4},{1,5},{2,6},{3,7},{4,8},{5,9},{6,10},{7,11},{8,12},{9,13},{1... | collective-permute-start | bytes 1572872 | tf_op jit(solution)/shard_map/ppermute | solution.py:226
  29.1 23.4 %collective-permute-start.15 = (bf16[4,128,512]{2,1,0:T(8,128)(2,1)S(1)}, bf16[4,128,512]{2,1,0:T(8,128)(2,1)S(1)}, u32[]{:S(2)}, u32[]{:S(2)}) collective-permute-start(bf16[4,128,512]{2,1,0:T(8,128)(2,1)S(1)} %collective-permute-done.14.refs_1_), channel_id=1, source_target_pairs={{0,4},{1,5},{2,6},{3,7},{4,8},{5,9},{6,10},{7,11},{8,12},{9,13},{1... | collective-permute-start | bytes 1572872 | tf_op jit(solution)/shard_map/ppermute | solution.py:226
  34.3 11.4 %collective-permute-start.16 = (bf16[128,1024]{1,0:T(8,128)(2,1)S(1)}, bf16[128,1024]{1,0:T(8,128)(2,1)S(1)}, u32[]{:S(2)}, u32[]{:S(2)}) collective-permute-start(bf16[128,1024]{1,0:T(8,128)(2,1)S(1)} %get-tuple-element.55), channel_id=1, source_target_pairs={{0,1},{1,0},{2,3},{3,2},{4,5},{5,4},{6,7},{7,6},{8,9},{9,8},{10,11... | collective-permute-start | bytes 786440 | tf_op jit(solution)/shard_map/ppermute | solution.py:222
  34.4 11.4 %collective-permute-start.17 = (bf16[128,1024]{1,0:T(8,128)(2,1)S(1)}, bf16[128,1024]{1,0:T(8,128)(2,1)S(1)}, u32[]{:S(2)}, u32[]{:S(2)}) collective-permute-start(bf16[128,1024]{1,0:T(8,128)(2,1)S(1)} %get-tuple-element.56), channel_id=1, source_target_pairs={{0,2},{1,3},{2,0},{3,1},{4,6},{5,7},{6,4},{7,5},{8,10},{9,11},{10,... | collective-permute-start | bytes 786440 | tf_op jit(solution)/shard_map/ppermute | solution.py:222
  35.9 12.3 %collective-permute-start.18 = (bf16[128,1024]{1,0:T(8,128)(2,1)S(1)}, bf16[128,1024]{1,0:T(8,128)(2,1)S(1)}, u32[]{:S(2)}, u32[]{:S(2)}) collective-permute-start(bf16[128,1024]{1,0:T(8,128)(2,1)S(1)} %get-tuple-element.57), channel_id=1, source_target_pairs={{0,3},{1,2},{2,1},{3,0},{4,7},{5,6},{6,5},{7,4},{8,11},{9,10},{10,... | collective-permute-start | bytes 786440 | tf_op jit(solution)/shard_map/ppermute | solution.py:222
  41.2 23.8 %collective-permute-start.4 = (bf16[4,128,512]{2,1,0:T(8,128)(2,1)S(1)}, bf16[4,128,512]{2,1,0:T(8,128)(2,1)S(1)}, u32[]{:S(2)}, u32[]{:S(2)}) collective-permute-start(bf16[4,128,512]{2,1,0:T(8,128)(2,1)S(1)} %collective-permute-done.3.refs_1_), channel_id=1, source_target_pairs={{0,4},{1,5},{2,6},{3,7},{4,8},{5,9},{6,10},{7,11},{8,12},{9,13},{1... | collective-permute-start | bytes 1572872 | tf_op jit(solution)/shard_map/ppermute | solution.py:226
  45.7 19.3 %collective-permute-start.5 = (bf16[128,1024]{1,0:T(8,128)(2,1)S(1)}, bf16[128,1024]{1,0:T(8,128)(2,1)S(1)}, u32[]{:S(2)}, u32[]{:S(2)}) collective-permute-start(bf16[128,1024]{1,0:T(8,128)(2,1)S(1)} %get-tuple-element.43), channel_id=1, source_target_pairs={{0,1},{1,0},{2,3},{3,2},{4,5},{5,4},{6,7},{7,6},{8,9},{9,8},{10,11... | collective-permute-start | bytes 786440 | tf_op jit(solution)/shard_map/ppermute | solution.py:222
  45.8 19.3 %collective-permute-start.6 = (bf16[128,1024]{1,0:T(8,128)(2,1)S(1)}, bf16[128,1024]{1,0:T(8,128)(2,1)S(1)}, u32[]{:S(2)}, u32[]{:S(2)}) collective-permute-start(bf16[128,1024]{1,0:T(8,128)(2,1)S(1)} %get-tuple-element.44), channel_id=1, source_target_pairs={{0,2},{1,3},{2,0},{3,1},{4,6},{5,7},{6,4},{7,5},{8,10},{9,11},{10,... | collective-permute-start | bytes 786440 | tf_op jit(solution)/shard_map/ppermute | solution.py:222
  48.2 16.8 %collective-permute-start.7 = (bf16[128,1024]{1,0:T(8,128)(2,1)S(1)}, bf16[128,1024]{1,0:T(8,128)(2,1)S(1)}, u32[]{:S(2)}, u32[]{:S(2)}) collective-permute-start(bf16[128,1024]{1,0:T(8,128)(2,1)S(1)} %get-tuple-element.45), channel_id=1, source_target_pairs={{0,3},{1,2},{2,1},{3,0},{4,7},{5,6},{6,5},{7,4},{8,11},{9,10},{10,... | collective-permute-start | bytes 786440 | tf_op jit(solution)/shard_map/ppermute | solution.py:222
  63.5 16.0 %collective-permute-start.27 = (bf16[4,128,512]{2,1,0:T(8,128)(2,1)S(1)}, bf16[4,128,512]{2,1,0:T(8,128)(2,1)S(1)}, u32[]{:S(2)}, u32[]{:S(2)}) collective-permute-start(bf16[4,128,512]{2,1,0:T(8,128)(2,1)S(1)} %get-tuple-element.67), channel_id=1, source_target_pairs={{4,0},{5,1},{6,2},{7,3},{8,4},{9,5},{10,6},{11,7},{12,8},{13,9},{1... | collective-permute-start | bytes 1572872 | tf_op jit(solution)/shard_map/ppermute | solution.py:226
  76.1 17.8 %collective-permute-start.22 = (bf16[4,128,512]{2,1,0:T(8,128)(2,1)S(1)}, bf16[4,128,512]{2,1,0:T(8,128)(2,1)S(1)}, u32[]{:S(2)}, u32[]{:S(2)}) collective-permute-start(bf16[4,128,512]{2,1,0:T(8,128)(2,1)S(1)} %get-tuple-element.64), channel_id=1, source_target_pairs={{4,0},{5,1},{6,2},{7,3},{8,4},{9,5},{10,6},{11,7},{12,8},{13,9},{1... | collective-permute-start | bytes 1572872 | tf_op jit(solution)/shard_map/ppermute | solution.py:226
  79.6 25.6 %collective-permute-start.28 = (bf16[4,128,512]{2,1,0:T(8,128)(2,1)S(1)}, bf16[4,128,512]{2,1,0:T(8,128)(2,1)S(1)}, u32[]{:S(2)}, u32[]{:S(2)}) collective-permute-start(bf16[4,128,512]{2,1,0:T(8,128)(2,1)S(1)} %add_convert_fusion.1), channel_id=1, source_target_pairs={{4,0},{5,1},{6,2},{7,3},{8,4},{9,5},{10,6},{11,7},{12,8},{13,9},{1... | collective-permute-start | bytes 1572872 | tf_op jit(solution)/shard_map/ppermute | solution.py:226
  94.1 21.1 %collective-permute-start.23 = (bf16[4,128,512]{2,1,0:T(8,128)(2,1)S(1)}, bf16[4,128,512]{2,1,0:T(8,128)(2,1)S(1)}, u32[]{:S(2)}, u32[]{:S(2)}) collective-permute-start(bf16[4,128,512]{2,1,0:T(8,128)(2,1)S(1)} %add_convert_fusion.3), channel_id=1, source_target_pairs={{4,0},{5,1},{6,2},{7,3},{8,4},{9,5},{10,6},{11,7},{12,8},{13,9},{1... | collective-permute-start | bytes 1572872 | tf_op jit(solution)/shard_map/ppermute | solution.py:226
  95.4 19.9 %collective-permute-start.19 = (bf16[128,1024]{1,0:T(8,128)(2,1)S(1)}, bf16[128,1024]{1,0:T(8,128)(2,1)S(1)}, u32[]{:S(2)}, u32[]{:S(2)}) collective-permute-start(bf16[128,1024]{1,0:T(8,128)(2,1)S(1)} %get-tuple-element.59), channel_id=1, source_target_pairs={{0,1},{1,0},{2,3},{3,2},{4,5},{5,4},{6,7},{7,6},{8,9},{9,8},{10,11... | collective-permute-start | bytes 786440 | tf_op jit(solution)/shard_map/ppermute | solution.py:222
  95.5 21.5 %collective-permute-start.20 = (bf16[128,1024]{1,0:T(8,128)(2,1)S(1)}, bf16[128,1024]{1,0:T(8,128)(2,1)S(1)}, u32[]{:S(2)}, u32[]{:S(2)}) collective-permute-start(bf16[128,1024]{1,0:T(8,128)(2,1)S(1)} %get-tuple-element.60), channel_id=1, source_target_pairs={{0,2},{1,3},{2,0},{3,1},{4,6},{5,7},{6,4},{7,5},{8,10},{9,11},{10,... | collective-permute-start | bytes 786440 | tf_op jit(solution)/shard_map/ppermute | solution.py:222
  97.0 20.3 %collective-permute-start.21 = (bf16[128,1024]{1,0:T(8,128)(2,1)S(1)}, bf16[128,1024]{1,0:T(8,128)(2,1)S(1)}, u32[]{:S(2)}, u32[]{:S(2)}) collective-permute-start(bf16[128,1024]{1,0:T(8,128)(2,1)S(1)} %get-tuple-element.61), channel_id=1, source_target_pairs={{0,3},{1,2},{2,1},{3,0},{4,7},{5,6},{6,5},{7,4},{8,11},{9,10},{10,... | collective-permute-start | bytes 786440 | tf_op jit(solution)/shard_map/ppermute | solution.py:222
  105.2 12.7 %collective-permute-start.10 = (bf16[128,1024]{1,0:T(8,128)(2,1)S(1)}, bf16[128,1024]{1,0:T(8,128)(2,1)S(1)}, u32[]{:S(2)}, u32[]{:S(2)}) collective-permute-start(bf16[128,1024]{1,0:T(8,128)(2,1)S(1)} %get-tuple-element.49), channel_id=1, source_target_pairs={{0,3},{1,2},{2,1},{3,0},{4,7},{5,6},{6,5},{7,4},{8,11},{9,10},{10,... | collective-permute-start | bytes 786440 | tf_op jit(solution)/shard_map/ppermute | solution.py:222
  115.3 9.2 %collective-permute-start.9 = (bf16[128,1024]{1,0:T(8,128)(2,1)S(1)}, bf16[128,1024]{1,0:T(8,128)(2,1)S(1)}, u32[]{:S(2)}, u32[]{:S(2)}) collective-permute-start(bf16[128,1024]{1,0:T(8,128)(2,1)S(1)} %get-tuple-element.48), channel_id=1, source_target_pairs={{0,2},{1,3},{2,0},{3,1},{4,6},{5,7},{6,4},{7,5},{8,10},{9,11},{10,... | collective-permute-start | bytes 786440 | tf_op jit(solution)/shard_map/ppermute | solution.py:222
  117.0 9.1 %collective-permute-start.29 = (bf16[128,512]{1,0:T(8,128)(2,1)S(1)}, bf16[128,512]{1,0:T(8,128)(2,1)S(1)}, u32[]{:S(2)}, u32[]{:S(2)}) collective-permute-start(bf16[128,512]{1,0:T(8,128)(2,1)S(1)} %get-tuple-element.74), channel_id=1, source_target_pairs={{0,1},{1,0},{2,3},{3,2},{4,5},{5,4},{6,7},{7,6},{8,9},{9,8},{10,11... | collective-permute-start | bytes 393224 | tf_op jit(solution)/shard_map/ppermute | solution.py:222
  117.3 11.1 %collective-permute-start.30 = (bf16[128,512]{1,0:T(8,128)(2,1)S(1)}, bf16[128,512]{1,0:T(8,128)(2,1)S(1)}, u32[]{:S(2)}, u32[]{:S(2)}) collective-permute-start(bf16[128,512]{1,0:T(8,128)(2,1)S(1)} %get-tuple-element.73), channel_id=1, source_target_pairs={{0,2},{1,3},{2,0},{3,1},{4,6},{5,7},{6,4},{7,5},{8,10},{9,11},{10,... | collective-permute-start | bytes 393224 | tf_op jit(solution)/shard_map/ppermute | solution.py:222
  117.9 11.5 %collective-permute-start.31 = (bf16[128,512]{1,0:T(8,128)(2,1)S(1)}, bf16[128,512]{1,0:T(8,128)(2,1)S(1)}, u32[]{:S(2)}, u32[]{:S(2)}) collective-permute-start(bf16[128,512]{1,0:T(8,128)(2,1)S(1)} %get-tuple-element.72), channel_id=1, source_target_pairs={{0,3},{1,2},{2,1},{3,0},{4,7},{5,6},{6,5},{7,4},{8,11},{9,10},{10,... | collective-permute-start | bytes 393224 | tf_op jit(solution)/shard_map/ppermute | solution.py:222
  119.0 10.3 %collective-permute-start.24 = (bf16[128,512]{1,0:T(8,128)(2,1)S(1)}, bf16[128,512]{1,0:T(8,128)(2,1)S(1)}, u32[]{:S(2)}, u32[]{:S(2)}) collective-permute-start(bf16[128,512]{1,0:T(8,128)(2,1)S(1)} %get-tuple-element.78), channel_id=1, source_target_pairs={{0,1},{1,0},{2,3},{3,2},{4,5},{5,4},{6,7},{7,6},{8,9},{9,8},{10,11... | collective-permute-start | bytes 393224 | tf_op jit(solution)/shard_map/ppermute | solution.py:222
  126.0 8.9 %collective-permute-start.26 = (bf16[128,512]{1,0:T(8,128)(2,1)S(1)}, bf16[128,512]{1,0:T(8,128)(2,1)S(1)}, u32[]{:S(2)}, u32[]{:S(2)}) collective-permute-start(bf16[128,512]{1,0:T(8,128)(2,1)S(1)} %get-tuple-element.76), channel_id=1, source_target_pairs={{0,3},{1,2},{2,1},{3,0},{4,7},{5,6},{6,5},{7,4},{8,11},{9,10},{10,... | collective-permute-start | bytes 393224 | tf_op jit(solution)/shard_map/ppermute | solution.py:222
  (12 other events, 85.7 us)

commit v2 on v1

--- a/solution.py
+++ b/solution.py
@@ -12,6 +12,15 @@
 WINDOW = 1024
 INNER = 2
 CHUNKS = (2, 2)
+STEPS = ("kv0", "kv1", "z0", "q0", "q1", "z1", "att0", "o0", "r0", "dx0", "att1", "o1", "r1", "dx1")
+GATES = {
+    "kv1": ("kv0",),
+    "pack": ("kv0",),
+    "q1": ("q0",),
+    "r11": ("o0",),
+    "r21": ("o1",),
+    "dx1": ("o1",),
+}
 SOFTCAP = 50.0
 TANH_SCALE = 1.0 / (12.0 * SOFTCAP)
 EXP2_SCALE = SOFTCAP * math.log2(math.e)
@@ -201,54 +210,85 @@
     )(info, *kvs, *qs)
 
 
+def after(value, *earlier):
+    leaves = [leaf for leaf in jax.tree.leaves(earlier)]
+    return lax.optimization_barrier((value, leaves))[0] if leaves else value
+
+
 def on_device(queries, keys, values, output_gradient):
     rows = queries.shape[0]
     tp = lax.axis_size("tp")
     ctx = lax.axis_size("ctx")
     members = INNER * tp
-    planes = ctx // INNER
     heads_dev = keys.shape[1] // HEAD // members
     group = queries.shape[1] // keys.shape[1]
     hops = max(1, WINDOW // (members * rows))
     device = lax.axis_index("ctx") * tp + lax.axis_index("tp")
-    me = device % members
-    plane = device // members
-    info = jnp.stack([me, plane]).astype(jnp.int32)
+    info = jnp.stack([device % members, device // members]).astype(jnp.int32)
     axes = ("ctx", "tp")
-
-    def swap(piece, m):
-        if m == 0:
-            return piece
-        return lax.ppermute(piece, axes, [(i, i ^ m) for i in range(ctx * tp)])
+    count = len(CHUNKS)
+
+    def swap(pieces):
+        pairs = [[(i, i ^ m) for i in range(ctx * tp)] for m in range(members)]
+        return [pieces[0]] + [lax.ppermute(pieces[m], axes, pairs[m]) for m in range(1, members)]
 
     def hop(array, by):
         pairs = [(i, i + by * members) for i in range(ctx * tp) if 0 <= i + by * members < ctx * tp]
         return lax.ppermute(array, axes, pairs)
 
     kv_packed = pack(info, keys, values, CHUNKS, members, 1, heads_dev)
-    q_packed = pack(info, queries, output_gradient, CHUNKS, members, group, heads_dev)
-    kv_own = []
-    for c in range(len(CHUNKS)):
-        kv_own.append(jnp.stack([swap(kv_packed[c * members + m], m) for m in range(members)]))
-    q_pieces = []
-    kv_all = []
-    for c in range(len(CHUNKS)):
-        halo = [kv_own[c]]
-        for _ in range(hops):
-            halo.insert(0, hop(halo[0], 1))
-        kv_all.append(halo)
-        q_pieces.append([swap(q_packed[c * members + m], m) for m in range(members)])
-    o_pieces, dkv_pieces = [], []
-    for c in range(len(CHUNKS)):
-        results = attention(info, kv_all[c], q_pieces[c], group)
-        os, dkvs = results[:members], results[members:]
-        o_pieces += [swap(os[m], m) for m in range(members)]
-        carried = dkvs[0]
-        for k in range(1, hops + 1):
-            carried = (hop(carried, -1).astype(F32) + dkvs[k].astype(F32)).astype(BF16)
-        dkv_pieces += [swap(carried[m], m) for m in range(members)]
-    attended, query_grad = unpack(info, o_pieces, CHUNKS, members, group, heads_dev)
-    key_grad, value_grad = unpack(info, dkv_pieces, CHUNKS, members, 1, heads_dev)
+    done = {}
+    q_packed = []
+
+    def gated(value, step):
+        earlier = [done[name] for name in GATES.get(step, ()) if name in done]
+        return after(value, *earlier)
+
+    def run(step):
+        kind, c = step[:-1], int(step[-1])
+        if kind == "kv":
+            done[step] = swap(gated(kv_packed[c * members : (c + 1) * members], step))
+        elif kind == "q":
+            if not q_packed:
+                q_packed.extend(
+                    pack(info, gated(queries, "pack"), output_gradient, CHUNKS, members, group, heads_dev)
+                )
+            done[step] = swap(gated(q_packed[c * members : (c + 1) * members], step))
+        elif kind.startswith("z"):
+            k = int(kind[1:])
+            if k == 1:
+                done[f"z0{c}"] = jnp.stack(done[f"kv{c}"])
+            done[step] = hop(gated(done[f"z{k - 1}{c}"], step), 1)
+        elif kind == "att":
+            halo = [done[f"z{k}{c}"] for k in range(hops, -1, -1)]
+            halo, pieces = gated((halo, done[f"q{c}"]), step)
+            results = attention(info, halo, pieces, group)
+            done[step] = results[members:]
+            done[f"os{c}"] = results[:members]
+            done[f"r0{c}"] = results[members]
+        elif kind == "o":
+            done[step] = swap(gated(done[f"os{c}"], step))
+        elif kind.startswith("r"):
+            k = int(kind[1:])
+            arrived = hop(gated(done[f"r{k - 1}{c}"], step), -1)
+            done[step] = (arrived.astype(F32) + done[f"att{c}"][k].astype(F32)).astype(BF16)
+        else:
+            carried = gated(done[f"r{hops}{c}"], step)
+            done[step] = swap([carried[m] for m in range(members)])
+
+    for step in STEPS:
+        kind = step[:-1]
+        if kind in ("z", "r"):
+            for k in range(1, hops + 1):
+                run(f"{kind}{k}{step[-1]}")
+        else:
+            run(step)
+    attended, query_grad = unpack(
+        info, sum([done[f"o{c}"] for c in range(count)], []), CHUNKS, members, group, heads_dev
+    )
+    key_grad, value_grad = unpack(
+        info, sum([done[f"dx{c}"] for c in range(count)], []), CHUNKS, members, 1, heads_dev
+    )
     return attended, query_grad, key_grad, value_grad
 
 

time: 137 us -> 130 us (0.949)
  waiting for transfers between devices: 66.1 us -> 59.6 us
    ppermute x24, waiting for transfers between devices: 25.5 us -> 20.9 us  [swap(): lax.ppermute(pieces[m], axes, pairs[m])]
    ppermute x8, waiting for transfers between devices: 40.6 us -> 38.7 us  [hop(): return lax.ppermute(array, axes, pairs)]
  transfers between devices with their start and end apart: 32 -> 32, of which waited for: 15 -> 13; matrix products, arithmetic and copies ran while one was open for 1% -> 1% of each run, Pallas kernels for 19% -> 20%
where the time goes in v2:
time: 130 us; the launch traced here: 129 us
  waiting for transfers between devices  59.6 us (46%)
  starting transfers between devices  37.8 us (29%)
  Pallas kernels  28.2 us (22%)
  local copies, waits for them, and re-layouts  2.16 us (2%)
    ppermute x8, waiting for transfers between devices, hop(): return lax.ppermute(array, axes, pairs)  38.7 us
    pallas_call x2, Pallas kernels, attention(): pl.pallas_call(functools.partial(attention_kernel, members, planes - 1, g...  22.1 us
    ppermute x8, starting transfers between devices, hop(): return lax.ppermute(array, axes, pairs)  21 us
    ppermute x24, waiting for transfers between devices, swap(): lax.ppermute(pieces[m], axes, pairs[m])  20.9 us
    ppermute x24, starting transfers between devices, swap(): lax.ppermute(pieces[m], axes, pairs[m])  16.8 us
    pallas_call x2, Pallas kernels, unpack(): pl.pallas_call(functools.partial(unpack_kernel, chunks, members, group, h...  4.15 us
  transfers between devices with their start and end apart: 32, of which 13 were waited for; matrix products, arithmetic and copies ran while one was open for 1% of the time, Pallas kernels for 20%

profile of v2, /device:TPU:0, one launch (start us, length us, event | category | flops | bytes accessed | tf_op | source)
XLA Modules:
  0.0 129.5 jit_solution(14298498205741070534)
XLA Ops:
  4.2 2.6 %collective-permute-start.1 = (bf16[128,512]{1,0:T(8,128)(2,1)S(1)}, bf16[128,512]{1,0:T(8,128)(2,1)S(1)}, u32[]{:S(2)}, u32[]{:S(2)}) collective-permute-start(bf16[128,512]{1,0:T(8,128)(2,1)S(1)} %get-tuple-element.52), channel_id=1, source_target_pairs={{0,2},{1,3},{2,0},{3,1},{4,6},{5,7},{6,4},{7,5},{8,10},{9,11},{10,... | collective-permute-start | bytes 393224 | tf_op jit(solution)/shard_map/ppermute | solution.py:233
  6.8 4.3 %collective-permute-done.1 = bf16[128,512]{1,0:T(8,128)(2,1)S(1)} collective-permute-done((bf16[128,512]{1,0:T(8,128)(2,1)S(1)}, bf16[128,512]{1,0:T(8,128)(2,1)S(1)}, u32[]{:S(2)}, u32[]{:S(2)}) %collective-permute-start.1) | collective-permute-done | bytes 131104 | tf_op jit(solution)/shard_map/ppermute | solution.py:233
  11.1 2.3 %collective-permute-done.2 = bf16[128,512]{1,0:T(8,128)(2,1)S(1)} collective-permute-done((bf16[128,512]{1,0:T(8,128)(2,1)S(1)}, bf16[128,512]{1,0:T(8,128)(2,1)S(1)}, u32[]{:S(2)}, u32[]{:S(2)}) %collective-permute-start.2) | collective-permute-done | bytes 131104 | tf_op jit(solution)/shard_map/ppermute | solution.py:233
  13.4 3.7 %collective-permute-start.3 = (bf16[4,128,512]{2,1,0:T(8,128)(2,1)S(1)}, bf16[4,128,512]{2,1,0:T(8,128)(2,1)S(1)}, u32[]{:S(2)}, u32[]{:S(2)}) collective-permute-start(bf16[4,128,512]{2,1,0:T(8,128)(2,1)S(1)} %pad_maximum_fusion.refs_2_), channel_id=1, source_target_pairs={{0,4},{1,5},{2,6},{3,7},{4,8},{5,9},{6,10},{7,11},{8,12},{9,13},{1... | collective-permute-start | bytes 1572872 | tf_op jit(solution)/shard_map/ppermute | solution.py:237
  17.2 1.6 %collective-permute-start.12 = (bf16[128,512]{1,0:T(8,128)(2,1)S(1)}, bf16[128,512]{1,0:T(8,128)(2,1)S(1)}, u32[]{:S(2)}, u32[]{:S(2)}) collective-permute-start(bf16[128,512]{1,0:T(8,128)(2,1)S(1)} %get-tuple-element.69), channel_id=1, source_target_pairs={{0,2},{1,3},{2,0},{3,1},{4,6},{5,7},{6,4},{7,5},{8,10},{9,11},{10,... | collective-permute-start | bytes 393224 | tf_op jit(solution)/shard_map/ppermute | solution.py:233
  19.1 4.5 %collective-permute-done.12 = bf16[128,512]{1,0:T(8,128)(2,1)S(1)} collective-permute-done((bf16[128,512]{1,0:T(8,128)(2,1)S(1)}, bf16[128,512]{1,0:T(8,128)(2,1)S(1)}, u32[]{:S(2)}, u32[]{:S(2)}) %collective-permute-start.12) | collective-permute-done | bytes 131104 | tf_op jit(solution)/shard_map/ppermute | solution.py:233
  23.6 1.9 %collective-permute-done.13 = bf16[128,512]{1,0:T(8,128)(2,1)S(1)} collective-permute-done((bf16[128,512]{1,0:T(8,128)(2,1)S(1)}, bf16[128,512]{1,0:T(8,128)(2,1)S(1)}, u32[]{:S(2)}, u32[]{:S(2)}) %collective-permute-start.13) | collective-permute-done | bytes 131104 | tf_op jit(solution)/shard_map/ppermute | solution.py:233
  25.6 3.5 %collective-permute-start.14 = (bf16[4,128,512]{2,1,0:T(8,128)(2,1)S(1)}, bf16[4,128,512]{2,1,0:T(8,128)(2,1)S(1)}, u32[]{:S(2)}, u32[]{:S(2)}) collective-permute-start(bf16[4,128,512]{2,1,0:T(8,128)(2,1)S(1)} %pad_maximum_fusion.1.refs_2_), channel_id=1, source_target_pairs={{0,4},{1,5},{2,6},{3,7},{4,8},{5,9},{6,10},{7,11},{8,12},{9,13},{1... | collective-permute-start | bytes 1572872 | tf_op jit(solution)/shard_map/ppermute | solution.py:237
  29.1 4.1 %collective-permute-start.4 = (bf16[4,128,512]{2,1,0:T(8,128)(2,1)S(1)}, bf16[4,128,512]{2,1,0:T(8,128)(2,1)S(1)}, u32[]{:S(2)}, u32[]{:S(2)}) collective-permute-start(bf16[4,128,512]{2,1,0:T(8,128)(2,1)S(1)} %collective-permute-done.3.refs_1_), channel_id=1, source_target_pairs={{0,4},{1,5},{2,6},{3,7},{4,8},{5,9},{6,10},{7,11},{8,12},{9,13},{1... | collective-permute-start | bytes 1572872 | tf_op jit(solution)/shard_map/ppermute | solution.py:237
  34.4 1.6 %collective-permute-start.6 = (bf16[128,1024]{1,0:T(8,128)(2,1)S(1)}, bf16[128,1024]{1,0:T(8,128)(2,1)S(1)}, u32[]{:S(2)}, u32[]{:S(2)}) collective-permute-start(bf16[128,1024]{1,0:T(8,128)(2,1)S(1)} %get-tuple-element.57), channel_id=1, source_target_pairs={{0,2},{1,3},{2,0},{3,1},{4,6},{5,7},{6,4},{7,5},{8,10},{9,11},{10,... | collective-permute-start | bytes 786440 | tf_op jit(solution)/shard_map/ppermute | solution.py:233
  36.2 5.0 %collective-permute-done.14.refs_1_ = bf16[4,128,512]{2,1,0:T(8,128)(2,1)S(1)} collective-permute-done((bf16[4,128,512]{2,1,0:T(8,128)(2,1)S(1)}, bf16[4,128,512]{2,1,0:T(8,128)(2,1)S(1)}, u32[]{:S(2)}, u32[]{:S(2)}) %collective-permute-start.14) | collective-permute-done | bytes 524320 | tf_op jit(solution)/shard_map/ppermute | solution.py:237
  41.2 4.4 %collective-permute-start.15 = (bf16[4,128,512]{2,1,0:T(8,128)(2,1)S(1)}, bf16[4,128,512]{2,1,0:T(8,128)(2,1)S(1)}, u32[]{:S(2)}, u32[]{:S(2)}) collective-permute-start(bf16[4,128,512]{2,1,0:T(8,128)(2,1)S(1)} %collective-permute-done.14.refs_1_), channel_id=1, source_target_pairs={{0,4},{1,5},{2,6},{3,7},{4,8},{5,9},{6,10},{7,11},{8,12},{9,13},{1... | collective-permute-start | bytes 1572872 | tf_op jit(solution)/shard_map/ppermute | solution.py:237
  45.7 2.6 %collective-permute-done.7.refs_6_ = bf16[128,1024]{1,0:T(8,128)(2,1)S(1)} collective-permute-done((bf16[128,1024]{1,0:T(8,128)(2,1)S(1)}, bf16[128,1024]{1,0:T(8,128)(2,1)S(1)}, u32[]{:S(2)}, u32[]{:S(2)}) %collective-permute-start.7) | collective-permute-done | bytes 262176 | tf_op jit(solution)/shard_map/ppermute | solution.py:233
  50.1 2.4 %collective-permute-done.4.refs_0_ = bf16[4,128,512]{2,1,0:T(8,128)(2,1)S(1)} collective-permute-done((bf16[4,128,512]{2,1,0:T(8,128)(2,1)S(1)}, bf16[4,128,512]{2,1,0:T(8,128)(2,1)S(1)}, u32[]{:S(2)}, u32[]{:S(2)}) %collective-permute-start.4) | collective-permute-done | bytes 524320 | tf_op jit(solution)/shard_map/ppermute | solution.py:237
  52.5 11.0 %attention.2 = (bf16[128,1024]{1,0:T(8,128)(2,1)S(1)}, bf16[128,1024]{1,0:T(8,128)(2,1)S(1)}, bf16[128,1024]{1,0:T(8,128)(2,1)S(1)}, bf16[128,1024]{1,0:T(8,128)...) custom-call(s32[2]{0:T(128)S(1)} %pad_add_fusion.info, ...), custom_call_target="tpu_custom_call" | custom-call | flops 3623878656 | bytes 5242880 | tf_op jit(solution)/shard_map/attention/pallas_call | solution.py:185
  65.1 1.5 %collective-permute-start.9 = (bf16[128,1024]{1,0:T(8,128)(2,1)S(1)}, bf16[128,1024]{1,0:T(8,128)(2,1)S(1)}, u32[]{:S(2)}, u32[]{:S(2)}) collective-permute-start(bf16[128,1024]{1,0:T(8,128)(2,1)S(1)} %get-tuple-element.61), channel_id=1, source_target_pairs={{0,2},{1,3},{2,0},{3,1},{4,6},{5,7},{6,4},{7,5},{8,10},{9,11},{10,... | collective-permute-start | bytes 786440 | tf_op jit(solution)/shard_map/ppermute | solution.py:233
  67.0 11.0 %attention.3 = (bf16[128,1024]{1,0:T(8,128)(2,1)S(1)}, bf16[128,1024]{1,0:T(8,128)(2,1)S(1)}, bf16[128,1024]{1,0:T(8,128)(2,1)S(1)}, bf16[128,1024]{1,0:T(8,128)...) custom-call(s32[2]{0:T(128)S(1)} %pad_add_fusion.info, ...), custom_call_target="tpu_custom_call" | custom-call | flops 3623878656 | bytes 5242880 | tf_op jit(solution)/shard_map/attention/pallas_call | solution.py:185
  83.8 12.8 %collective-permute-done.27 = bf16[4,128,512]{2,1,0:T(8,128)(2,1)S(1)} collective-permute-done((bf16[4,128,512]{2,1,0:T(8,128)(2,1)S(1)}, bf16[4,128,512]{2,1,0:T(8,128)(2,1)S(1)}, u32[]{:S(2)}, u32[]{:S(2)}) %collective-permute-start.27) | collective-permute-done | bytes 524320 | tf_op jit(solution)/shard_map/ppermute | solution.py:237
  98.1 9.8 %collective-permute-done.23 = bf16[4,128,512]{2,1,0:T(8,128)(2,1)S(1)} collective-permute-done((bf16[4,128,512]{2,1,0:T(8,128)(2,1)S(1)}, bf16[4,128,512]{2,1,0:T(8,128)(2,1)S(1)}, u32[]{:S(2)}, u32[]{:S(2)}) %collective-permute-start.23) | collective-permute-done | bytes 524320 | tf_op jit(solution)/shard_map/ppermute | solution.py:237
  110.0 8.8 %collective-permute-done.28 = bf16[4,128,512]{2,1,0:T(8,128)(2,1)S(1)} collective-permute-done((bf16[4,128,512]{2,1,0:T(8,128)(2,1)S(1)}, bf16[4,128,512]{2,1,0:T(8,128)(2,1)S(1)}, u32[]{:S(2)}, u32[]{:S(2)}) %collective-permute-start.28) | collective-permute-done | bytes 524320 | tf_op jit(solution)/shard_map/ppermute | solution.py:237
  120.9 2.4 %unpack.2 = (bf16[128,4096]{1,0:T(8,128)(2,1)}, bf16[128,4096]{1,0:T(8,128)(2,1)}) custom-call(s32[2]{0:T(128)S(1)} %pad_add_fusion.info, bf16[128,1024]{1,0:T(8,128)(2,1)S(1)} %get-tuple-element.59.refs_0_, bf16[128,1024]{1,0:T(8,128)(2,1)S(1)} %collective-permute-done.8.refs_1_, bf16[128,1024]{1,0:T(8,128)(2,1)S(1)} %collective-permute-done.9.refs_2_, ...), custom_call_target="tpu_custom_call" | custom-call | tf_op jit(solution)/shard_map/unpack/pallas_call | solution.py:96
  123.3 1.5 %collective-permute-done.31.refs_7_ = bf16[128,512]{1,0:T(8,128)(2,1)S(1)} collective-permute-done((bf16[128,512]{1,0:T(8,128)(2,1)S(1)}, bf16[128,512]{1,0:T(8,128)(2,1)S(1)}, u32[]{:S(2)}, u32[]{:S(2)}) %collective-permute-start.31) | collective-permute-done | bytes 131104 | tf_op jit(solution)/shard_map/ppermute | solution.py:233
  124.8 2.8 %collective-permute-done.30.refs_6_ = bf16[128,512]{1,0:T(8,128)(2,1)S(1)} collective-permute-done((bf16[128,512]{1,0:T(8,128)(2,1)S(1)}, bf16[128,512]{1,0:T(8,128)(2,1)S(1)}, u32[]{:S(2)}, u32[]{:S(2)}) %collective-permute-start.30) | collective-permute-done | bytes 131104 | tf_op jit(solution)/shard_map/ppermute | solution.py:233
  127.7 1.8 %unpack.3 = (bf16[128,2048]{1,0:T(8,128)(2,1)}, bf16[128,2048]{1,0:T(8,128)(2,1)}) custom-call(s32[2]{0:T(128)S(1)} %pad_add_fusion.info, bf16[128,512]{1,0:T(8,128)(2,1)S(1)} %get-tuple-element.103.refs_0_, bf16[128,512]{1,0:T(8,128)(2,1)S(1)} %collective-permute-done.24.refs_1_, bf16[128,512]{1,0:T(8,128)(2,1)S(1)} %collective-permute-done.25.refs_2_, ...), custom_call_target="tpu_custom_call" | custom-call | tf_op jit(solution)/shard_map/unpack/pallas_call | solution.py:96
  (63 shorter events, 20.8 us)
Async XLA Ops:
  13.4 15.6 %collective-permute-start.3 = (bf16[4,128,512]{2,1,0:T(8,128)(2,1)S(1)}, bf16[4,128,512]{2,1,0:T(8,128)(2,1)S(1)}, u32[]{:S(2)}, u32[]{:S(2)}) collective-permute-start(bf16[4,128,512]{2,1,0:T(8,128)(2,1)S(1)} %pad_maximum_fusion.refs_2_), channel_id=1, source_target_pairs={{0,4},{1,5},{2,6},{3,7},{4,8},{5,9},{6,10},{7,11},{8,12},{9,13},{1... | collective-permute-start | bytes 1572872 | tf_op jit(solution)/shard_map/ppermute | solution.py:237
  25.6 15.7 %collective-permute-start.14 = (bf16[4,128,512]{2,1,0:T(8,128)(2,1)S(1)}, bf16[4,128,512]{2,1,0:T(8,128)(2,1)S(1)}, u32[]{:S(2)}, u32[]{:S(2)}) collective-permute-start(bf16[4,128,512]{2,1,0:T(8,128)(2,1)S(1)} %pad_maximum_fusion.1.refs_2_), channel_id=1, source_target_pairs={{0,4},{1,5},{2,6},{3,7},{4,8},{5,9},{6,10},{7,11},{8,12},{9,13},{1... | collective-permute-start | bytes 1572872 | tf_op jit(solution)/shard_map/ppermute | solution.py:237
  29.1 23.4 %collective-permute-start.4 = (bf16[4,128,512]{2,1,0:T(8,128)(2,1)S(1)}, bf16[4,128,512]{2,1,0:T(8,128)(2,1)S(1)}, u32[]{:S(2)}, u32[]{:S(2)}) collective-permute-start(bf16[4,128,512]{2,1,0:T(8,128)(2,1)S(1)} %collective-permute-done.3.refs_1_), channel_id=1, source_target_pairs={{0,4},{1,5},{2,6},{3,7},{4,8},{5,9},{6,10},{7,11},{8,12},{9,13},{1... | collective-permute-start | bytes 1572872 | tf_op jit(solution)/shard_map/ppermute | solution.py:237
  34.3 11.4 %collective-permute-start.5 = (bf16[128,1024]{1,0:T(8,128)(2,1)S(1)}, bf16[128,1024]{1,0:T(8,128)(2,1)S(1)}, u32[]{:S(2)}, u32[]{:S(2)}) collective-permute-start(bf16[128,1024]{1,0:T(8,128)(2,1)S(1)} %get-tuple-element.56), channel_id=1, source_target_pairs={{0,1},{1,0},{2,3},{3,2},{4,5},{5,4},{6,7},{7,6},{8,9},{9,8},{10,11... | collective-permute-start | bytes 786440 | tf_op jit(solution)/shard_map/ppermute | solution.py:233
  34.4 11.3 %collective-permute-start.6 = (bf16[128,1024]{1,0:T(8,128)(2,1)S(1)}, bf16[128,1024]{1,0:T(8,128)(2,1)S(1)}, u32[]{:S(2)}, u32[]{:S(2)}) collective-permute-start(bf16[128,1024]{1,0:T(8,128)(2,1)S(1)} %get-tuple-element.57), channel_id=1, source_target_pairs={{0,2},{1,3},{2,0},{3,1},{4,6},{5,7},{6,4},{7,5},{8,10},{9,11},{10,... | collective-permute-start | bytes 786440 | tf_op jit(solution)/shard_map/ppermute | solution.py:233
  35.9 12.3 %collective-permute-start.7 = (bf16[128,1024]{1,0:T(8,128)(2,1)S(1)}, bf16[128,1024]{1,0:T(8,128)(2,1)S(1)}, u32[]{:S(2)}, u32[]{:S(2)}) collective-permute-start(bf16[128,1024]{1,0:T(8,128)(2,1)S(1)} %get-tuple-element.58), channel_id=1, source_target_pairs={{0,3},{1,2},{2,1},{3,0},{4,7},{5,6},{6,5},{7,4},{8,11},{9,10},{10,... | collective-permute-start | bytes 786440 | tf_op jit(solution)/shard_map/ppermute | solution.py:233
  41.2 25.7 %collective-permute-start.15 = (bf16[4,128,512]{2,1,0:T(8,128)(2,1)S(1)}, bf16[4,128,512]{2,1,0:T(8,128)(2,1)S(1)}, u32[]{:S(2)}, u32[]{:S(2)}) collective-permute-start(bf16[4,128,512]{2,1,0:T(8,128)(2,1)S(1)} %collective-permute-done.14.refs_1_), channel_id=1, source_target_pairs={{0,4},{1,5},{2,6},{3,7},{4,8},{5,9},{6,10},{7,11},{8,12},{9,13},{1... | collective-permute-start | bytes 1572872 | tf_op jit(solution)/shard_map/ppermute | solution.py:237
  48.3 16.7 %collective-permute-start.16 = (bf16[128,1024]{1,0:T(8,128)(2,1)S(1)}, bf16[128,1024]{1,0:T(8,128)(2,1)S(1)}, u32[]{:S(2)}, u32[]{:S(2)}) collective-permute-start(bf16[128,1024]{1,0:T(8,128)(2,1)S(1)} %get-tuple-element.76), channel_id=1, source_target_pairs={{0,1},{1,0},{2,3},{3,2},{4,5},{5,4},{6,7},{7,6},{8,9},{9,8},{10,11... | collective-permute-start | bytes 786440 | tf_op jit(solution)/shard_map/ppermute | solution.py:233
  48.5 16.6 %collective-permute-start.17 = (bf16[128,1024]{1,0:T(8,128)(2,1)S(1)}, bf16[128,1024]{1,0:T(8,128)(2,1)S(1)}, u32[]{:S(2)}, u32[]{:S(2)}) collective-permute-start(bf16[128,1024]{1,0:T(8,128)(2,1)S(1)} %get-tuple-element.77), channel_id=1, source_target_pairs={{0,2},{1,3},{2,0},{3,1},{4,6},{5,7},{6,4},{7,5},{8,10},{9,11},{10,... | collective-permute-start | bytes 786440 | tf_op jit(solution)/shard_map/ppermute | solution.py:233
  50.0 16.6 %collective-permute-start.18 = (bf16[128,1024]{1,0:T(8,128)(2,1)S(1)}, bf16[128,1024]{1,0:T(8,128)(2,1)S(1)}, u32[]{:S(2)}, u32[]{:S(2)}) collective-permute-start(bf16[128,1024]{1,0:T(8,128)(2,1)S(1)} %get-tuple-element.78), channel_id=1, source_target_pairs={{0,3},{1,2},{2,1},{3,0},{4,7},{5,6},{6,5},{7,4},{8,11},{9,10},{10,... | collective-permute-start | bytes 786440 | tf_op jit(solution)/shard_map/ppermute | solution.py:233
  63.5 16.7 %collective-permute-start.22 = (bf16[4,128,512]{2,1,0:T(8,128)(2,1)S(1)}, bf16[4,128,512]{2,1,0:T(8,128)(2,1)S(1)}, u32[]{:S(2)}, u32[]{:S(2)}) collective-permute-start(bf16[4,128,512]{2,1,0:T(8,128)(2,1)S(1)} %get-tuple-element.85), channel_id=1, source_target_pairs={{4,0},{5,1},{6,2},{7,3},{8,4},{9,5},{10,6},{11,7},{12,8},{13,9},{1... | collective-permute-start | bytes 1572872 | tf_op jit(solution)/shard_map/ppermute | solution.py:237
  65.0 13.0 %collective-permute-start.8 = (bf16[128,1024]{1,0:T(8,128)(2,1)S(1)}, bf16[128,1024]{1,0:T(8,128)(2,1)S(1)}, u32[]{:S(2)}, u32[]{:S(2)}) collective-permute-start(bf16[128,1024]{1,0:T(8,128)(2,1)S(1)} %get-tuple-element.60), channel_id=1, source_target_pairs={{0,1},{1,0},{2,3},{3,2},{4,5},{5,4},{6,7},{7,6},{8,9},{9,8},{10,11... | collective-permute-start | bytes 786440 | tf_op jit(solution)/shard_map/ppermute | solution.py:233
  65.1 12.9 %collective-permute-start.9 = (bf16[128,1024]{1,0:T(8,128)(2,1)S(1)}, bf16[128,1024]{1,0:T(8,128)(2,1)S(1)}, u32[]{:S(2)}, u32[]{:S(2)}) collective-permute-start(bf16[128,1024]{1,0:T(8,128)(2,1)S(1)} %get-tuple-element.61), channel_id=1, source_target_pairs={{0,2},{1,3},{2,0},{3,1},{4,6},{5,7},{6,4},{7,5},{8,10},{9,11},{10,... | collective-permute-start | bytes 786440 | tf_op jit(solution)/shard_map/ppermute | solution.py:233
  66.7 12.3 %collective-permute-start.10 = (bf16[128,1024]{1,0:T(8,128)(2,1)S(1)}, bf16[128,1024]{1,0:T(8,128)(2,1)S(1)}, u32[]{:S(2)}, u32[]{:S(2)}) collective-permute-start(bf16[128,1024]{1,0:T(8,128)(2,1)S(1)} %get-tuple-element.62), channel_id=1, source_target_pairs={{0,3},{1,2},{2,1},{3,0},{4,7},{5,6},{6,5},{7,4},{8,11},{9,10},{10,... | collective-permute-start | bytes 786440 | tf_op jit(solution)/shard_map/ppermute | solution.py:233
  79.0 17.7 %collective-permute-start.27 = (bf16[4,128,512]{2,1,0:T(8,128)(2,1)S(1)}, bf16[4,128,512]{2,1,0:T(8,128)(2,1)S(1)}, u32[]{:S(2)}, u32[]{:S(2)}) collective-permute-start(bf16[4,128,512]{2,1,0:T(8,128)(2,1)S(1)} %get-tuple-element.89), channel_id=1, source_target_pairs={{4,0},{5,1},{6,2},{7,3},{8,4},{9,5},{10,6},{11,7},{12,8},{13,9},{1... | collective-permute-start | bytes 1572872 | tf_op jit(solution)/shard_map/ppermute | solution.py:237
  80.4 27.5 %collective-permute-start.23 = (bf16[4,128,512]{2,1,0:T(8,128)(2,1)S(1)}, bf16[4,128,512]{2,1,0:T(8,128)(2,1)S(1)}, u32[]{:S(2)}, u32[]{:S(2)}) collective-permute-start(bf16[4,128,512]{2,1,0:T(8,128)(2,1)S(1)} %add_convert_fusion.3), channel_id=1, source_target_pairs={{4,0},{5,1},{6,2},{7,3},{8,4},{9,5},{10,6},{11,7},{12,8},{13,9},{1... | collective-permute-start | bytes 1572872 | tf_op jit(solution)/shard_map/ppermute | solution.py:237
  81.7 15.1 %collective-permute-start.19 = (bf16[128,1024]{1,0:T(8,128)(2,1)S(1)}, bf16[128,1024]{1,0:T(8,128)(2,1)S(1)}, u32[]{:S(2)}, u32[]{:S(2)}) collective-permute-start(bf16[128,1024]{1,0:T(8,128)(2,1)S(1)} %get-tuple-element.80), channel_id=1, source_target_pairs={{0,1},{1,0},{2,3},{3,2},{4,5},{5,4},{6,7},{7,6},{8,9},{9,8},{10,11... | collective-permute-start | bytes 786440 | tf_op jit(solution)/shard_map/ppermute | solution.py:233
  82.4 14.5 %collective-permute-start.20 = (bf16[128,1024]{1,0:T(8,128)(2,1)S(1)}, bf16[128,1024]{1,0:T(8,128)(2,1)S(1)}, u32[]{:S(2)}, u32[]{:S(2)}) collective-permute-start(bf16[128,1024]{1,0:T(8,128)(2,1)S(1)} %get-tuple-element.81), channel_id=1, source_target_pairs={{0,2},{1,3},{2,0},{3,1},{4,6},{5,7},{6,4},{7,5},{8,10},{9,11},{10,... | collective-permute-start | bytes 786440 | tf_op jit(solution)/shard_map/ppermute | solution.py:233
  83.8 13.0 %collective-permute-start.21 = (bf16[128,1024]{1,0:T(8,128)(2,1)S(1)}, bf16[128,1024]{1,0:T(8,128)(2,1)S(1)}, u32[]{:S(2)}, u32[]{:S(2)}) collective-permute-start(bf16[128,1024]{1,0:T(8,128)(2,1)S(1)} %get-tuple-element.82), channel_id=1, source_target_pairs={{0,3},{1,2},{2,1},{3,0},{4,7},{5,6},{6,5},{7,4},{8,11},{9,10},{10,... | collective-permute-start | bytes 786440 | tf_op jit(solution)/shard_map/ppermute | solution.py:233
  96.8 22.0 %collective-permute-start.28 = (bf16[4,128,512]{2,1,0:T(8,128)(2,1)S(1)}, bf16[4,128,512]{2,1,0:T(8,128)(2,1)S(1)}, u32[]{:S(2)}, u32[]{:S(2)}) collective-permute-start(bf16[4,128,512]{2,1,0:T(8,128)(2,1)S(1)} %add_convert_fusion.1), channel_id=1, source_target_pairs={{4,0},{5,1},{6,2},{7,3},{8,4},{9,5},{10,6},{11,7},{12,8},{13,9},{1... | collective-permute-start | bytes 1572872 | tf_op jit(solution)/shard_map/ppermute | solution.py:237
  108.1 12.5 %collective-permute-start.26 = (bf16[128,512]{1,0:T(8,128)(2,1)S(1)}, bf16[128,512]{1,0:T(8,128)(2,1)S(1)}, u32[]{:S(2)}, u32[]{:S(2)}) collective-permute-start(bf16[128,512]{1,0:T(8,128)(2,1)S(1)} %get-tuple-element.100), channel_id=1, source_target_pairs={{0,3},{1,2},{2,1},{3,0},{4,7},{5,6},{6,5},{7,4},{8,11},{9,10},{10,... | collective-permute-start | bytes 393224 | tf_op jit(solution)/shard_map/ppermute | solution.py:233
  108.7 14.6 %collective-permute-start.25 = (bf16[128,512]{1,0:T(8,128)(2,1)S(1)}, bf16[128,512]{1,0:T(8,128)(2,1)S(1)}, u32[]{:S(2)}, u32[]{:S(2)}) collective-permute-start(bf16[128,512]{1,0:T(8,128)(2,1)S(1)} %get-tuple-element.101), channel_id=1, source_target_pairs={{0,2},{1,3},{2,0},{3,1},{4,6},{5,7},{6,4},{7,5},{8,10},{9,11},{10,... | collective-permute-start | bytes 393224 | tf_op jit(solution)/shard_map/ppermute | solution.py:233
  109.7 13.6 %collective-permute-start.24 = (bf16[128,512]{1,0:T(8,128)(2,1)S(1)}, bf16[128,512]{1,0:T(8,128)(2,1)S(1)}, u32[]{:S(2)}, u32[]{:S(2)}) collective-permute-start(bf16[128,512]{1,0:T(8,128)(2,1)S(1)} %get-tuple-element.102), channel_id=1, source_target_pairs={{0,1},{1,0},{2,3},{3,2},{4,5},{5,4},{6,7},{7,6},{8,9},{9,8},{10,11... | collective-permute-start | bytes 393224 | tf_op jit(solution)/shard_map/ppermute | solution.py:233
  120.0 7.7 %collective-permute-start.30 = (bf16[128,512]{1,0:T(8,128)(2,1)S(1)}, bf16[128,512]{1,0:T(8,128)(2,1)S(1)}, u32[]{:S(2)}, u32[]{:S(2)}) collective-permute-start(bf16[128,512]{1,0:T(8,128)(2,1)S(1)} %get-tuple-element.97), channel_id=1, source_target_pairs={{0,2},{1,3},{2,0},{3,1},{4,6},{5,7},{6,4},{7,5},{8,10},{9,11},{10,... | collective-permute-start | bytes 393224 | tf_op jit(solution)/shard_map/ppermute | solution.py:233
  (12 other events, 86.3 us)

commit v3 on v2

--- a/solution.py
+++ b/solution.py
@@ -12,6 +12,7 @@
 WINDOW = 1024
 INNER = 2
 CHUNKS = (2, 2)
+CALLS = ((0, 0, 2), (1, 0, 2))
 STEPS = ("kv0", "kv1", "z0", "q0", "q1", "z1", "att0", "o0", "r0", "dx0", "att1", "o1", "r1", "dx1")
 GATES = {
     "kv1": ("kv0",),
@@ -27,6 +28,8 @@
 SCORE_SCALE = 1.0 / 12.0
 F32 = jnp.float32
 BF16 = jnp.bfloat16
+BUFFERS = 2
+JOIN = 3
 
 
 def dot(a, b, ca, cb):
@@ -109,12 +112,11 @@
     q_refs = refs[planes : planes + members]
     o_refs = refs[planes + members : planes + 2 * members]
     dkv_refs = refs[planes + 2 * members : 2 * planes + 2 * members]
-    k_s, v_s, kt_s, vt_s, dk_s, dv_s, p_s, eg_s, ds_s = refs[2 * planes + 2 * members :]
+    k_s, v_s, kt_s, vt_s, dk_s, dv_s, q_s, o_s, p_all, eg_all, ds_all = refs[2 * planes + 2 * members :]
     me = info[0]
     plane = info[1]
     blocks = WINDOW // rows + 1
     wide = group * rows
-    span = blocks * rows
     for k in range(planes):
         for s in range(members):
             at = (k * members + s) * rows
@@ -123,49 +125,93 @@
             v_s[at : at + rows, :] = piece[:, HEAD:]
             kt_s[:, at : at + rows] = piece[:, :HEAD].T
             vt_s[:, at : at + rows] = piece[:, HEAD:].T
-    dk_s[...] = jnp.zeros_like(dk_s)
-    dv_s[...] = jnp.zeros_like(dv_s)
+    for m in range(members):
+        q_s[m] = q_refs[m][...]
     key_at = lax.broadcasted_iota(jnp.int32, (rows, wide), 0)
     query_at = lax.broadcasted_iota(jnp.int32, (rows, wide), 1) % rows
-    after = key_at > query_at
-    for m in range(members):
-        s = me ^ m
-        base = pl.multiple_of(s * rows, rows)
-        q_all = q_refs[m]
+    behind = key_at > query_at
+    seen = [(plane >= hops - k).astype(F32) for k in range(planes)]
+    pairs = [(b, min(b + JOIN, blocks)) for b in range(0, blocks, JOIN)]
+    state = {}
+
+    def forward(s):
+        p_s, eg_s = p_all.at[s % BUFFERS], eg_all.at[s % BUFFERS]
+        q_all = q_s[me ^ s]
         q = jnp.concatenate([q_all[:, g * HEAD : (g + 1) * HEAD] for g in range(group)], axis=0)
         go = jnp.concatenate([q_all[:, (group + g) * HEAD : (group + g + 1) * HEAD] for g in range(group)], axis=0)
-        total = jnp.zeros((1, wide), F32)
-        for b in range(blocks):
-            score = dot(k_s[pl.ds(pl.multiple_of(base + b * rows, rows), rows), :], q, 1, 1)
-            t = jnp.tanh(score * TANH_SCALE)
-            e = jnp.exp2(t * EXP2_SCALE)
-            if b == 0:
-                e = jnp.where(after, e, 0.0)
-            if b == blocks - 1:
-                e = jnp.where(after, 0.0, e)
-            seen = plane - hops + lax.div(s + b, members) >= 0
-            total = total + jnp.where(seen, jnp.sum(e, axis=0, keepdims=True), 0.0)
-            p_s[b * rows : (b + 1) * rows, :] = e.astype(BF16)
-            eg_s[b * rows : (b + 1) * rows, :] = e * (1.0 - t * t)
+        totals = [jnp.zeros((8, wide), F32) for _ in range(planes)]
+        for low, high in pairs:
+            scores = dot(k_s[(s + low) * rows : (s + high) * rows, :], q, 1, 1)
+            for b in range(low, high):
+                score = scores[(b - low) * rows : (b - low + 1) * rows]
+                t = jnp.tanh(score * TANH_SCALE)
+                e = jnp.exp2(t * EXP2_SCALE)
+                if b == 0:
+                    e = jnp.where(behind, e, 0.0)
+                if b == blocks - 1:
+                    e = jnp.where(behind, 0.0, e)
+                k = (s + b) // members
+                totals[k] = totals[k] + jnp.sum(e.reshape(rows // 8, 8, wide), axis=0)
+                p_s[b * rows : (b + 1) * rows, :] = e.astype(BF16)
+                eg_s[b * rows : (b + 1) * rows, :] = e * (1.0 - t * t)
+            yield
+        total = sum(jnp.sum(totals[k], axis=0, keepdims=True) * seen[k] for k in range(planes))
         inverse = 1.0 / total
-        band = pl.ds(base, span)
-        p = p_s[...]
-        ot = (dot(vt_s[:, band], p, 1, 0) * inverse).astype(BF16)
         got = (go.astype(F32).T * inverse).astype(BF16)
+        ot = dot(vt_s[:, s * rows : (s + blocks) * rows], p_s[...], 1, 0)
+        ot = (ot * inverse).astype(BF16)
         gdot = jnp.sum(ot.astype(F32) * got.astype(F32), axis=0, keepdims=True)
-        for b in range(blocks):
-            part = slice(b * rows, (b + 1) * rows)
-            dp = dot(v_s[pl.ds(pl.multiple_of(base + b * rows, rows), rows), :], got, 1, 0)
-            ds_s[part, :] = ((dp - gdot) * eg_s[part, :]).astype(BF16)
-        ds = ds_s[...]
-        dqt = dot(kt_s[:, band], ds, 1, 0) * SCORE_SCALE
-        dk_s[band, :] += dot(ds, q, 1, 0)
-        dv_s[band, :] += dot(p, got, 1, 1)
         o = ot.astype(F32).T.astype(BF16)
-        dq = dqt.T.astype(BF16)
         for g in range(group):
-            o_refs[m][:, g * HEAD : (g + 1) * HEAD] = o[g * rows : (g + 1) * rows]
-            o_refs[m][:, (group + g) * HEAD : (group + g + 1) * HEAD] = dq[g * rows : (g + 1) * rows]
+            o_s[me ^ s, :, g * HEAD : (g + 1) * HEAD] = o[g * rows : (g + 1) * rows]
+        state[s] = (q, got, gdot)
+        yield
+
+    def inner(s):
+        eg_s, ds_s = eg_all.at[s % BUFFERS], ds_all.at[s % BUFFERS]
+        q, got, gdot = state[s]
+        for low, high in pairs:
+            dps = dot(v_s[(s + low) * rows : (s + high) * rows, :], got, 1, 0)
+            part = slice(low * rows, high * rows)
+            ds_s[part, :] = ((dps - gdot) * eg_s[part, :]).astype(BF16)
+            yield
+
+    def outer(s):
+        p_s, ds_s = p_all.at[s % BUFFERS], ds_all.at[s % BUFFERS]
+        q, got, gdot = state.pop(s)
+        old = slice(s * rows, (s + blocks - 1) * rows)
+        new = slice((s + blocks - 1) * rows, (s + blocks) * rows)
+
+        def add(into, value):
+            if s:
+                into[old, :] += value[: (blocks - 1) * rows]
+                into[new, :] = value[(blocks - 1) * rows :]
+            else:
+                into[: blocks * rows, :] = value
+
+        add(dv_s, dot(p_s[...], got, 1, 1))
+        yield
+        add(dk_s, dot(ds_s[...], q, 1, 0))
+        yield
+        dqt = dot(kt_s[:, s * rows : (s + blocks) * rows], ds_s[...], 1, 0)
+        dq = (dqt * SCORE_SCALE).T.astype(BF16)
+        for g in range(group):
+            o_s[me ^ s, :, (group + g) * HEAD : (group + g + 1) * HEAD] = dq[g * rows : (g + 1) * rows]
+        yield
+
+    def together(*walks):
+        walks = list(walks)
+        while walks:
+            for walk in list(walks):
+                if next(walk, walk) is walk:
+                    walks.remove(walk)
+
+    together(forward(0))
+    for s in range(members):
+        together(inner(s))
+        together(*([forward(s + 1)] if s + 1 < members else []), outer(s))
+    for m in range(members):
+        o_refs[m][...] = o_s[m]
     for k in range(planes):
         for s in range(members):
             at = (k * members + s) * rows
@@ -173,22 +219,27 @@
             dkv_refs[k][me ^ s, :, HEAD:] = dv_s[at : at + rows, :].astype(BF16)
 
 
-def attention(info, kvs, qs, group):
+def attention(info, kvs, qs, group, first=0, heads=None):
     planes, members = len(kvs), len(qs)
     rows = qs[0].shape[0]
-    heads = kvs[0].shape[2] // (2 * HEAD)
+    heads = heads or kvs[0].shape[2] // (2 * HEAD)
     keys_all = planes * members * rows
     wide = group * rows
     span = WINDOW + rows
-    kv_spec = pl.BlockSpec((members, rows, 2 * HEAD), lambda h: (0, 0, h))
-    q_spec = pl.BlockSpec((rows, 2 * group * HEAD), lambda h: (0, h))
+
+    def kv_spec(start):
+        return pl.BlockSpec((members, rows, 2 * HEAD), lambda h: (0, 0, h + start))
+
+    def q_spec(start):
+        return pl.BlockSpec((rows, 2 * group * HEAD), lambda h: (0, h + start))
+
     return pl.pallas_call(
         functools.partial(attention_kernel, members, planes - 1, group, rows),
         grid=(heads,),
-        out_shape=[jax.ShapeDtypeStruct(q.shape, BF16) for q in qs]
-        + [jax.ShapeDtypeStruct(kv.shape, BF16) for kv in kvs],
-        in_specs=[smem()] + [kv_spec] * planes + [q_spec] * members,
-        out_specs=[q_spec] * members + [kv_spec] * planes,
+        out_shape=[jax.ShapeDtypeStruct((rows, heads * 2 * group * HEAD), BF16)] * members
+        + [jax.ShapeDtypeStruct((members, rows, heads * 2 * HEAD), BF16)] * planes,
+        in_specs=[smem()] + [kv_spec(first)] * planes + [q_spec(first)] * members,
+        out_specs=[q_spec(0)] * members + [kv_spec(0)] * planes,
         scratch_shapes=[
             pltpu.VMEM((keys_all, HEAD), BF16),
             pltpu.VMEM((keys_all, HEAD), BF16),
@@ -196,14 +247,16 @@
             pltpu.VMEM((HEAD, keys_all), BF16),
             pltpu.VMEM((keys_all, HEAD), F32),
             pltpu.VMEM((keys_all, HEAD), F32),
-            pltpu.VMEM((span, wide), BF16),
-            pltpu.VMEM((span, wide), F32),
-            pltpu.VMEM((span, wide), BF16),
+            pltpu.VMEM((members, rows, 2 * group * HEAD), BF16),
+            pltpu.VMEM((members, rows, 2 * group * HEAD), BF16),
+            pltpu.VMEM((BUFFERS, span, wide), BF16),
+            pltpu.VMEM((BUFFERS, span, wide), F32),
+            pltpu.VMEM((BUFFERS, span, wide), BF16),
         ],
         compiler_params=pltpu.CompilerParams(vmem_limit_bytes=40 * 2**20),
         cost_estimate=pl.CostEstimate(
             flops=12 * heads * members * wide * span * HEAD,
-            bytes_accessed=2 * (2 * planes * kvs[0].size + 2 * members * qs[0].size),
+            bytes_accessed=2 * heads * members * rows * 4 * HEAD * (planes + group),
             transcendentals=2 * heads * members * wide * span,
         ),
         name="attention",
@@ -226,7 +279,6 @@
     device = lax.axis_index("ctx") * tp + lax.axis_index("tp")
     info = jnp.stack([device % members, device // members]).astype(jnp.int32)
     axes = ("ctx", "tp")
-    count = len(CHUNKS)
 
     def swap(pieces):
         pairs = [[(i, i ^ m) for i in range(ctx * tp)] for m in range(members)]
@@ -260,9 +312,10 @@
                 done[f"z0{c}"] = jnp.stack(done[f"kv{c}"])
             done[step] = hop(gated(done[f"z{k - 1}{c}"], step), 1)
         elif kind == "att":
-            halo = [done[f"z{k}{c}"] for k in range(hops, -1, -1)]
-            halo, pieces = gated((halo, done[f"q{c}"]), step)
-            results = attention(info, halo, pieces, group)
+            part, first, heads = CALLS[c]
+            halo = [done[f"z{k}{part}"] for k in range(hops, -1, -1)]
+            halo, pieces = gated((halo, done[f"q{part}"]), step)
+            results = attention(info, halo, pieces, group, first, heads)
             done[step] = results[members:]
             done[f"os{c}"] = results[:members]
             done[f"r0{c}"] = results[members]
@@ -283,12 +336,11 @@
                 run(f"{kind}{k}{step[-1]}")
         else:
             run(step)
-    attended, query_grad = unpack(
-        info, sum([done[f"o{c}"] for c in range(count)], []), CHUNKS, members, group, heads_dev
-    )
-    key_grad, value_grad = unpack(
-        info, sum([done[f"dx{c}"] for c in range(count)], []), CHUNKS, members, 1, heads_dev
-    )
+    returned = [heads for _, _, heads in CALLS]
+    o_all = sum([done[f"o{c}"] for c in range(len(CALLS))], [])
+    dkv_all = sum([done[f"dx{c}"] for c in range(len(CALLS))], [])
+    attended, query_grad = unpack(info, o_all, returned, members, group, heads_dev)
+    key_grad, value_grad = unpack(info, dkv_all, returned, members, 1, heads_dev)
     return attended, query_grad, key_grad, value_grad
 
 

time: 130 us -> 128 us (0.985)
  Pallas kernels: 28.2 us -> 24.1 us
  waiting for transfers between devices: 59.6 us -> 61.7 us
    pallas_call x2, Pallas kernels: 22.1 us -> 18 us  [attention(): pl.pallas_call(functools.partial(attention_kernel, members, planes - 1, g...]
    ppermute x24, waiting for transfers between devices: 20.9 us -> 22.9 us  [swap(): lax.ppermute(pieces[m], axes, pairs[m])]
  transfers between devices with their start and end apart: 32 -> 32, of which waited for: 13 -> 13; matrix products, arithmetic and copies ran while one was open for 1% -> 1% of each run, Pallas kernels for 20% -> 17%
where the time goes in v3:
time: 128 us; the launch traced here: 127 us
  waiting for transfers between devices  61.7 us (48%)
  starting transfers between devices  37.6 us (29%)
  Pallas kernels  24.1 us (19%)
  local copies, waits for them, and re-layouts  2.16 us (2%)
    ppermute x8, waiting for transfers between devices, hop(): return lax.ppermute(array, axes, pairs)  38.7 us
    ppermute x24, waiting for transfers between devices, swap(): lax.ppermute(pieces[m], axes, pairs[m])  22.9 us
    ppermute x8, starting transfers between devices, hop(): return lax.ppermute(array, axes, pairs)  20.8 us
    pallas_call x2, Pallas kernels, attention(): pl.pallas_call(functools.partial(attention_kernel, members, planes - 1, g...  18 us
    ppermute x24, starting transfers between devices, swap(): lax.ppermute(pieces[m], axes, pairs[m])  16.8 us
    pallas_call x2, Pallas kernels, unpack(): pl.pallas_call(functools.partial(unpack_kernel, chunks, members, group, h...  4.15 us
  transfers between devices with their start and end apart: 32, of which 13 were waited for; matrix products, arithmetic and copies ran while one was open for 1% of the time, Pallas kernels for 17%

profile of v3, /device:TPU:0, one launch (start us, length us, event | category | flops | bytes accessed | tf_op | source)
XLA Modules:
  0.0 127.3 jit_solution(17489691449825393481)
XLA Ops:
  4.2 2.6 %collective-permute-start.1 = (bf16[128,512]{1,0:T(8,128)(2,1)S(1)}, bf16[128,512]{1,0:T(8,128)(2,1)S(1)}, u32[]{:S(2)}, u32[]{:S(2)}) collective-permute-start(bf16[128,512]{1,0:T(8,128)(2,1)S(1)} %get-tuple-element.52), channel_id=1, source_target_pairs={{0,2},{1,3},{2,0},{3,1},{4,6},{5,7},{6,4},{7,5},{8,10},{9,11},{10,... | collective-permute-start | bytes 393224 | tf_op jit(solution)/shard_map/ppermute | solution.py:285
  6.8 4.3 %collective-permute-done.1 = bf16[128,512]{1,0:T(8,128)(2,1)S(1)} collective-permute-done((bf16[128,512]{1,0:T(8,128)(2,1)S(1)}, bf16[128,512]{1,0:T(8,128)(2,1)S(1)}, u32[]{:S(2)}, u32[]{:S(2)}) %collective-permute-start.1) | collective-permute-done | bytes 131104 | tf_op jit(solution)/shard_map/ppermute | solution.py:285
  11.1 2.3 %collective-permute-done.2 = bf16[128,512]{1,0:T(8,128)(2,1)S(1)} collective-permute-done((bf16[128,512]{1,0:T(8,128)(2,1)S(1)}, bf16[128,512]{1,0:T(8,128)(2,1)S(1)}, u32[]{:S(2)}, u32[]{:S(2)}) %collective-permute-start.2) | collective-permute-done | bytes 131104 | tf_op jit(solution)/shard_map/ppermute | solution.py:285
  13.4 3.7 %collective-permute-start.3 = (bf16[4,128,512]{2,1,0:T(8,128)(2,1)S(1)}, bf16[4,128,512]{2,1,0:T(8,128)(2,1)S(1)}, u32[]{:S(2)}, u32[]{:S(2)}) collective-permute-start(bf16[4,128,512]{2,1,0:T(8,128)(2,1)S(1)} %pad_maximum_fusion.refs_2_), channel_id=1, source_target_pairs={{0,4},{1,5},{2,6},{3,7},{4,8},{5,9},{6,10},{7,11},{8,12},{9,13},{1... | collective-permute-start | bytes 1572872 | tf_op jit(solution)/shard_map/ppermute | solution.py:289
  17.2 1.6 %collective-permute-start.12 = (bf16[128,512]{1,0:T(8,128)(2,1)S(1)}, bf16[128,512]{1,0:T(8,128)(2,1)S(1)}, u32[]{:S(2)}, u32[]{:S(2)}) collective-permute-start(bf16[128,512]{1,0:T(8,128)(2,1)S(1)} %get-tuple-element.69), channel_id=1, source_target_pairs={{0,2},{1,3},{2,0},{3,1},{4,6},{5,7},{6,4},{7,5},{8,10},{9,11},{10,... | collective-permute-start | bytes 393224 | tf_op jit(solution)/shard_map/ppermute | solution.py:285
  19.1 4.5 %collective-permute-done.12 = bf16[128,512]{1,0:T(8,128)(2,1)S(1)} collective-permute-done((bf16[128,512]{1,0:T(8,128)(2,1)S(1)}, bf16[128,512]{1,0:T(8,128)(2,1)S(1)}, u32[]{:S(2)}, u32[]{:S(2)}) %collective-permute-start.12) | collective-permute-done | bytes 131104 | tf_op jit(solution)/shard_map/ppermute | solution.py:285
  23.6 1.9 %collective-permute-done.13 = bf16[128,512]{1,0:T(8,128)(2,1)S(1)} collective-permute-done((bf16[128,512]{1,0:T(8,128)(2,1)S(1)}, bf16[128,512]{1,0:T(8,128)(2,1)S(1)}, u32[]{:S(2)}, u32[]{:S(2)}) %collective-permute-start.13) | collective-permute-done | bytes 131104 | tf_op jit(solution)/shard_map/ppermute | solution.py:285
  25.6 3.5 %collective-permute-start.14 = (bf16[4,128,512]{2,1,0:T(8,128)(2,1)S(1)}, bf16[4,128,512]{2,1,0:T(8,128)(2,1)S(1)}, u32[]{:S(2)}, u32[]{:S(2)}) collective-permute-start(bf16[4,128,512]{2,1,0:T(8,128)(2,1)S(1)} %pad_maximum_fusion.1.refs_2_), channel_id=1, source_target_pairs={{0,4},{1,5},{2,6},{3,7},{4,8},{5,9},{6,10},{7,11},{8,12},{9,13},{1... | collective-permute-start | bytes 1572872 | tf_op jit(solution)/shard_map/ppermute | solution.py:289
  29.1 4.1 %collective-permute-start.4 = (bf16[4,128,512]{2,1,0:T(8,128)(2,1)S(1)}, bf16[4,128,512]{2,1,0:T(8,128)(2,1)S(1)}, u32[]{:S(2)}, u32[]{:S(2)}) collective-permute-start(bf16[4,128,512]{2,1,0:T(8,128)(2,1)S(1)} %collective-permute-done.3.refs_1_), channel_id=1, source_target_pairs={{0,4},{1,5},{2,6},{3,7},{4,8},{5,9},{6,10},{7,11},{8,12},{9,13},{1... | collective-permute-start | bytes 1572872 | tf_op jit(solution)/shard_map/ppermute | solution.py:289
  34.4 1.6 %collective-permute-start.6 = (bf16[128,1024]{1,0:T(8,128)(2,1)S(1)}, bf16[128,1024]{1,0:T(8,128)(2,1)S(1)}, u32[]{:S(2)}, u32[]{:S(2)}) collective-permute-start(bf16[128,1024]{1,0:T(8,128)(2,1)S(1)} %get-tuple-element.57), channel_id=1, source_target_pairs={{0,2},{1,3},{2,0},{3,1},{4,6},{5,7},{6,4},{7,5},{8,10},{9,11},{10,... | collective-permute-start | bytes 786440 | tf_op jit(solution)/shard_map/ppermute | solution.py:285
  36.2 5.0 %collective-permute-done.14.refs_1_ = bf16[4,128,512]{2,1,0:T(8,128)(2,1)S(1)} collective-permute-done((bf16[4,128,512]{2,1,0:T(8,128)(2,1)S(1)}, bf16[4,128,512]{2,1,0:T(8,128)(2,1)S(1)}, u32[]{:S(2)}, u32[]{:S(2)}) %collective-permute-start.14) | collective-permute-done | bytes 524320 | tf_op jit(solution)/shard_map/ppermute | solution.py:289
  41.2 4.4 %collective-permute-start.15 = (bf16[4,128,512]{2,1,0:T(8,128)(2,1)S(1)}, bf16[4,128,512]{2,1,0:T(8,128)(2,1)S(1)}, u32[]{:S(2)}, u32[]{:S(2)}) collective-permute-start(bf16[4,128,512]{2,1,0:T(8,128)(2,1)S(1)} %collective-permute-done.14.refs_1_), channel_id=1, source_target_pairs={{0,4},{1,5},{2,6},{3,7},{4,8},{5,9},{6,10},{7,11},{8,12},{9,13},{1... | collective-permute-start | bytes 1572872 | tf_op jit(solution)/shard_map/ppermute | solution.py:289
  45.7 2.6 %collective-permute-done.7.refs_6_ = bf16[128,1024]{1,0:T(8,128)(2,1)S(1)} collective-permute-done((bf16[128,1024]{1,0:T(8,128)(2,1)S(1)}, bf16[128,1024]{1,0:T(8,128)(2,1)S(1)}, u32[]{:S(2)}, u32[]{:S(2)}) %collective-permute-start.7) | collective-permute-done | bytes 262176 | tf_op jit(solution)/shard_map/ppermute | solution.py:285
  50.1 2.4 %collective-permute-done.4.refs_0_ = bf16[4,128,512]{2,1,0:T(8,128)(2,1)S(1)} collective-permute-done((bf16[4,128,512]{2,1,0:T(8,128)(2,1)S(1)}, bf16[4,128,512]{2,1,0:T(8,128)(2,1)S(1)}, u32[]{:S(2)}, u32[]{:S(2)}) %collective-permute-start.4) | collective-permute-done | bytes 524320 | tf_op jit(solution)/shard_map/ppermute | solution.py:289
  52.5 9.0 %attention.2 = (bf16[128,1024]{1,0:T(8,128)(2,1)S(1)}, bf16[128,1024]{1,0:T(8,128)(2,1)S(1)}, bf16[128,1024]{1,0:T(8,128)(2,1)S(1)}, bf16[128,1024]{1,0:T(8,128)...) custom-call(s32[2]{0:T(128)S(1)} %pad_add_fusion.info, ...), custom_call_target="tpu_custom_call" | custom-call | flops 3623878656 | bytes 5242880 | tf_op jit(solution)/shard_map/attention/pallas_call | solution.py:236
  62.9 1.6 %collective-permute-start.9 = (bf16[128,1024]{1,0:T(8,128)(2,1)S(1)}, bf16[128,1024]{1,0:T(8,128)(2,1)S(1)}, u32[]{:S(2)}, u32[]{:S(2)}) collective-permute-start(bf16[128,1024]{1,0:T(8,128)(2,1)S(1)} %get-tuple-element.61), channel_id=1, source_target_pairs={{0,2},{1,3},{2,0},{3,1},{4,6},{5,7},{6,4},{7,5},{8,10},{9,11},{10,... | collective-permute-start | bytes 786440 | tf_op jit(solution)/shard_map/ppermute | solution.py:285
  64.8 9.0 %attention.3 = (bf16[128,1024]{1,0:T(8,128)(2,1)S(1)}, bf16[128,1024]{1,0:T(8,128)(2,1)S(1)}, bf16[128,1024]{1,0:T(8,128)(2,1)S(1)}, bf16[128,1024]{1,0:T(8,128)...) custom-call(s32[2]{0:T(128)S(1)} %pad_add_fusion.info, ...), custom_call_target="tpu_custom_call" | custom-call | flops 3623878656 | bytes 5242880 | tf_op jit(solution)/shard_map/attention/pallas_call | solution.py:236
  73.8 3.0 %collective-permute-done.10.refs_3_ = bf16[128,1024]{1,0:T(8,128)(2,1)S(1)} collective-permute-done((bf16[128,1024]{1,0:T(8,128)(2,1)S(1)}, bf16[128,1024]{1,0:T(8,128)(2,1)S(1)}, u32[]{:S(2)}, u32[]{:S(2)}) %collective-permute-start.10) | collective-permute-done | bytes 262176 | tf_op jit(solution)/shard_map/ppermute | solution.py:285
  81.6 12.8 %collective-permute-done.27 = bf16[4,128,512]{2,1,0:T(8,128)(2,1)S(1)} collective-permute-done((bf16[4,128,512]{2,1,0:T(8,128)(2,1)S(1)}, bf16[4,128,512]{2,1,0:T(8,128)(2,1)S(1)}, u32[]{:S(2)}, u32[]{:S(2)}) %collective-permute-start.27) | collective-permute-done | bytes 524320 | tf_op jit(solution)/shard_map/ppermute | solution.py:289
  95.9 9.8 %collective-permute-done.23 = bf16[4,128,512]{2,1,0:T(8,128)(2,1)S(1)} collective-permute-done((bf16[4,128,512]{2,1,0:T(8,128)(2,1)S(1)}, bf16[4,128,512]{2,1,0:T(8,128)(2,1)S(1)}, u32[]{:S(2)}, u32[]{:S(2)}) %collective-permute-start.23) | collective-permute-done | bytes 524320 | tf_op jit(solution)/shard_map/ppermute | solution.py:289
  107.8 8.8 %collective-permute-done.28 = bf16[4,128,512]{2,1,0:T(8,128)(2,1)S(1)} collective-permute-done((bf16[4,128,512]{2,1,0:T(8,128)(2,1)S(1)}, bf16[4,128,512]{2,1,0:T(8,128)(2,1)S(1)}, u32[]{:S(2)}, u32[]{:S(2)}) %collective-permute-start.28) | collective-permute-done | bytes 524320 | tf_op jit(solution)/shard_map/ppermute | solution.py:289
  118.7 2.4 %unpack.2 = (bf16[128,4096]{1,0:T(8,128)(2,1)}, bf16[128,4096]{1,0:T(8,128)(2,1)}) custom-call(s32[2]{0:T(128)S(1)} %pad_add_fusion.info, bf16[128,1024]{1,0:T(8,128)(2,1)S(1)} %get-tuple-element.59.refs_0_, bf16[128,1024]{1,0:T(8,128)(2,1)S(1)} %collective-permute-done.8.refs_1_, bf16[128,1024]{1,0:T(8,128)(2,1)S(1)} %collective-permute-done.9.refs_2_, ...), custom_call_target="tpu_custom_call" | custom-call | tf_op jit(solution)/shard_map/unpack/pallas_call | solution.py:99
  122.6 2.9 %collective-permute-done.30.refs_6_ = bf16[128,512]{1,0:T(8,128)(2,1)S(1)} collective-permute-done((bf16[128,512]{1,0:T(8,128)(2,1)S(1)}, bf16[128,512]{1,0:T(8,128)(2,1)S(1)}, u32[]{:S(2)}, u32[]{:S(2)}) %collective-permute-start.30) | collective-permute-done | bytes 131104 | tf_op jit(solution)/shard_map/ppermute | solution.py:285
  125.5 1.8 %unpack.3 = (bf16[128,2048]{1,0:T(8,128)(2,1)}, bf16[128,2048]{1,0:T(8,128)(2,1)}) custom-call(s32[2]{0:T(128)S(1)} %pad_add_fusion.info, bf16[128,512]{1,0:T(8,128)(2,1)S(1)} %get-tuple-element.103.refs_0_, bf16[128,512]{1,0:T(8,128)(2,1)S(1)} %collective-permute-done.24.refs_1_, bf16[128,512]{1,0:T(8,128)(2,1)S(1)} %collective-permute-done.25.refs_2_, ...), custom_call_target="tpu_custom_call" | custom-call | tf_op jit(solution)/shard_map/unpack/pallas_call | solution.py:99
  (63 shorter events, 21.2 us)
Async XLA Ops:
  13.4 15.6 %collective-permute-start.3 = (bf16[4,128,512]{2,1,0:T(8,128)(2,1)S(1)}, bf16[4,128,512]{2,1,0:T(8,128)(2,1)S(1)}, u32[]{:S(2)}, u32[]{:S(2)}) collective-permute-start(bf16[4,128,512]{2,1,0:T(8,128)(2,1)S(1)} %pad_maximum_fusion.refs_2_), channel_id=1, source_target_pairs={{0,4},{1,5},{2,6},{3,7},{4,8},{5,9},{6,10},{7,11},{8,12},{9,13},{1... | collective-permute-start | bytes 1572872 | tf_op jit(solution)/shard_map/ppermute | solution.py:289
  25.6 15.7 %collective-permute-start.14 = (bf16[4,128,512]{2,1,0:T(8,128)(2,1)S(1)}, bf16[4,128,512]{2,1,0:T(8,128)(2,1)S(1)}, u32[]{:S(2)}, u32[]{:S(2)}) collective-permute-start(bf16[4,128,512]{2,1,0:T(8,128)(2,1)S(1)} %pad_maximum_fusion.1.refs_2_), channel_id=1, source_target_pairs={{0,4},{1,5},{2,6},{3,7},{4,8},{5,9},{6,10},{7,11},{8,12},{9,13},{1... | collective-permute-start | bytes 1572872 | tf_op jit(solution)/shard_map/ppermute | solution.py:289
  29.1 23.4 %collective-permute-start.4 = (bf16[4,128,512]{2,1,0:T(8,128)(2,1)S(1)}, bf16[4,128,512]{2,1,0:T(8,128)(2,1)S(1)}, u32[]{:S(2)}, u32[]{:S(2)}) collective-permute-start(bf16[4,128,512]{2,1,0:T(8,128)(2,1)S(1)} %collective-permute-done.3.refs_1_), channel_id=1, source_target_pairs={{0,4},{1,5},{2,6},{3,7},{4,8},{5,9},{6,10},{7,11},{8,12},{9,13},{1... | collective-permute-start | bytes 1572872 | tf_op jit(solution)/shard_map/ppermute | solution.py:289
  34.3 11.4 %collective-permute-start.5 = (bf16[128,1024]{1,0:T(8,128)(2,1)S(1)}, bf16[128,1024]{1,0:T(8,128)(2,1)S(1)}, u32[]{:S(2)}, u32[]{:S(2)}) collective-permute-start(bf16[128,1024]{1,0:T(8,128)(2,1)S(1)} %get-tuple-element.56), channel_id=1, source_target_pairs={{0,1},{1,0},{2,3},{3,2},{4,5},{5,4},{6,7},{7,6},{8,9},{9,8},{10,11... | collective-permute-start | bytes 786440 | tf_op jit(solution)/shard_map/ppermute | solution.py:285
  34.4 11.3 %collective-permute-start.6 = (bf16[128,1024]{1,0:T(8,128)(2,1)S(1)}, bf16[128,1024]{1,0:T(8,128)(2,1)S(1)}, u32[]{:S(2)}, u32[]{:S(2)}) collective-permute-start(bf16[128,1024]{1,0:T(8,128)(2,1)S(1)} %get-tuple-element.57), channel_id=1, source_target_pairs={{0,2},{1,3},{2,0},{3,1},{4,6},{5,7},{6,4},{7,5},{8,10},{9,11},{10,... | collective-permute-start | bytes 786440 | tf_op jit(solution)/shard_map/ppermute | solution.py:285
  35.9 12.3 %collective-permute-start.7 = (bf16[128,1024]{1,0:T(8,128)(2,1)S(1)}, bf16[128,1024]{1,0:T(8,128)(2,1)S(1)}, u32[]{:S(2)}, u32[]{:S(2)}) collective-permute-start(bf16[128,1024]{1,0:T(8,128)(2,1)S(1)} %get-tuple-element.58), channel_id=1, source_target_pairs={{0,3},{1,2},{2,1},{3,0},{4,7},{5,6},{6,5},{7,4},{8,11},{9,10},{10,... | collective-permute-start | bytes 786440 | tf_op jit(solution)/shard_map/ppermute | solution.py:285
  41.2 23.5 %collective-permute-start.15 = (bf16[4,128,512]{2,1,0:T(8,128)(2,1)S(1)}, bf16[4,128,512]{2,1,0:T(8,128)(2,1)S(1)}, u32[]{:S(2)}, u32[]{:S(2)}) collective-permute-start(bf16[4,128,512]{2,1,0:T(8,128)(2,1)S(1)} %collective-permute-done.14.refs_1_), channel_id=1, source_target_pairs={{0,4},{1,5},{2,6},{3,7},{4,8},{5,9},{6,10},{7,11},{8,12},{9,13},{1... | collective-permute-start | bytes 1572872 | tf_op jit(solution)/shard_map/ppermute | solution.py:289
  48.3 14.5 %collective-permute-start.16 = (bf16[128,1024]{1,0:T(8,128)(2,1)S(1)}, bf16[128,1024]{1,0:T(8,128)(2,1)S(1)}, u32[]{:S(2)}, u32[]{:S(2)}) collective-permute-start(bf16[128,1024]{1,0:T(8,128)(2,1)S(1)} %get-tuple-element.76), channel_id=1, source_target_pairs={{0,1},{1,0},{2,3},{3,2},{4,5},{5,4},{6,7},{7,6},{8,9},{9,8},{10,11... | collective-permute-start | bytes 786440 | tf_op jit(solution)/shard_map/ppermute | solution.py:285
  48.5 14.3 %collective-permute-start.17 = (bf16[128,1024]{1,0:T(8,128)(2,1)S(1)}, bf16[128,1024]{1,0:T(8,128)(2,1)S(1)}, u32[]{:S(2)}, u32[]{:S(2)}) collective-permute-start(bf16[128,1024]{1,0:T(8,128)(2,1)S(1)} %get-tuple-element.77), channel_id=1, source_target_pairs={{0,2},{1,3},{2,0},{3,1},{4,6},{5,7},{6,4},{7,5},{8,10},{9,11},{10,... | collective-permute-start | bytes 786440 | tf_op jit(solution)/shard_map/ppermute | solution.py:285
  50.0 14.4 %collective-permute-start.18 = (bf16[128,1024]{1,0:T(8,128)(2,1)S(1)}, bf16[128,1024]{1,0:T(8,128)(2,1)S(1)}, u32[]{:S(2)}, u32[]{:S(2)}) collective-permute-start(bf16[128,1024]{1,0:T(8,128)(2,1)S(1)} %get-tuple-element.78), channel_id=1, source_target_pairs={{0,3},{1,2},{2,1},{3,0},{4,7},{5,6},{6,5},{7,4},{8,11},{9,10},{10,... | collective-permute-start | bytes 786440 | tf_op jit(solution)/shard_map/ppermute | solution.py:285
  61.5 16.6 %collective-permute-start.22 = (bf16[4,128,512]{2,1,0:T(8,128)(2,1)S(1)}, bf16[4,128,512]{2,1,0:T(8,128)(2,1)S(1)}, u32[]{:S(2)}, u32[]{:S(2)}) collective-permute-start(bf16[4,128,512]{2,1,0:T(8,128)(2,1)S(1)} %get-tuple-element.85), channel_id=1, source_target_pairs={{4,0},{5,1},{6,2},{7,3},{8,4},{9,5},{10,6},{11,7},{12,8},{13,9},{1... | collective-permute-start | bytes 1572872 | tf_op jit(solution)/shard_map/ppermute | solution.py:289
  62.8 11.0 %collective-permute-start.8 = (bf16[128,1024]{1,0:T(8,128)(2,1)S(1)}, bf16[128,1024]{1,0:T(8,128)(2,1)S(1)}, u32[]{:S(2)}, u32[]{:S(2)}) collective-permute-start(bf16[128,1024]{1,0:T(8,128)(2,1)S(1)} %get-tuple-element.60), channel_id=1, source_target_pairs={{0,1},{1,0},{2,3},{3,2},{4,5},{5,4},{6,7},{7,6},{8,9},{9,8},{10,11... | collective-permute-start | bytes 786440 | tf_op jit(solution)/shard_map/ppermute | solution.py:285
  62.9 10.9 %collective-permute-start.9 = (bf16[128,1024]{1,0:T(8,128)(2,1)S(1)}, bf16[128,1024]{1,0:T(8,128)(2,1)S(1)}, u32[]{:S(2)}, u32[]{:S(2)}) collective-permute-start(bf16[128,1024]{1,0:T(8,128)(2,1)S(1)} %get-tuple-element.61), channel_id=1, source_target_pairs={{0,2},{1,3},{2,0},{3,1},{4,6},{5,7},{6,4},{7,5},{8,10},{9,11},{10,... | collective-permute-start | bytes 786440 | tf_op jit(solution)/shard_map/ppermute | solution.py:285
  64.5 12.3 %collective-permute-start.10 = (bf16[128,1024]{1,0:T(8,128)(2,1)S(1)}, bf16[128,1024]{1,0:T(8,128)(2,1)S(1)}, u32[]{:S(2)}, u32[]{:S(2)}) collective-permute-start(bf16[128,1024]{1,0:T(8,128)(2,1)S(1)} %get-tuple-element.62), channel_id=1, source_target_pairs={{0,3},{1,2},{2,1},{3,0},{4,7},{5,6},{6,5},{7,4},{8,11},{9,10},{10,... | collective-permute-start | bytes 786440 | tf_op jit(solution)/shard_map/ppermute | solution.py:285
  76.8 17.7 %collective-permute-start.27 = (bf16[4,128,512]{2,1,0:T(8,128)(2,1)S(1)}, bf16[4,128,512]{2,1,0:T(8,128)(2,1)S(1)}, u32[]{:S(2)}, u32[]{:S(2)}) collective-permute-start(bf16[4,128,512]{2,1,0:T(8,128)(2,1)S(1)} %get-tuple-element.89), channel_id=1, source_target_pairs={{4,0},{5,1},{6,2},{7,3},{8,4},{9,5},{10,6},{11,7},{12,8},{13,9},{1... | collective-permute-start | bytes 1572872 | tf_op jit(solution)/shard_map/ppermute | solution.py:289
  78.2 27.5 %collective-permute-start.23 = (bf16[4,128,512]{2,1,0:T(8,128)(2,1)S(1)}, bf16[4,128,512]{2,1,0:T(8,128)(2,1)S(1)}, u32[]{:S(2)}, u32[]{:S(2)}) collective-permute-start(bf16[4,128,512]{2,1,0:T(8,128)(2,1)S(1)} %add_convert_fusion.3), channel_id=1, source_target_pairs={{4,0},{5,1},{6,2},{7,3},{8,4},{9,5},{10,6},{11,7},{12,8},{13,9},{1... | collective-permute-start | bytes 1572872 | tf_op jit(solution)/shard_map/ppermute | solution.py:289
  79.5 15.1 %collective-permute-start.19 = (bf16[128,1024]{1,0:T(8,128)(2,1)S(1)}, bf16[128,1024]{1,0:T(8,128)(2,1)S(1)}, u32[]{:S(2)}, u32[]{:S(2)}) collective-permute-start(bf16[128,1024]{1,0:T(8,128)(2,1)S(1)} %get-tuple-element.80), channel_id=1, source_target_pairs={{0,1},{1,0},{2,3},{3,2},{4,5},{5,4},{6,7},{7,6},{8,9},{9,8},{10,11... | collective-permute-start | bytes 786440 | tf_op jit(solution)/shard_map/ppermute | solution.py:285
  80.2 14.5 %collective-permute-start.20 = (bf16[128,1024]{1,0:T(8,128)(2,1)S(1)}, bf16[128,1024]{1,0:T(8,128)(2,1)S(1)}, u32[]{:S(2)}, u32[]{:S(2)}) collective-permute-start(bf16[128,1024]{1,0:T(8,128)(2,1)S(1)} %get-tuple-element.81), channel_id=1, source_target_pairs={{0,2},{1,3},{2,0},{3,1},{4,6},{5,7},{6,4},{7,5},{8,10},{9,11},{10,... | collective-permute-start | bytes 786440 | tf_op jit(solution)/shard_map/ppermute | solution.py:285
  81.6 13.0 %collective-permute-start.21 = (bf16[128,1024]{1,0:T(8,128)(2,1)S(1)}, bf16[128,1024]{1,0:T(8,128)(2,1)S(1)}, u32[]{:S(2)}, u32[]{:S(2)}) collective-permute-start(bf16[128,1024]{1,0:T(8,128)(2,1)S(1)} %get-tuple-element.82), channel_id=1, source_target_pairs={{0,3},{1,2},{2,1},{3,0},{4,7},{5,6},{6,5},{7,4},{8,11},{9,10},{10,... | collective-permute-start | bytes 786440 | tf_op jit(solution)/shard_map/ppermute | solution.py:285
  94.6 22.0 %collective-permute-start.28 = (bf16[4,128,512]{2,1,0:T(8,128)(2,1)S(1)}, bf16[4,128,512]{2,1,0:T(8,128)(2,1)S(1)}, u32[]{:S(2)}, u32[]{:S(2)}) collective-permute-start(bf16[4,128,512]{2,1,0:T(8,128)(2,1)S(1)} %add_convert_fusion.1), channel_id=1, source_target_pairs={{4,0},{5,1},{6,2},{7,3},{8,4},{9,5},{10,6},{11,7},{12,8},{13,9},{1... | collective-permute-start | bytes 1572872 | tf_op jit(solution)/shard_map/ppermute | solution.py:289
  105.9 12.6 %collective-permute-start.26 = (bf16[128,512]{1,0:T(8,128)(2,1)S(1)}, bf16[128,512]{1,0:T(8,128)(2,1)S(1)}, u32[]{:S(2)}, u32[]{:S(2)}) collective-permute-start(bf16[128,512]{1,0:T(8,128)(2,1)S(1)} %get-tuple-element.100), channel_id=1, source_target_pairs={{0,3},{1,2},{2,1},{3,0},{4,7},{5,6},{6,5},{7,4},{8,11},{9,10},{10,... | collective-permute-start | bytes 393224 | tf_op jit(solution)/shard_map/ppermute | solution.py:285
  106.5 14.6 %collective-permute-start.25 = (bf16[128,512]{1,0:T(8,128)(2,1)S(1)}, bf16[128,512]{1,0:T(8,128)(2,1)S(1)}, u32[]{:S(2)}, u32[]{:S(2)}) collective-permute-start(bf16[128,512]{1,0:T(8,128)(2,1)S(1)} %get-tuple-element.101), channel_id=1, source_target_pairs={{0,2},{1,3},{2,0},{3,1},{4,6},{5,7},{6,4},{7,5},{8,10},{9,11},{10,... | collective-permute-start | bytes 393224 | tf_op jit(solution)/shard_map/ppermute | solution.py:285
  107.5 13.6 %collective-permute-start.24 = (bf16[128,512]{1,0:T(8,128)(2,1)S(1)}, bf16[128,512]{1,0:T(8,128)(2,1)S(1)}, u32[]{:S(2)}, u32[]{:S(2)}) collective-permute-start(bf16[128,512]{1,0:T(8,128)(2,1)S(1)} %get-tuple-element.102), channel_id=1, source_target_pairs={{0,1},{1,0},{2,3},{3,2},{4,5},{5,4},{6,7},{7,6},{8,9},{9,8},{10,11... | collective-permute-start | bytes 393224 | tf_op jit(solution)/shard_map/ppermute | solution.py:285
  117.8 7.7 %collective-permute-start.30 = (bf16[128,512]{1,0:T(8,128)(2,1)S(1)}, bf16[128,512]{1,0:T(8,128)(2,1)S(1)}, u32[]{:S(2)}, u32[]{:S(2)}) collective-permute-start(bf16[128,512]{1,0:T(8,128)(2,1)S(1)} %get-tuple-element.97), channel_id=1, source_target_pairs={{0,2},{1,3},{2,0},{3,1},{4,6},{5,7},{6,4},{7,5},{8,10},{9,11},{10,... | collective-permute-start | bytes 393224 | tf_op jit(solution)/shard_map/ppermute | solution.py:285
  (12 other events, 86.2 us)

commit v4 on v3

--- a/solution.py
+++ b/solution.py
@@ -13,14 +13,15 @@
 INNER = 2
 CHUNKS = (2, 2)
 CALLS = ((0, 0, 2), (1, 0, 2))
-STEPS = ("kv0", "kv1", "z0", "q0", "q1", "z1", "att0", "o0", "r0", "dx0", "att1", "o1", "r1", "dx1")
+DIRECT_IN = ()
+DIRECT_OUT = (1,)
+STEPS = ("kv0", "kv1", "z0", "q0", "q1", "z1", "att0", "o0", "r0", "dx0", "att1", "o1", "dx1", "r1")
 GATES = {
     "kv1": ("kv0",),
     "pack": ("kv0",),
     "q1": ("q0",),
     "r11": ("o0",),
-    "r21": ("o1",),
-    "dx1": ("o1",),
+    "r21": ("o1", "dx1"),
 }
 SOFTCAP = 50.0
 TANH_SCALE = 1.0 / (12.0 * SOFTCAP)
@@ -77,33 +78,43 @@
     )(info, a, b)
 
 
-def unpack_kernel(chunks, members, group, heads_dev, info, *refs):
+def unpack_kernel(chunks, members, group, heads_dev, later, info, *refs):
     me = info[0]
-    ins, (a_ref, b_ref) = refs[:-2], refs[-2:]
+    count = len(chunks) * members
+    ins, more, (a_ref, b_ref) = refs[:count], dict(zip(later, refs[count:-2])), refs[-2:]
     first = 0
     for c, heads in enumerate(chunks):
         for m in range(members):
-            src = ins[c * members + m]
+            at = c * members + m
             base = (me ^ m) * heads_dev + first
+
+            def block(column):
+                part = slice(column * HEAD, (column + 1) * HEAD)
+                if at not in more:
+                    return ins[at][:, part]
+                return (ins[at][:, part].astype(F32) + more[at][:, part].astype(F32)).astype(BF16)
+
             for h in range(heads):
                 for g in range(group):
                     target = head_cols((base + h) * group + g)
-                    a_ref[:, target] = src[:, (2 * h * group + g) * HEAD : (2 * h * group + g + 1) * HEAD]
-                    b_ref[:, target] = src[:, ((2 * h + 1) * group + g) * HEAD : ((2 * h + 1) * group + g + 1) * HEAD]
+                    a_ref[:, target] = block(2 * h * group + g)
+                    b_ref[:, target] = block((2 * h + 1) * group + g)
         first += heads
 
 
-def unpack(info, pieces, chunks, members, group, heads_dev):
+def unpack(info, pieces, later, chunks, members, group, heads_dev):
     rows = pieces[0].shape[0]
     width = members * heads_dev * group * HEAD
+    where = tuple(later)
+    more = [later[at] for at in where]
     return pl.pallas_call(
-        functools.partial(unpack_kernel, chunks, members, group, heads_dev),
+        functools.partial(unpack_kernel, chunks, members, group, heads_dev, where),
         out_shape=[jax.ShapeDtypeStruct((rows, width), BF16)] * 2,
-        in_specs=[smem()] + [vmem()] * len(pieces),
+        in_specs=[smem()] + [vmem()] * (len(pieces) + len(more)),
         out_specs=[vmem()] * 2,
         compiler_params=pltpu.CompilerParams(vmem_limit_bytes=40 * 2**20),
         name="unpack",
-    )(info, *pieces)
+    )(info, *pieces, *more)
 
 
 def attention_kernel(members, hops, group, rows, info, *refs):
@@ -288,6 +299,14 @@
         pairs = [(i, i + by * members) for i in range(ctx * tp) if 0 <= i + by * members < ctx * tp]
         return lax.ppermute(array, axes, pairs)
 
+    def hop_across(pieces, by):
+        count = ctx * tp
+        pairs = [
+            [(i, (i ^ m) + by * members) for i in range(count) if 0 <= (i ^ m) + by * members < count]
+            for m in range(members)
+        ]
+        return [lax.ppermute(pieces[m], axes, pairs[m]) for m in range(members)]
+
     kv_packed = pack(info, keys, values, CHUNKS, members, 1, heads_dev)
     done = {}
     q_packed = []
@@ -308,11 +327,18 @@
             done[step] = swap(gated(q_packed[c * members : (c + 1) * members], step))
         elif kind.startswith("z"):
             k = int(kind[1:])
-            if k == 1:
-                done[f"z0{c}"] = jnp.stack(done[f"kv{c}"])
-            done[step] = hop(gated(done[f"z{k - 1}{c}"], step), 1)
+            if k == 1 and c in DIRECT_IN:
+                pieces = hop_across(gated(kv_packed[c * members : (c + 1) * members], step), 1)
+                done[f"first{c}"] = pieces[0]
+                done[step] = jnp.stack(pieces)
+            else:
+                if k == 1:
+                    done[f"z0{c}"] = jnp.stack(done[f"kv{c}"])
+                done[step] = hop(gated(done[f"z{k - 1}{c}"], step), 1)
         elif kind == "att":
             part, first, heads = CALLS[c]
+            if f"z0{part}" not in done:
+                done[f"z0{part}"] = jnp.stack(done[f"kv{part}"])
             halo = [done[f"z{k}{part}"] for k in range(hops, -1, -1)]
             halo, pieces = gated((halo, done[f"q{part}"]), step)
             results = attention(info, halo, pieces, group, first, heads)
@@ -323,10 +349,14 @@
             done[step] = swap(gated(done[f"os{c}"], step))
         elif kind.startswith("r"):
             k = int(kind[1:])
-            arrived = hop(gated(done[f"r{k - 1}{c}"], step), -1)
+            carried = gated(done[f"r{k - 1}{c}"], step)
+            if k == hops and c in DIRECT_OUT:
+                done[step] = hop_across([carried[m] for m in range(members)], -1)
+                return
+            arrived = hop(carried, -1)
             done[step] = (arrived.astype(F32) + done[f"att{c}"][k].astype(F32)).astype(BF16)
         else:
-            carried = gated(done[f"r{hops}{c}"], step)
+            carried = gated(done[f"att{c}"][hops] if c in DIRECT_OUT else done[f"r{hops}{c}"], step)
             done[step] = swap([carried[m] for m in range(members)])
 
     for step in STEPS:
@@ -339,8 +369,9 @@
     returned = [heads for _, _, heads in CALLS]
     o_all = sum([done[f"o{c}"] for c in range(len(CALLS))], [])
     dkv_all = sum([done[f"dx{c}"] for c in range(len(CALLS))], [])
-    attended, query_grad = unpack(info, o_all, returned, members, group, heads_dev)
-    key_grad, value_grad = unpack(info, dkv_all, returned, members, 1, heads_dev)
+    attended, query_grad = unpack(info, o_all, {}, returned, members, group, heads_dev)
+    later = {c * members + m: done[f"r{hops}{c}"][m] for c in DIRECT_OUT for m in range(members)}
+    key_grad, value_grad = unpack(info, dkv_all, later, returned, members, 1, heads_dev)
     return attended, query_grad, key_grad, value_grad
 
 

time: 128 us -> 118 us (0.922)
  waiting for transfers between devices: 61.7 us -> 48.8 us
  starting transfers between devices: 37.6 us -> 40.9 us
    ppermute x8 -> x7, waiting for transfers between devices: 38.7 us -> 16.6 us  [hop(): return lax.ppermute(array, axes, pairs)]
    ppermute x0 -> x4, waiting for transfers between devices: none -> 7.05 us  [hop_across(): return [lax.ppermute(pieces[m], axes, pairs[m]) for m in range(members)]]
    ppermute x0 -> x4, starting transfers between devices: none -> 5.17 us  [hop_across(): return [lax.ppermute(pieces[m], axes, pairs[m]) for m in range(members)]]
    ppermute x24, waiting for transfers between devices: 22.9 us -> 25.2 us  [swap(): lax.ppermute(pieces[m], axes, pairs[m])]
    ppermute x8 -> x7, starting transfers between devices: 20.8 us -> 19.5 us  [hop(): return lax.ppermute(array, axes, pairs)]
  transfers between devices with their start and end apart: 32 -> 35, of which waited for: 13 -> 19; matrix products, arithmetic and copies ran while one was open for 1% -> 1% of each run, Pallas kernels for 17% -> 18%
where the time goes in v4:
time: 118 us
  waiting for transfers between devices  48.8 us (41%)
  starting transfers between devices  40.9 us (35%)
  Pallas kernels  24.1 us (20%)
  local copies, waits for them, and re-layouts  2.2 us (2%)
    ppermute x24, waiting for transfers between devices, swap(): lax.ppermute(pieces[m], axes, pairs[m])  25.2 us
    ppermute x7, starting transfers between devices, hop(): return lax.ppermute(array, axes, pairs)  19.5 us
    pallas_call x2, Pallas kernels, attention(): pl.pallas_call(functools.partial(attention_kernel, members, planes - 1, g...  18 us
    ppermute x7, waiting for transfers between devices, hop(): return lax.ppermute(array, axes, pairs)  16.6 us
    ppermute x24, starting transfers between devices, swap(): lax.ppermute(pieces[m], axes, pairs[m])  16.3 us
    ppermute x4, waiting for transfers between devices, hop_across(): return [lax.ppermute(pieces[m], axes, pairs[m]) for m in range(members)]  7.05 us
    ppermute x4, starting transfers between devices, hop_across(): return [lax.ppermute(pieces[m], axes, pairs[m]) for m in range(members)]  5.17 us
    pallas_call x2, Pallas kernels, unpack(): pl.pallas_call(functools.partial(unpack_kernel, chunks, members, group, h...  4.14 us
  transfers between devices with their start and end apart: 35, of which 19 were waited for; matrix products, arithmetic and copies ran while one was open for 1% of the time, Pallas kernels for 18%

profile of v4, /device:TPU:0, one launch (start us, length us, event | category | flops | bytes accessed | tf_op | source)
XLA Modules:
  0.0 117.7 jit_solution(7743204617027829186)
XLA Ops:
  4.2 2.6 %collective-permute-start.1 = (bf16[128,512]{1,0:T(8,128)(2,1)S(1)}, bf16[128,512]{1,0:T(8,128)(2,1)S(1)}, u32[]{:S(2)}, u32[]{:S(2)}) collective-permute-start(bf16[128,512]{1,0:T(8,128)(2,1)S(1)} %get-tuple-element.51), channel_id=1, source_target_pairs={{0,2},{1,3},{2,0},{3,1},{4,6},{5,7},{6,4},{7,5},{8,10},{9,11},{10,... | collective-permute-start | bytes 393224 | tf_op jit(solution)/shard_map/ppermute | solution.py:296
  6.8 4.3 %collective-permute-done.1 = bf16[128,512]{1,0:T(8,128)(2,1)S(1)} collective-permute-done((bf16[128,512]{1,0:T(8,128)(2,1)S(1)}, bf16[128,512]{1,0:T(8,128)(2,1)S(1)}, u32[]{:S(2)}, u32[]{:S(2)}) %collective-permute-start.1) | collective-permute-done | bytes 131104 | tf_op jit(solution)/shard_map/ppermute | solution.py:296
  11.1 2.3 %collective-permute-done.2 = bf16[128,512]{1,0:T(8,128)(2,1)S(1)} collective-permute-done((bf16[128,512]{1,0:T(8,128)(2,1)S(1)}, bf16[128,512]{1,0:T(8,128)(2,1)S(1)}, u32[]{:S(2)}, u32[]{:S(2)}) %collective-permute-start.2) | collective-permute-done | bytes 131104 | tf_op jit(solution)/shard_map/ppermute | solution.py:296
  13.4 3.7 %collective-permute-start.3 = (bf16[4,128,512]{2,1,0:T(8,128)(2,1)S(1)}, bf16[4,128,512]{2,1,0:T(8,128)(2,1)S(1)}, u32[]{:S(2)}, u32[]{:S(2)}) collective-permute-start(bf16[4,128,512]{2,1,0:T(8,128)(2,1)S(1)} %pad_maximum_fusion.refs_2_), channel_id=1, source_target_pairs={{0,4},{1,5},{2,6},{3,7},{4,8},{5,9},{6,10},{7,11},{8,12},{9,13},{1... | collective-permute-start | bytes 1572872 | tf_op jit(solution)/shard_map/ppermute | solution.py:300
  19.1 4.5 %collective-permute-done.12 = bf16[128,512]{1,0:T(8,128)(2,1)S(1)} collective-permute-done((bf16[128,512]{1,0:T(8,128)(2,1)S(1)}, bf16[128,512]{1,0:T(8,128)(2,1)S(1)}, u32[]{:S(2)}, u32[]{:S(2)}) %collective-permute-start.12) | collective-permute-done | bytes 131104 | tf_op jit(solution)/shard_map/ppermute | solution.py:296
  23.6 1.9 %collective-permute-done.13 = bf16[128,512]{1,0:T(8,128)(2,1)S(1)} collective-permute-done((bf16[128,512]{1,0:T(8,128)(2,1)S(1)}, bf16[128,512]{1,0:T(8,128)(2,1)S(1)}, u32[]{:S(2)}, u32[]{:S(2)}) %collective-permute-start.13) | collective-permute-done | bytes 131104 | tf_op jit(solution)/shard_map/ppermute | solution.py:296
  25.6 3.5 %collective-permute-start.14 = (bf16[4,128,512]{2,1,0:T(8,128)(2,1)S(1)}, bf16[4,128,512]{2,1,0:T(8,128)(2,1)S(1)}, u32[]{:S(2)}, u32[]{:S(2)}) collective-permute-start(bf16[4,128,512]{2,1,0:T(8,128)(2,1)S(1)} %pad_maximum_fusion.1.refs_2_), channel_id=1, source_target_pairs={{0,4},{1,5},{2,6},{3,7},{4,8},{5,9},{6,10},{7,11},{8,12},{9,13},{1... | collective-permute-start | bytes 1572872 | tf_op jit(solution)/shard_map/ppermute | solution.py:300
  29.1 4.1 %collective-permute-start.4 = (bf16[4,128,512]{2,1,0:T(8,128)(2,1)S(1)}, bf16[4,128,512]{2,1,0:T(8,128)(2,1)S(1)}, u32[]{:S(2)}, u32[]{:S(2)}) collective-permute-start(bf16[4,128,512]{2,1,0:T(8,128)(2,1)S(1)} %collective-permute-done.3.refs_1_), channel_id=1, source_target_pairs={{0,4},{1,5},{2,6},{3,7},{4,8},{5,9},{6,10},{7,11},{8,12},{9,13},{1... | collective-permute-start | bytes 1572872 | tf_op jit(solution)/shard_map/ppermute | solution.py:300
  36.2 5.0 %collective-permute-done.14.refs_1_ = bf16[4,128,512]{2,1,0:T(8,128)(2,1)S(1)} collective-permute-done((bf16[4,128,512]{2,1,0:T(8,128)(2,1)S(1)}, bf16[4,128,512]{2,1,0:T(8,128)(2,1)S(1)}, u32[]{:S(2)}, u32[]{:S(2)}) %collective-permute-start.14) | collective-permute-done | bytes 524320 | tf_op jit(solution)/shard_map/ppermute | solution.py:300
  41.2 4.4 %collective-permute-start.15 = (bf16[4,128,512]{2,1,0:T(8,128)(2,1)S(1)}, bf16[4,128,512]{2,1,0:T(8,128)(2,1)S(1)}, u32[]{:S(2)}, u32[]{:S(2)}) collective-permute-start(bf16[4,128,512]{2,1,0:T(8,128)(2,1)S(1)} %collective-permute-done.14.refs_1_), channel_id=1, source_target_pairs={{0,4},{1,5},{2,6},{3,7},{4,8},{5,9},{6,10},{7,11},{8,12},{9,13},{1... | collective-permute-start | bytes 1572872 | tf_op jit(solution)/shard_map/ppermute | solution.py:300
  45.7 2.6 %collective-permute-done.7.refs_6_ = bf16[128,1024]{1,0:T(8,128)(2,1)S(1)} collective-permute-done((bf16[128,1024]{1,0:T(8,128)(2,1)S(1)}, bf16[128,1024]{1,0:T(8,128)(2,1)S(1)}, u32[]{:S(2)}, u32[]{:S(2)}) %collective-permute-start.7) | collective-permute-done | bytes 262176 | tf_op jit(solution)/shard_map/ppermute | solution.py:296
  50.1 2.4 %collective-permute-done.4.refs_0_ = bf16[4,128,512]{2,1,0:T(8,128)(2,1)S(1)} collective-permute-done((bf16[4,128,512]{2,1,0:T(8,128)(2,1)S(1)}, bf16[4,128,512]{2,1,0:T(8,128)(2,1)S(1)}, u32[]{:S(2)}, u32[]{:S(2)}) %collective-permute-start.4) | collective-permute-done | bytes 524320 | tf_op jit(solution)/shard_map/ppermute | solution.py:300
  52.5 9.0 %attention.2 = (bf16[128,1024]{1,0:T(8,128)(2,1)S(1)}, bf16[128,1024]{1,0:T(8,128)(2,1)S(1)}, bf16[128,1024]{1,0:T(8,128)(2,1)S(1)}, bf16[128,1024]{1,0:T(8,128)...) custom-call(s32[2]{0:T(128)S(1)} %pad_add_fusion.info, ...), custom_call_target="tpu_custom_call" | custom-call | flops 3623878656 | bytes 5242880 | tf_op jit(solution)/shard_map/attention/pallas_call | solution.py:247
  64.7 9.0 %attention.3 = (bf16[128,1024]{1,0:T(8,128)(2,1)S(1)}, bf16[128,1024]{1,0:T(8,128)(2,1)S(1)}, bf16[128,1024]{1,0:T(8,128)(2,1)S(1)}, bf16[128,1024]{1,0:T(8,128)...) custom-call(s32[2]{0:T(128)S(1)} %pad_add_fusion.info, ...), custom_call_target="tpu_custom_call" | custom-call | flops 3623878656 | bytes 5242880 | tf_op jit(solution)/shard_map/attention/pallas_call | solution.py:247
  73.8 1.6 %collective-permute-done.10.refs_3_ = bf16[128,1024]{1,0:T(8,128)(2,1)S(1)} collective-permute-done((bf16[128,1024]{1,0:T(8,128)(2,1)S(1)}, bf16[128,1024]{1,0:T(8,128)(2,1)S(1)}, u32[]{:S(2)}, u32[]{:S(2)}) %collective-permute-start.10) | collective-permute-done | bytes 262176 | tf_op jit(solution)/shard_map/ppermute | solution.py:296
  76.8 1.7 %collective-permute-start.29 = (bf16[128,512]{1,0:T(8,128)(2,1)S(1)}, bf16[128,512]{1,0:T(8,128)(2,1)S(1)}, u32[]{:S(2)}, u32[]{:S(2)}) collective-permute-start(bf16[128,512]{1,0:T(8,128)(2,1)S(1)} %get-tuple-element.98), channel_id=1, source_target_pairs={{0,3},{1,2},{2,1},{3,0},{4,7},{5,6},{6,5},{7,4},{8,11},{9,10},{10,... | collective-permute-start | bytes 393224 | tf_op jit(solution)/shard_map/ppermute | solution.py:296
  83.4 2.0 %collective-permute-done.28.refs_6_ = bf16[128,512]{1,0:T(8,128)(2,1)S(1)} collective-permute-done((bf16[128,512]{1,0:T(8,128)(2,1)S(1)}, bf16[128,512]{1,0:T(8,128)(2,1)S(1)}, u32[]{:S(2)}, u32[]{:S(2)}) %collective-permute-start.28) | collective-permute-done | bytes 131104 | tf_op jit(solution)/shard_map/ppermute | solution.py:296
  85.9 6.7 %collective-permute-done.30 = bf16[4,128,512]{2,1,0:T(8,128)(2,1)S(1)} collective-permute-done((bf16[4,128,512]{2,1,0:T(8,128)(2,1)S(1)}, bf16[4,128,512]{2,1,0:T(8,128)(2,1)S(1)}, u32[]{:S(2)}, u32[]{:S(2)}) %collective-permute-start.30) | collective-permute-done | bytes 524320 | tf_op jit(solution)/shard_map/ppermute | solution.py:300
  93.9 3.2 %collective-permute-done.21.refs_7_ = bf16[128,1024]{1,0:T(8,128)(2,1)S(1)} collective-permute-done((bf16[128,1024]{1,0:T(8,128)(2,1)S(1)}, bf16[128,1024]{1,0:T(8,128)(2,1)S(1)}, u32[]{:S(2)}, u32[]{:S(2)}) %collective-permute-start.21) | collective-permute-done | bytes 262176 | tf_op jit(solution)/shard_map/ppermute | solution.py:296
  105.1 2.3 %collective-permute-done.34.refs_11_ = bf16[128,512]{1,0:T(8,128)(2,1)S(1)} collective-permute-done((bf16[128,512]{1,0:T(8,128)(2,1)S(1)}, bf16[128,512]{1,0:T(8,128)(2,1)S(1)}, u32[]{:S(2)}, u32[]{:S(2)}) %collective-permute-start.34) | collective-permute-done | bytes 131104 | tf_op jit(solution)/shard_map/ppermute | solution.py:308
  107.9 2.5 %collective-permute-done.33.refs_10_ = bf16[128,512]{1,0:T(8,128)(2,1)S(1)} collective-permute-done((bf16[128,512]{1,0:T(8,128)(2,1)S(1)}, bf16[128,512]{1,0:T(8,128)(2,1)S(1)}, u32[]{:S(2)}, u32[]{:S(2)}) %collective-permute-start.33) | collective-permute-done | bytes 131104 | tf_op jit(solution)/shard_map/ppermute | solution.py:308
  110.4 2.4 %unpack.2 = (bf16[128,4096]{1,0:T(8,128)(2,1)}, bf16[128,4096]{1,0:T(8,128)(2,1)}) custom-call(s32[2]{0:T(128)S(1)} %pad_add_fusion.info, bf16[128,1024]{1,0:T(8,128)(2,1)S(1)} %get-tuple-element.58.refs_0_, bf16[128,1024]{1,0:T(8,128)(2,1)S(1)} %collective-permute-done.8.refs_1_, bf16[128,1024]{1,0:T(8,128)(2,1)S(1)} %collective-permute-done.9.refs_2_, ...), custom_call_target="tpu_custom_call" | custom-call | tf_op jit(solution)/shard_map/unpack/pallas_call | solution.py:110
  112.8 2.2 %collective-permute-done.31.refs_8_ = bf16[128,512]{1,0:T(8,128)(2,1)S(1)} collective-permute-done((bf16[128,512]{1,0:T(8,128)(2,1)S(1)}, bf16[128,512]{1,0:T(8,128)(2,1)S(1)}, u32[]{:S(2)}, u32[]{:S(2)}) %collective-permute-start.31) | collective-permute-done | bytes 131104 | tf_op jit(solution)/shard_map/ppermute | solution.py:308
  115.9 1.8 %unpack.3 = (bf16[128,2048]{1,0:T(8,128)(2,1)}, bf16[128,2048]{1,0:T(8,128)(2,1)}) custom-call(s32[2]{0:T(128)S(1)} %pad_add_fusion.info, bf16[128,512]{1,0:T(8,128)(2,1)S(1)} %get-tuple-element.105.refs_0_, bf16[128,512]{1,0:T(8,128)(2,1)S(1)} %collective-permute-done.24.refs_1_, bf16[128,512]{1,0:T(8,128)(2,1)S(1)} %collective-permute-done.25.refs_2_, ...), custom_call_target="tpu_custom_call" | custom-call | tf_op jit(solution)/shard_map/unpack/pallas_call | solution.py:110
  (69 shorter events, 31.1 us)
Async XLA Ops:
  13.4 15.6 %collective-permute-start.3 = (bf16[4,128,512]{2,1,0:T(8,128)(2,1)S(1)}, bf16[4,128,512]{2,1,0:T(8,128)(2,1)S(1)}, u32[]{:S(2)}, u32[]{:S(2)}) collective-permute-start(bf16[4,128,512]{2,1,0:T(8,128)(2,1)S(1)} %pad_maximum_fusion.refs_2_), channel_id=1, source_target_pairs={{0,4},{1,5},{2,6},{3,7},{4,8},{5,9},{6,10},{7,11},{8,12},{9,13},{1... | collective-permute-start | bytes 1572872 | tf_op jit(solution)/shard_map/ppermute | solution.py:300
  25.6 15.7 %collective-permute-start.14 = (bf16[4,128,512]{2,1,0:T(8,128)(2,1)S(1)}, bf16[4,128,512]{2,1,0:T(8,128)(2,1)S(1)}, u32[]{:S(2)}, u32[]{:S(2)}) collective-permute-start(bf16[4,128,512]{2,1,0:T(8,128)(2,1)S(1)} %pad_maximum_fusion.1.refs_2_), channel_id=1, source_target_pairs={{0,4},{1,5},{2,6},{3,7},{4,8},{5,9},{6,10},{7,11},{8,12},{9,13},{1... | collective-permute-start | bytes 1572872 | tf_op jit(solution)/shard_map/ppermute | solution.py:300
  29.1 23.4 %collective-permute-start.4 = (bf16[4,128,512]{2,1,0:T(8,128)(2,1)S(1)}, bf16[4,128,512]{2,1,0:T(8,128)(2,1)S(1)}, u32[]{:S(2)}, u32[]{:S(2)}) collective-permute-start(bf16[4,128,512]{2,1,0:T(8,128)(2,1)S(1)} %collective-permute-done.3.refs_1_), channel_id=1, source_target_pairs={{0,4},{1,5},{2,6},{3,7},{4,8},{5,9},{6,10},{7,11},{8,12},{9,13},{1... | collective-permute-start | bytes 1572872 | tf_op jit(solution)/shard_map/ppermute | solution.py:300
  34.3 11.4 %collective-permute-start.5 = (bf16[128,1024]{1,0:T(8,128)(2,1)S(1)}, bf16[128,1024]{1,0:T(8,128)(2,1)S(1)}, u32[]{:S(2)}, u32[]{:S(2)}) collective-permute-start(bf16[128,1024]{1,0:T(8,128)(2,1)S(1)} %get-tuple-element.55), channel_id=1, source_target_pairs={{0,1},{1,0},{2,3},{3,2},{4,5},{5,4},{6,7},{7,6},{8,9},{9,8},{10,11... | collective-permute-start | bytes 786440 | tf_op jit(solution)/shard_map/ppermute | solution.py:296
  34.4 11.3 %collective-permute-start.6 = (bf16[128,1024]{1,0:T(8,128)(2,1)S(1)}, bf16[128,1024]{1,0:T(8,128)(2,1)S(1)}, u32[]{:S(2)}, u32[]{:S(2)}) collective-permute-start(bf16[128,1024]{1,0:T(8,128)(2,1)S(1)} %get-tuple-element.56), channel_id=1, source_target_pairs={{0,2},{1,3},{2,0},{3,1},{4,6},{5,7},{6,4},{7,5},{8,10},{9,11},{10,... | collective-permute-start | bytes 786440 | tf_op jit(solution)/shard_map/ppermute | solution.py:296
  35.9 12.3 %collective-permute-start.7 = (bf16[128,1024]{1,0:T(8,128)(2,1)S(1)}, bf16[128,1024]{1,0:T(8,128)(2,1)S(1)}, u32[]{:S(2)}, u32[]{:S(2)}) collective-permute-start(bf16[128,1024]{1,0:T(8,128)(2,1)S(1)} %get-tuple-element.57), channel_id=1, source_target_pairs={{0,3},{1,2},{2,1},{3,0},{4,7},{5,6},{6,5},{7,4},{8,11},{9,10},{10,... | collective-permute-start | bytes 786440 | tf_op jit(solution)/shard_map/ppermute | solution.py:296
  41.2 23.5 %collective-permute-start.15 = (bf16[4,128,512]{2,1,0:T(8,128)(2,1)S(1)}, bf16[4,128,512]{2,1,0:T(8,128)(2,1)S(1)}, u32[]{:S(2)}, u32[]{:S(2)}) collective-permute-start(bf16[4,128,512]{2,1,0:T(8,128)(2,1)S(1)} %collective-permute-done.14.refs_1_), channel_id=1, source_target_pairs={{0,4},{1,5},{2,6},{3,7},{4,8},{5,9},{6,10},{7,11},{8,12},{9,13},{1... | collective-permute-start | bytes 1572872 | tf_op jit(solution)/shard_map/ppermute | solution.py:300
  48.3 13.3 %collective-permute-start.16 = (bf16[128,1024]{1,0:T(8,128)(2,1)S(1)}, bf16[128,1024]{1,0:T(8,128)(2,1)S(1)}, u32[]{:S(2)}, u32[]{:S(2)}) collective-permute-start(bf16[128,1024]{1,0:T(8,128)(2,1)S(1)} %get-tuple-element.75), channel_id=1, source_target_pairs={{0,1},{1,0},{2,3},{3,2},{4,5},{5,4},{6,7},{7,6},{8,9},{9,8},{10,11... | collective-permute-start | bytes 786440 | tf_op jit(solution)/shard_map/ppermute | solution.py:296
  48.5 14.6 %collective-permute-start.17 = (bf16[128,1024]{1,0:T(8,128)(2,1)S(1)}, bf16[128,1024]{1,0:T(8,128)(2,1)S(1)}, u32[]{:S(2)}, u32[]{:S(2)}) collective-permute-start(bf16[128,1024]{1,0:T(8,128)(2,1)S(1)} %get-tuple-element.76), channel_id=1, source_target_pairs={{0,2},{1,3},{2,0},{3,1},{4,6},{5,7},{6,4},{7,5},{8,10},{9,11},{10,... | collective-permute-start | bytes 786440 | tf_op jit(solution)/shard_map/ppermute | solution.py:296
  50.0 13.4 %collective-permute-start.18 = (bf16[128,1024]{1,0:T(8,128)(2,1)S(1)}, bf16[128,1024]{1,0:T(8,128)(2,1)S(1)}, u32[]{:S(2)}, u32[]{:S(2)}) collective-permute-start(bf16[128,1024]{1,0:T(8,128)(2,1)S(1)} %get-tuple-element.77), channel_id=1, source_target_pairs={{0,3},{1,2},{2,1},{3,0},{4,7},{5,6},{6,5},{7,4},{8,11},{9,10},{10,... | collective-permute-start | bytes 786440 | tf_op jit(solution)/shard_map/ppermute | solution.py:296
  61.5 12.3 %collective-permute-start.8 = (bf16[128,1024]{1,0:T(8,128)(2,1)S(1)}, bf16[128,1024]{1,0:T(8,128)(2,1)S(1)}, u32[]{:S(2)}, u32[]{:S(2)}) collective-permute-start(bf16[128,1024]{1,0:T(8,128)(2,1)S(1)} %get-tuple-element.59), channel_id=1, source_target_pairs={{0,1},{1,0},{2,3},{3,2},{4,5},{5,4},{6,7},{7,6},{8,9},{9,8},{10,11... | collective-permute-start | bytes 786440 | tf_op jit(solution)/shard_map/ppermute | solution.py:296
  61.6 12.2 %collective-permute-start.9 = (bf16[128,1024]{1,0:T(8,128)(2,1)S(1)}, bf16[128,1024]{1,0:T(8,128)(2,1)S(1)}, u32[]{:S(2)}, u32[]{:S(2)}) collective-permute-start(bf16[128,1024]{1,0:T(8,128)(2,1)S(1)} %get-tuple-element.60), channel_id=1, source_target_pairs={{0,2},{1,3},{2,0},{3,1},{4,6},{5,7},{6,4},{7,5},{8,10},{9,11},{10,... | collective-permute-start | bytes 786440 | tf_op jit(solution)/shard_map/ppermute | solution.py:296
  63.1 12.3 %collective-permute-start.10 = (bf16[128,1024]{1,0:T(8,128)(2,1)S(1)}, bf16[128,1024]{1,0:T(8,128)(2,1)S(1)}, u32[]{:S(2)}, u32[]{:S(2)}) collective-permute-start(bf16[128,1024]{1,0:T(8,128)(2,1)S(1)} %get-tuple-element.61), channel_id=1, source_target_pairs={{0,3},{1,2},{2,1},{3,0},{4,7},{5,6},{6,5},{7,4},{8,11},{9,10},{10,... | collective-permute-start | bytes 786440 | tf_op jit(solution)/shard_map/ppermute | solution.py:296
  63.4 16.8 %collective-permute-start.22 = (bf16[4,128,512]{2,1,0:T(8,128)(2,1)S(1)}, bf16[4,128,512]{2,1,0:T(8,128)(2,1)S(1)}, u32[]{:S(2)}, u32[]{:S(2)}) collective-permute-start(bf16[4,128,512]{2,1,0:T(8,128)(2,1)S(1)} %get-tuple-element.84), channel_id=1, source_target_pairs={{4,0},{5,1},{6,2},{7,3},{8,4},{9,5},{10,6},{11,7},{12,8},{13,9},{1... | collective-permute-start | bytes 1572872 | tf_op jit(solution)/shard_map/ppermute | solution.py:300
  75.4 17.1 %collective-permute-start.30 = (bf16[4,128,512]{2,1,0:T(8,128)(2,1)S(1)}, bf16[4,128,512]{2,1,0:T(8,128)(2,1)S(1)}, u32[]{:S(2)}, u32[]{:S(2)}) collective-permute-start(bf16[4,128,512]{2,1,0:T(8,128)(2,1)S(1)} %get-tuple-element.89), channel_id=1, source_target_pairs={{4,0},{5,1},{6,2},{7,3},{8,4},{9,5},{10,6},{11,7},{12,8},{13,9},{1... | collective-permute-start | bytes 1572872 | tf_op jit(solution)/shard_map/ppermute | solution.py:300
  80.4 23.4 %collective-permute-start.23 = (bf16[4,128,512]{2,1,0:T(8,128)(2,1)S(1)}, bf16[4,128,512]{2,1,0:T(8,128)(2,1)S(1)}, u32[]{:S(2)}, u32[]{:S(2)}) collective-permute-start(bf16[4,128,512]{2,1,0:T(8,128)(2,1)S(1)} %add_convert_fusion.2), channel_id=1, source_target_pairs={{4,0},{5,1},{6,2},{7,3},{8,4},{9,5},{10,6},{11,7},{12,8},{13,9},{1... | collective-permute-start | bytes 1572872 | tf_op jit(solution)/shard_map/ppermute | solution.py:300
  81.7 12.2 %collective-permute-start.19 = (bf16[128,1024]{1,0:T(8,128)(2,1)S(1)}, bf16[128,1024]{1,0:T(8,128)(2,1)S(1)}, u32[]{:S(2)}, u32[]{:S(2)}) collective-permute-start(bf16[128,1024]{1,0:T(8,128)(2,1)S(1)} %get-tuple-element.79), channel_id=1, source_target_pairs={{0,1},{1,0},{2,3},{3,2},{4,5},{5,4},{6,7},{7,6},{8,9},{9,8},{10,11... | collective-permute-start | bytes 786440 | tf_op jit(solution)/shard_map/ppermute | solution.py:296
  82.4 11.6 %collective-permute-start.20 = (bf16[128,1024]{1,0:T(8,128)(2,1)S(1)}, bf16[128,1024]{1,0:T(8,128)(2,1)S(1)}, u32[]{:S(2)}, u32[]{:S(2)}) collective-permute-start(bf16[128,1024]{1,0:T(8,128)(2,1)S(1)} %get-tuple-element.80), channel_id=1, source_target_pairs={{0,2},{1,3},{2,0},{3,1},{4,6},{5,7},{6,4},{7,5},{8,10},{9,11},{10,... | collective-permute-start | bytes 786440 | tf_op jit(solution)/shard_map/ppermute | solution.py:296
  85.5 11.7 %collective-permute-start.21 = (bf16[128,1024]{1,0:T(8,128)(2,1)S(1)}, bf16[128,1024]{1,0:T(8,128)(2,1)S(1)}, u32[]{:S(2)}, u32[]{:S(2)}) collective-permute-start(bf16[128,1024]{1,0:T(8,128)(2,1)S(1)} %get-tuple-element.81), channel_id=1, source_target_pairs={{0,3},{1,2},{2,1},{3,0},{4,7},{5,6},{6,5},{7,4},{8,11},{9,10},{10,... | collective-permute-start | bytes 786440 | tf_op jit(solution)/shard_map/ppermute | solution.py:296
  97.2 10.2 %collective-permute-start.34 = (bf16[128,512]{1,0:T(8,128)(2,1)S(1)}, bf16[128,512]{1,0:T(8,128)(2,1)S(1)}, u32[]{:S(2)}, u32[]{:S(2)}) collective-permute-start(bf16[128,512]{1,0:T(8,128)(2,1)S(1)} %get-tuple-element.94), channel_id=1, source_target_pairs={{4,3},{5,2},{6,1},{7,0},{8,7},{9,6},{10,5},{11,4},{12,11},{13,10},... | collective-permute-start | bytes 393224 | tf_op jit(solution)/shard_map/ppermute | solution.py:308
  98.5 11.9 %collective-permute-start.33 = (bf16[128,512]{1,0:T(8,128)(2,1)S(1)}, bf16[128,512]{1,0:T(8,128)(2,1)S(1)}, u32[]{:S(2)}, u32[]{:S(2)}) collective-permute-start(bf16[128,512]{1,0:T(8,128)(2,1)S(1)} %get-tuple-element.95), channel_id=1, source_target_pairs={{4,2},{5,3},{6,0},{7,1},{8,6},{9,7},{10,4},{11,5},{12,10},{13,11},... | collective-permute-start | bytes 393224 | tf_op jit(solution)/shard_map/ppermute | solution.py:308
  99.8 13.0 %collective-permute-start.32 = (bf16[128,512]{1,0:T(8,128)(2,1)S(1)}, bf16[128,512]{1,0:T(8,128)(2,1)S(1)}, u32[]{:S(2)}, u32[]{:S(2)}) collective-permute-start(bf16[128,512]{1,0:T(8,128)(2,1)S(1)} %get-tuple-element.96), channel_id=1, source_target_pairs={{4,1},{5,0},{6,3},{7,2},{8,5},{9,4},{10,7},{11,6},{12,9},{13,8},{1... | collective-permute-start | bytes 393224 | tf_op jit(solution)/shard_map/ppermute | solution.py:308
  101.1 13.9 %collective-permute-start.31 = (bf16[128,512]{1,0:T(8,128)(2,1)S(1)}, bf16[128,512]{1,0:T(8,128)(2,1)S(1)}, u32[]{:S(2)}, u32[]{:S(2)}) collective-permute-start(bf16[128,512]{1,0:T(8,128)(2,1)S(1)} %get-tuple-element.97), channel_id=1, source_target_pairs={{4,0},{5,1},{6,2},{7,3},{8,4},{9,5},{10,6},{11,7},{12,8},{13,9},{1... | collective-permute-start | bytes 393224 | tf_op jit(solution)/shard_map/ppermute | solution.py:308
  104.0 11.0 %collective-permute-start.26 = (bf16[128,512]{1,0:T(8,128)(2,1)S(1)}, bf16[128,512]{1,0:T(8,128)(2,1)S(1)}, u32[]{:S(2)}, u32[]{:S(2)}) collective-permute-start(bf16[128,512]{1,0:T(8,128)(2,1)S(1)} %get-tuple-element.102), channel_id=1, source_target_pairs={{0,3},{1,2},{2,1},{3,0},{4,7},{5,6},{6,5},{7,4},{8,11},{9,10},{10,... | collective-permute-start | bytes 393224 | tf_op jit(solution)/shard_map/ppermute | solution.py:296
  (15 other events, 101.2 us)

commit v5 on v4

--- a/solution.py
+++ b/solution.py
@@ -117,27 +117,18 @@
     )(info, *pieces, *more)
 
 
-def attention_kernel(members, hops, group, rows, info, *refs):
+def attention_kernel(members, hops, group, rows, heads, info, *refs):
     planes = hops + 1
     kv_refs = refs[:planes]
     q_refs = refs[planes : planes + members]
     o_refs = refs[planes + members : planes + 2 * members]
     dkv_refs = refs[planes + 2 * members : 2 * planes + 2 * members]
-    k_s, v_s, kt_s, vt_s, dk_s, dv_s, q_s, o_s, p_all, eg_all, ds_all = refs[2 * planes + 2 * members :]
+    k_all, v_all, kt_all, vt_all, dk_all, dv_all, q_s, o_s, p_all, eg_all, ds_all = refs[2 * planes + 2 * members :]
     me = info[0]
     plane = info[1]
     blocks = WINDOW // rows + 1
     wide = group * rows
-    for k in range(planes):
-        for s in range(members):
-            at = (k * members + s) * rows
-            piece = kv_refs[k][me ^ s]
-            k_s[at : at + rows, :] = piece[:, :HEAD]
-            v_s[at : at + rows, :] = piece[:, HEAD:]
-            kt_s[:, at : at + rows] = piece[:, :HEAD].T
-            vt_s[:, at : at + rows] = piece[:, HEAD:].T
-    for m in range(members):
-        q_s[m] = q_refs[m][...]
+    wide_q = 2 * group * HEAD
     key_at = lax.broadcasted_iota(jnp.int32, (rows, wide), 0)
     query_at = lax.broadcasted_iota(jnp.int32, (rows, wide), 1) % rows
     behind = key_at > query_at
@@ -145,9 +136,26 @@
     pairs = [(b, min(b + JOIN, blocks)) for b in range(0, blocks, JOIN)]
     state = {}
 
-    def forward(s):
-        p_s, eg_s = p_all.at[s % BUFFERS], eg_all.at[s % BUFFERS]
-        q_all = q_s[me ^ s]
+    def prepare(h):
+        k_s, v_s, kt_s, vt_s = k_all.at[h % BUFFERS], v_all.at[h % BUFFERS], kt_all.at[h % BUFFERS], vt_all.at[h % BUFFERS]
+        for m in range(members):
+            q_s[h, m] = q_refs[m][:, h * wide_q : (h + 1) * wide_q]
+        for k in range(planes):
+            for s in range(members):
+                at = (k * members + s) * rows
+                keys = kv_refs[k][me ^ s, :, 2 * h * HEAD : (2 * h + 1) * HEAD]
+                values = kv_refs[k][me ^ s, :, (2 * h + 1) * HEAD : (2 * h + 2) * HEAD]
+                k_s[at : at + rows, :] = keys
+                v_s[at : at + rows, :] = values
+                kt_s[:, at : at + rows] = keys.T
+                vt_s[:, at : at + rows] = values.T
+            yield
+
+    def forward(h, s):
+        turn = (h * members + s) % BUFFERS
+        k_s, vt_s = k_all.at[h % BUFFERS], vt_all.at[h % BUFFERS]
+        p_s, eg_s = p_all.at[turn], eg_all.at[turn]
+        q_all = q_s[h, me ^ s]
         q = jnp.concatenate([q_all[:, g * HEAD : (g + 1) * HEAD] for g in range(group)], axis=0)
         go = jnp.concatenate([q_all[:, (group + g) * HEAD : (group + g + 1) * HEAD] for g in range(group)], axis=0)
         totals = [jnp.zeros((8, wide), F32) for _ in range(planes)]
@@ -174,22 +182,25 @@
         gdot = jnp.sum(ot.astype(F32) * got.astype(F32), axis=0, keepdims=True)
         o = ot.astype(F32).T.astype(BF16)
         for g in range(group):
-            o_s[me ^ s, :, g * HEAD : (g + 1) * HEAD] = o[g * rows : (g + 1) * rows]
-        state[s] = (q, got, gdot)
+            o_s[h, me ^ s, :, g * HEAD : (g + 1) * HEAD] = o[g * rows : (g + 1) * rows]
+        state[h, s] = (q, got, gdot)
         yield
 
-    def inner(s):
-        eg_s, ds_s = eg_all.at[s % BUFFERS], ds_all.at[s % BUFFERS]
-        q, got, gdot = state[s]
+    def inner(h, s):
+        turn = (h * members + s) % BUFFERS
+        v_s, eg_s, ds_s = v_all.at[h % BUFFERS], eg_all.at[turn], ds_all.at[turn]
+        q, got, gdot = state[h, s]
         for low, high in pairs:
             dps = dot(v_s[(s + low) * rows : (s + high) * rows, :], got, 1, 0)
             part = slice(low * rows, high * rows)
             ds_s[part, :] = ((dps - gdot) * eg_s[part, :]).astype(BF16)
             yield
 
-    def outer(s):
-        p_s, ds_s = p_all.at[s % BUFFERS], ds_all.at[s % BUFFERS]
-        q, got, gdot = state.pop(s)
+    def outer(h, s):
+        turn = (h * members + s) % BUFFERS
+        kt_s, dk_s, dv_s = kt_all.at[h % BUFFERS], dk_all.at[h % BUFFERS], dv_all.at[h % BUFFERS]
+        p_s, ds_s = p_all.at[turn], ds_all.at[turn]
+        q, got, gdot = state.pop((h, s))
         old = slice(s * rows, (s + blocks - 1) * rows)
         new = slice((s + blocks - 1) * rows, (s + blocks) * rows)
 
@@ -207,8 +218,20 @@
         dqt = dot(kt_s[:, s * rows : (s + blocks) * rows], ds_s[...], 1, 0)
         dq = (dqt * SCORE_SCALE).T.astype(BF16)
         for g in range(group):
-            o_s[me ^ s, :, (group + g) * HEAD : (group + g + 1) * HEAD] = dq[g * rows : (g + 1) * rows]
+            o_s[h, me ^ s, :, (group + g) * HEAD : (group + g + 1) * HEAD] = dq[g * rows : (g + 1) * rows]
         yield
+
+    def finish(h):
+        dk_s, dv_s = dk_all.at[h % BUFFERS], dv_all.at[h % BUFFERS]
+        for k in range(planes):
+            for s in range(members):
+                at = (k * members + s) * rows
+                keys = (dk_s[at : at + rows, :] * SCORE_SCALE).astype(BF16)
+                dkv_refs[k][me ^ s, :, 2 * h * HEAD : (2 * h + 1) * HEAD] = keys
+                dkv_refs[k][me ^ s, :, (2 * h + 1) * HEAD : (2 * h + 2) * HEAD] = dv_s[at : at + rows, :].astype(BF16)
+            yield
+        for m in range(members):
+            o_refs[m][:, h * wide_q : (h + 1) * wide_q] = o_s[h, m]
 
     def together(*walks):
         walks = list(walks)
@@ -217,49 +240,44 @@
                 if next(walk, walk) is walk:
                     walks.remove(walk)
 
-    together(forward(0))
-    for s in range(members):
-        together(inner(s))
-        together(*([forward(s + 1)] if s + 1 < members else []), outer(s))
-    for m in range(members):
-        o_refs[m][...] = o_s[m]
-    for k in range(planes):
-        for s in range(members):
-            at = (k * members + s) * rows
-            dkv_refs[k][me ^ s, :, :HEAD] = (dk_s[at : at + rows, :] * SCORE_SCALE).astype(BF16)
-            dkv_refs[k][me ^ s, :, HEAD:] = dv_s[at : at + rows, :].astype(BF16)
+    tiles = [(h, s) for h in range(heads) for s in range(members)]
+    together(prepare(0))
+    together(forward(0, 0))
+    for i, (h, s) in enumerate(tiles):
+        together(inner(h, s))
+        beside = [outer(h, s)]
+        if i + 1 < len(tiles):
+            beside.insert(0, forward(*tiles[i + 1]))
+        if s == 1 and h + 1 < heads:
+            beside.append(prepare(h + 1))
+        if s == 0 and h > 0:
+            beside.append(finish(h - 1))
+        together(*beside)
+    together(finish(heads - 1))
 
 
 def attention(info, kvs, qs, group, first=0, heads=None):
     planes, members = len(kvs), len(qs)
     rows = qs[0].shape[0]
-    heads = heads or kvs[0].shape[2] // (2 * HEAD)
+    heads = kvs[0].shape[2] // (2 * HEAD)
     keys_all = planes * members * rows
     wide = group * rows
     span = WINDOW + rows
-
-    def kv_spec(start):
-        return pl.BlockSpec((members, rows, 2 * HEAD), lambda h: (0, 0, h + start))
-
-    def q_spec(start):
-        return pl.BlockSpec((rows, 2 * group * HEAD), lambda h: (0, h + start))
-
     return pl.pallas_call(
-        functools.partial(attention_kernel, members, planes - 1, group, rows),
-        grid=(heads,),
-        out_shape=[jax.ShapeDtypeStruct((rows, heads * 2 * group * HEAD), BF16)] * members
-        + [jax.ShapeDtypeStruct((members, rows, heads * 2 * HEAD), BF16)] * planes,
-        in_specs=[smem()] + [kv_spec(first)] * planes + [q_spec(first)] * members,
-        out_specs=[q_spec(0)] * members + [kv_spec(0)] * planes,
+        functools.partial(attention_kernel, members, planes - 1, group, rows, heads),
+        out_shape=[jax.ShapeDtypeStruct(q.shape, BF16) for q in qs]
+        + [jax.ShapeDtypeStruct(kv.shape, BF16) for kv in kvs],
+        in_specs=[smem()] + [vmem()] * (planes + members),
+        out_specs=[vmem()] * (planes + members),
         scratch_shapes=[
-            pltpu.VMEM((keys_all, HEAD), BF16),
-            pltpu.VMEM((keys_all, HEAD), BF16),
-            pltpu.VMEM((HEAD, keys_all), BF16),
-            pltpu.VMEM((HEAD, keys_all), BF16),
-            pltpu.VMEM((keys_all, HEAD), F32),
-            pltpu.VMEM((keys_all, HEAD), F32),
-            pltpu.VMEM((members, rows, 2 * group * HEAD), BF16),
-            pltpu.VMEM((members, rows, 2 * group * HEAD), BF16),
+            pltpu.VMEM((BUFFERS, keys_all, HEAD), BF16),
+            pltpu.VMEM((BUFFERS, keys_all, HEAD), BF16),
+            pltpu.VMEM((BUFFERS, HEAD, keys_all), BF16),
+            pltpu.VMEM((BUFFERS, HEAD, keys_all), BF16),
+            pltpu.VMEM((BUFFERS, keys_all, HEAD), F32),
+            pltpu.VMEM((BUFFERS, keys_all, HEAD), F32),
+            pltpu.VMEM((heads, members, rows, 2 * group * HEAD), BF16),
+            pltpu.VMEM((heads, members, rows, 2 * group * HEAD), BF16),
             pltpu.VMEM((BUFFERS, span, wide), BF16),
             pltpu.VMEM((BUFFERS, span, wide), F32),
             pltpu.VMEM((BUFFERS, span, wide), BF16),

time: 118 us -> 117 us (level)
  Pallas kernels: 24.1 us -> 22.6 us
    pallas_call x2, Pallas kernels: 18 us -> 16.5 us  [attention(): pl.pallas_call(functools.partial(attention_kernel, members, planes - 1, g...]
  transfers between devices with their start and end apart: 35 -> 35, of which waited for: 19 -> 19; matrix products, arithmetic and copies ran while one was open for 1% -> 1% of each run, Pallas kernels for 18% -> 17%
where the time goes in v5:
time: 117 us
  waiting for transfers between devices  49.4 us (42%)
  starting transfers between devices  41.1 us (35%)
  Pallas kernels  22.6 us (19%)
  local copies, waits for them, and re-layouts  2.2 us (2%)
    ppermute x24, waiting for transfers between devices, swap(): lax.ppermute(pieces[m], axes, pairs[m])  25.8 us
    ppermute x7, starting transfers between devices, hop(): return lax.ppermute(array, axes, pairs)  19.7 us
    ppermute x7, waiting for transfers between devices, hop(): return lax.ppermute(array, axes, pairs)  16.6 us
    pallas_call x2, Pallas kernels, attention(): pl.pallas_call(functools.partial(attention_kernel, members, planes - 1, g...  16.5 us
    ppermute x24, starting transfers between devices, swap(): lax.ppermute(pieces[m], axes, pairs[m])  16.3 us
    ppermute x4, waiting for transfers between devices, hop_across(): return [lax.ppermute(pieces[m], axes, pairs[m]) for m in range(members)]  7.05 us
    ppermute x4, starting transfers between devices, hop_across(): return [lax.ppermute(pieces[m], axes, pairs[m]) for m in range(members)]  5.17 us
    pallas_call x2, Pallas kernels, unpack(): pl.pallas_call(functools.partial(unpack_kernel, chunks, members, group, h...  4.14 us
  transfers between devices with their start and end apart: 35, of which 19 were waited for; matrix products, arithmetic and copies ran while one was open for 1% of the time, Pallas kernels for 17%

profile of v5, /device:TPU:0, one launch (start us, length us, event | category | flops | bytes accessed | tf_op | source)
XLA Modules:
  0.0 116.9 jit_solution(14873144793478733606)
XLA Ops:
  4.2 2.6 %collective-permute-start.1 = (bf16[128,512]{1,0:T(8,128)(2,1)S(1)}, bf16[128,512]{1,0:T(8,128)(2,1)S(1)}, u32[]{:S(2)}, u32[]{:S(2)}) collective-permute-start(bf16[128,512]{1,0:T(8,128)(2,1)S(1)} %get-tuple-element.51), channel_id=1, source_target_pairs={{0,2},{1,3},{2,0},{3,1},{4,6},{5,7},{6,4},{7,5},{8,10},{9,11},{10,... | collective-permute-start | bytes 393224 | tf_op jit(solution)/shard_map/ppermute | solution.py:314
  6.8 4.3 %collective-permute-done.1 = bf16[128,512]{1,0:T(8,128)(2,1)S(1)} collective-permute-done((bf16[128,512]{1,0:T(8,128)(2,1)S(1)}, bf16[128,512]{1,0:T(8,128)(2,1)S(1)}, u32[]{:S(2)}, u32[]{:S(2)}) %collective-permute-start.1) | collective-permute-done | bytes 131104 | tf_op jit(solution)/shard_map/ppermute | solution.py:314
  11.1 2.3 %collective-permute-done.2 = bf16[128,512]{1,0:T(8,128)(2,1)S(1)} collective-permute-done((bf16[128,512]{1,0:T(8,128)(2,1)S(1)}, bf16[128,512]{1,0:T(8,128)(2,1)S(1)}, u32[]{:S(2)}, u32[]{:S(2)}) %collective-permute-start.2) | collective-permute-done | bytes 131104 | tf_op jit(solution)/shard_map/ppermute | solution.py:314
  13.4 3.7 %collective-permute-start.3 = (bf16[4,128,512]{2,1,0:T(8,128)(2,1)S(1)}, bf16[4,128,512]{2,1,0:T(8,128)(2,1)S(1)}, u32[]{:S(2)}, u32[]{:S(2)}) collective-permute-start(bf16[4,128,512]{2,1,0:T(8,128)(2,1)S(1)} %pad_maximum_fusion.refs_2_), channel_id=1, source_target_pairs={{0,4},{1,5},{2,6},{3,7},{4,8},{5,9},{6,10},{7,11},{8,12},{9,13},{1... | collective-permute-start | bytes 1572872 | tf_op jit(solution)/shard_map/ppermute | solution.py:318
  19.1 4.5 %collective-permute-done.12 = bf16[128,512]{1,0:T(8,128)(2,1)S(1)} collective-permute-done((bf16[128,512]{1,0:T(8,128)(2,1)S(1)}, bf16[128,512]{1,0:T(8,128)(2,1)S(1)}, u32[]{:S(2)}, u32[]{:S(2)}) %collective-permute-start.12) | collective-permute-done | bytes 131104 | tf_op jit(solution)/shard_map/ppermute | solution.py:314
  23.6 1.9 %collective-permute-done.13 = bf16[128,512]{1,0:T(8,128)(2,1)S(1)} collective-permute-done((bf16[128,512]{1,0:T(8,128)(2,1)S(1)}, bf16[128,512]{1,0:T(8,128)(2,1)S(1)}, u32[]{:S(2)}, u32[]{:S(2)}) %collective-permute-start.13) | collective-permute-done | bytes 131104 | tf_op jit(solution)/shard_map/ppermute | solution.py:314
  25.6 3.5 %collective-permute-start.14 = (bf16[4,128,512]{2,1,0:T(8,128)(2,1)S(1)}, bf16[4,128,512]{2,1,0:T(8,128)(2,1)S(1)}, u32[]{:S(2)}, u32[]{:S(2)}) collective-permute-start(bf16[4,128,512]{2,1,0:T(8,128)(2,1)S(1)} %pad_maximum_fusion.1.refs_2_), channel_id=1, source_target_pairs={{0,4},{1,5},{2,6},{3,7},{4,8},{5,9},{6,10},{7,11},{8,12},{9,13},{1... | collective-permute-start | bytes 1572872 | tf_op jit(solution)/shard_map/ppermute | solution.py:318
  29.1 4.1 %collective-permute-start.4 = (bf16[4,128,512]{2,1,0:T(8,128)(2,1)S(1)}, bf16[4,128,512]{2,1,0:T(8,128)(2,1)S(1)}, u32[]{:S(2)}, u32[]{:S(2)}) collective-permute-start(bf16[4,128,512]{2,1,0:T(8,128)(2,1)S(1)} %collective-permute-done.3.refs_1_), channel_id=1, source_target_pairs={{0,4},{1,5},{2,6},{3,7},{4,8},{5,9},{6,10},{7,11},{8,12},{9,13},{1... | collective-permute-start | bytes 1572872 | tf_op jit(solution)/shard_map/ppermute | solution.py:318
  36.2 5.0 %collective-permute-done.14.refs_1_ = bf16[4,128,512]{2,1,0:T(8,128)(2,1)S(1)} collective-permute-done((bf16[4,128,512]{2,1,0:T(8,128)(2,1)S(1)}, bf16[4,128,512]{2,1,0:T(8,128)(2,1)S(1)}, u32[]{:S(2)}, u32[]{:S(2)}) %collective-permute-start.14) | collective-permute-done | bytes 524320 | tf_op jit(solution)/shard_map/ppermute | solution.py:318
  41.2 4.4 %collective-permute-start.15 = (bf16[4,128,512]{2,1,0:T(8,128)(2,1)S(1)}, bf16[4,128,512]{2,1,0:T(8,128)(2,1)S(1)}, u32[]{:S(2)}, u32[]{:S(2)}) collective-permute-start(bf16[4,128,512]{2,1,0:T(8,128)(2,1)S(1)} %collective-permute-done.14.refs_1_), channel_id=1, source_target_pairs={{0,4},{1,5},{2,6},{3,7},{4,8},{5,9},{6,10},{7,11},{8,12},{9,13},{1... | collective-permute-start | bytes 1572872 | tf_op jit(solution)/shard_map/ppermute | solution.py:318
  45.7 2.6 %collective-permute-done.7.refs_6_ = bf16[128,1024]{1,0:T(8,128)(2,1)S(1)} collective-permute-done((bf16[128,1024]{1,0:T(8,128)(2,1)S(1)}, bf16[128,1024]{1,0:T(8,128)(2,1)S(1)}, u32[]{:S(2)}, u32[]{:S(2)}) %collective-permute-start.7) | collective-permute-done | bytes 262176 | tf_op jit(solution)/shard_map/ppermute | solution.py:314
  50.1 2.4 %collective-permute-done.4.refs_0_ = bf16[4,128,512]{2,1,0:T(8,128)(2,1)S(1)} collective-permute-done((bf16[4,128,512]{2,1,0:T(8,128)(2,1)S(1)}, bf16[4,128,512]{2,1,0:T(8,128)(2,1)S(1)}, u32[]{:S(2)}, u32[]{:S(2)}) %collective-permute-start.4) | collective-permute-done | bytes 524320 | tf_op jit(solution)/shard_map/ppermute | solution.py:318
  52.5 8.2 %attention.2 = (bf16[128,1024]{1,0:T(8,128)(2,1)S(1)}, bf16[128,1024]{1,0:T(8,128)(2,1)S(1)}, bf16[128,1024]{1,0:T(8,128)(2,1)S(1)}, bf16[128,1024]{1,0:T(8,128)...) custom-call(s32[2]{0:T(128)S(1)} %pad_add_fusion.info, ...), custom_call_target="tpu_custom_call" | custom-call | flops 3623878656 | bytes 5242880 | tf_op jit(solution)/shard_map/attention/pallas_call | solution.py:266
  64.2 8.2 %attention.3 = (bf16[128,1024]{1,0:T(8,128)(2,1)S(1)}, bf16[128,1024]{1,0:T(8,128)(2,1)S(1)}, bf16[128,1024]{1,0:T(8,128)(2,1)S(1)}, bf16[128,1024]{1,0:T(8,128)...) custom-call(s32[2]{0:T(128)S(1)} %pad_add_fusion.info, ...), custom_call_target="tpu_custom_call" | custom-call | flops 3623878656 | bytes 5242880 | tf_op jit(solution)/shard_map/attention/pallas_call | solution.py:266
  72.4 2.2 %collective-permute-done.10.refs_3_ = bf16[128,1024]{1,0:T(8,128)(2,1)S(1)} collective-permute-done((bf16[128,1024]{1,0:T(8,128)(2,1)S(1)}, bf16[128,1024]{1,0:T(8,128)(2,1)S(1)}, u32[]{:S(2)}, u32[]{:S(2)}) %collective-permute-start.10) | collective-permute-done | bytes 262176 | tf_op jit(solution)/shard_map/ppermute | solution.py:314
  76.0 1.7 %collective-permute-start.29 = (bf16[128,512]{1,0:T(8,128)(2,1)S(1)}, bf16[128,512]{1,0:T(8,128)(2,1)S(1)}, u32[]{:S(2)}, u32[]{:S(2)}) collective-permute-start(bf16[128,512]{1,0:T(8,128)(2,1)S(1)} %get-tuple-element.98), channel_id=1, source_target_pairs={{0,3},{1,2},{2,1},{3,0},{4,7},{5,6},{6,5},{7,4},{8,11},{9,10},{10,... | collective-permute-start | bytes 393224 | tf_op jit(solution)/shard_map/ppermute | solution.py:314
  82.6 2.0 %collective-permute-done.28.refs_6_ = bf16[128,512]{1,0:T(8,128)(2,1)S(1)} collective-permute-done((bf16[128,512]{1,0:T(8,128)(2,1)S(1)}, bf16[128,512]{1,0:T(8,128)(2,1)S(1)}, u32[]{:S(2)}, u32[]{:S(2)}) %collective-permute-start.28) | collective-permute-done | bytes 131104 | tf_op jit(solution)/shard_map/ppermute | solution.py:314
  85.2 6.6 %collective-permute-done.30 = bf16[4,128,512]{2,1,0:T(8,128)(2,1)S(1)} collective-permute-done((bf16[4,128,512]{2,1,0:T(8,128)(2,1)S(1)}, bf16[4,128,512]{2,1,0:T(8,128)(2,1)S(1)}, u32[]{:S(2)}, u32[]{:S(2)}) %collective-permute-start.30) | collective-permute-done | bytes 524320 | tf_op jit(solution)/shard_map/ppermute | solution.py:318
  93.2 3.2 %collective-permute-done.21.refs_7_ = bf16[128,1024]{1,0:T(8,128)(2,1)S(1)} collective-permute-done((bf16[128,1024]{1,0:T(8,128)(2,1)S(1)}, bf16[128,1024]{1,0:T(8,128)(2,1)S(1)}, u32[]{:S(2)}, u32[]{:S(2)}) %collective-permute-start.21) | collective-permute-done | bytes 262176 | tf_op jit(solution)/shard_map/ppermute | solution.py:314
  104.3 2.3 %collective-permute-done.34.refs_11_ = bf16[128,512]{1,0:T(8,128)(2,1)S(1)} collective-permute-done((bf16[128,512]{1,0:T(8,128)(2,1)S(1)}, bf16[128,512]{1,0:T(8,128)(2,1)S(1)}, u32[]{:S(2)}, u32[]{:S(2)}) %collective-permute-start.34) | collective-permute-done | bytes 131104 | tf_op jit(solution)/shard_map/ppermute | solution.py:326
  107.1 2.5 %collective-permute-done.33.refs_10_ = bf16[128,512]{1,0:T(8,128)(2,1)S(1)} collective-permute-done((bf16[128,512]{1,0:T(8,128)(2,1)S(1)}, bf16[128,512]{1,0:T(8,128)(2,1)S(1)}, u32[]{:S(2)}, u32[]{:S(2)}) %collective-permute-start.33) | collective-permute-done | bytes 131104 | tf_op jit(solution)/shard_map/ppermute | solution.py:326
  109.7 2.4 %unpack.2 = (bf16[128,4096]{1,0:T(8,128)(2,1)}, bf16[128,4096]{1,0:T(8,128)(2,1)}) custom-call(s32[2]{0:T(128)S(1)} %pad_add_fusion.info, bf16[128,1024]{1,0:T(8,128)(2,1)S(1)} %get-tuple-element.58.refs_0_, bf16[128,1024]{1,0:T(8,128)(2,1)S(1)} %collective-permute-done.8.refs_1_, bf16[128,1024]{1,0:T(8,128)(2,1)S(1)} %collective-permute-done.9.refs_2_, ...), custom_call_target="tpu_custom_call" | custom-call | tf_op jit(solution)/shard_map/unpack/pallas_call | solution.py:110
  112.0 2.2 %collective-permute-done.31.refs_8_ = bf16[128,512]{1,0:T(8,128)(2,1)S(1)} collective-permute-done((bf16[128,512]{1,0:T(8,128)(2,1)S(1)}, bf16[128,512]{1,0:T(8,128)(2,1)S(1)}, u32[]{:S(2)}, u32[]{:S(2)}) %collective-permute-start.31) | collective-permute-done | bytes 131104 | tf_op jit(solution)/shard_map/ppermute | solution.py:326
  115.1 1.8 %unpack.3 = (bf16[128,2048]{1,0:T(8,128)(2,1)}, bf16[128,2048]{1,0:T(8,128)(2,1)}) custom-call(s32[2]{0:T(128)S(1)} %pad_add_fusion.info, bf16[128,512]{1,0:T(8,128)(2,1)S(1)} %get-tuple-element.105.refs_0_, bf16[128,512]{1,0:T(8,128)(2,1)S(1)} %collective-permute-done.24.refs_1_, bf16[128,512]{1,0:T(8,128)(2,1)S(1)} %collective-permute-done.25.refs_2_, ...), custom_call_target="tpu_custom_call" | custom-call | tf_op jit(solution)/shard_map/unpack/pallas_call | solution.py:110
  (69 shorter events, 31.3 us)
Async XLA Ops:
  13.4 15.6 %collective-permute-start.3 = (bf16[4,128,512]{2,1,0:T(8,128)(2,1)S(1)}, bf16[4,128,512]{2,1,0:T(8,128)(2,1)S(1)}, u32[]{:S(2)}, u32[]{:S(2)}) collective-permute-start(bf16[4,128,512]{2,1,0:T(8,128)(2,1)S(1)} %pad_maximum_fusion.refs_2_), channel_id=1, source_target_pairs={{0,4},{1,5},{2,6},{3,7},{4,8},{5,9},{6,10},{7,11},{8,12},{9,13},{1... | collective-permute-start | bytes 1572872 | tf_op jit(solution)/shard_map/ppermute | solution.py:318
  25.6 15.7 %collective-permute-start.14 = (bf16[4,128,512]{2,1,0:T(8,128)(2,1)S(1)}, bf16[4,128,512]{2,1,0:T(8,128)(2,1)S(1)}, u32[]{:S(2)}, u32[]{:S(2)}) collective-permute-start(bf16[4,128,512]{2,1,0:T(8,128)(2,1)S(1)} %pad_maximum_fusion.1.refs_2_), channel_id=1, source_target_pairs={{0,4},{1,5},{2,6},{3,7},{4,8},{5,9},{6,10},{7,11},{8,12},{9,13},{1... | collective-permute-start | bytes 1572872 | tf_op jit(solution)/shard_map/ppermute | solution.py:318
  29.1 23.4 %collective-permute-start.4 = (bf16[4,128,512]{2,1,0:T(8,128)(2,1)S(1)}, bf16[4,128,512]{2,1,0:T(8,128)(2,1)S(1)}, u32[]{:S(2)}, u32[]{:S(2)}) collective-permute-start(bf16[4,128,512]{2,1,0:T(8,128)(2,1)S(1)} %collective-permute-done.3.refs_1_), channel_id=1, source_target_pairs={{0,4},{1,5},{2,6},{3,7},{4,8},{5,9},{6,10},{7,11},{8,12},{9,13},{1... | collective-permute-start | bytes 1572872 | tf_op jit(solution)/shard_map/ppermute | solution.py:318
  34.3 11.4 %collective-permute-start.5 = (bf16[128,1024]{1,0:T(8,128)(2,1)S(1)}, bf16[128,1024]{1,0:T(8,128)(2,1)S(1)}, u32[]{:S(2)}, u32[]{:S(2)}) collective-permute-start(bf16[128,1024]{1,0:T(8,128)(2,1)S(1)} %get-tuple-element.55), channel_id=1, source_target_pairs={{0,1},{1,0},{2,3},{3,2},{4,5},{5,4},{6,7},{7,6},{8,9},{9,8},{10,11... | collective-permute-start | bytes 786440 | tf_op jit(solution)/shard_map/ppermute | solution.py:314
  34.4 11.3 %collective-permute-start.6 = (bf16[128,1024]{1,0:T(8,128)(2,1)S(1)}, bf16[128,1024]{1,0:T(8,128)(2,1)S(1)}, u32[]{:S(2)}, u32[]{:S(2)}) collective-permute-start(bf16[128,1024]{1,0:T(8,128)(2,1)S(1)} %get-tuple-element.56), channel_id=1, source_target_pairs={{0,2},{1,3},{2,0},{3,1},{4,6},{5,7},{6,4},{7,5},{8,10},{9,11},{10,... | collective-permute-start | bytes 786440 | tf_op jit(solution)/shard_map/ppermute | solution.py:314
  35.9 12.3 %collective-permute-start.7 = (bf16[128,1024]{1,0:T(8,128)(2,1)S(1)}, bf16[128,1024]{1,0:T(8,128)(2,1)S(1)}, u32[]{:S(2)}, u32[]{:S(2)}) collective-permute-start(bf16[128,1024]{1,0:T(8,128)(2,1)S(1)} %get-tuple-element.57), channel_id=1, source_target_pairs={{0,3},{1,2},{2,1},{3,0},{4,7},{5,6},{6,5},{7,4},{8,11},{9,10},{10,... | collective-permute-start | bytes 786440 | tf_op jit(solution)/shard_map/ppermute | solution.py:314
  41.2 22.9 %collective-permute-start.15 = (bf16[4,128,512]{2,1,0:T(8,128)(2,1)S(1)}, bf16[4,128,512]{2,1,0:T(8,128)(2,1)S(1)}, u32[]{:S(2)}, u32[]{:S(2)}) collective-permute-start(bf16[4,128,512]{2,1,0:T(8,128)(2,1)S(1)} %collective-permute-done.14.refs_1_), channel_id=1, source_target_pairs={{0,4},{1,5},{2,6},{3,7},{4,8},{5,9},{6,10},{7,11},{8,12},{9,13},{1... | collective-permute-start | bytes 1572872 | tf_op jit(solution)/shard_map/ppermute | solution.py:318
  48.3 12.5 %collective-permute-start.16 = (bf16[128,1024]{1,0:T(8,128)(2,1)S(1)}, bf16[128,1024]{1,0:T(8,128)(2,1)S(1)}, u32[]{:S(2)}, u32[]{:S(2)}) collective-permute-start(bf16[128,1024]{1,0:T(8,128)(2,1)S(1)} %get-tuple-element.75), channel_id=1, source_target_pairs={{0,1},{1,0},{2,3},{3,2},{4,5},{5,4},{6,7},{7,6},{8,9},{9,8},{10,11... | collective-permute-start | bytes 786440 | tf_op jit(solution)/shard_map/ppermute | solution.py:314
  48.5 13.8 %collective-permute-start.17 = (bf16[128,1024]{1,0:T(8,128)(2,1)S(1)}, bf16[128,1024]{1,0:T(8,128)(2,1)S(1)}, u32[]{:S(2)}, u32[]{:S(2)}) collective-permute-start(bf16[128,1024]{1,0:T(8,128)(2,1)S(1)} %get-tuple-element.76), channel_id=1, source_target_pairs={{0,2},{1,3},{2,0},{3,1},{4,6},{5,7},{6,4},{7,5},{8,10},{9,11},{10,... | collective-permute-start | bytes 786440 | tf_op jit(solution)/shard_map/ppermute | solution.py:314
  50.0 12.6 %collective-permute-start.18 = (bf16[128,1024]{1,0:T(8,128)(2,1)S(1)}, bf16[128,1024]{1,0:T(8,128)(2,1)S(1)}, u32[]{:S(2)}, u32[]{:S(2)}) collective-permute-start(bf16[128,1024]{1,0:T(8,128)(2,1)S(1)} %get-tuple-element.77), channel_id=1, source_target_pairs={{0,3},{1,2},{2,1},{3,0},{4,7},{5,6},{6,5},{7,4},{8,11},{9,10},{10,... | collective-permute-start | bytes 786440 | tf_op jit(solution)/shard_map/ppermute | solution.py:314
  60.7 11.7 %collective-permute-start.8 = (bf16[128,1024]{1,0:T(8,128)(2,1)S(1)}, bf16[128,1024]{1,0:T(8,128)(2,1)S(1)}, u32[]{:S(2)}, u32[]{:S(2)}) collective-permute-start(bf16[128,1024]{1,0:T(8,128)(2,1)S(1)} %get-tuple-element.59), channel_id=1, source_target_pairs={{0,1},{1,0},{2,3},{3,2},{4,5},{5,4},{6,7},{7,6},{8,9},{9,8},{10,11... | collective-permute-start | bytes 786440 | tf_op jit(solution)/shard_map/ppermute | solution.py:314
  60.8 11.6 %collective-permute-start.9 = (bf16[128,1024]{1,0:T(8,128)(2,1)S(1)}, bf16[128,1024]{1,0:T(8,128)(2,1)S(1)}, u32[]{:S(2)}, u32[]{:S(2)}) collective-permute-start(bf16[128,1024]{1,0:T(8,128)(2,1)S(1)} %get-tuple-element.60), channel_id=1, source_target_pairs={{0,2},{1,3},{2,0},{3,1},{4,6},{5,7},{6,4},{7,5},{8,10},{9,11},{10,... | collective-permute-start | bytes 786440 | tf_op jit(solution)/shard_map/ppermute | solution.py:314
  62.4 12.3 %collective-permute-start.10 = (bf16[128,1024]{1,0:T(8,128)(2,1)S(1)}, bf16[128,1024]{1,0:T(8,128)(2,1)S(1)}, u32[]{:S(2)}, u32[]{:S(2)}) collective-permute-start(bf16[128,1024]{1,0:T(8,128)(2,1)S(1)} %get-tuple-element.61), channel_id=1, source_target_pairs={{0,3},{1,2},{2,1},{3,0},{4,7},{5,6},{6,5},{7,4},{8,11},{9,10},{10,... | collective-permute-start | bytes 786440 | tf_op jit(solution)/shard_map/ppermute | solution.py:314
  62.7 16.8 %collective-permute-start.22 = (bf16[4,128,512]{2,1,0:T(8,128)(2,1)S(1)}, bf16[4,128,512]{2,1,0:T(8,128)(2,1)S(1)}, u32[]{:S(2)}, u32[]{:S(2)}) collective-permute-start(bf16[4,128,512]{2,1,0:T(8,128)(2,1)S(1)} %get-tuple-element.84), channel_id=1, source_target_pairs={{4,0},{5,1},{6,2},{7,3},{8,4},{9,5},{10,6},{11,7},{12,8},{13,9},{1... | collective-permute-start | bytes 1572872 | tf_op jit(solution)/shard_map/ppermute | solution.py:318
  74.7 17.1 %collective-permute-start.30 = (bf16[4,128,512]{2,1,0:T(8,128)(2,1)S(1)}, bf16[4,128,512]{2,1,0:T(8,128)(2,1)S(1)}, u32[]{:S(2)}, u32[]{:S(2)}) collective-permute-start(bf16[4,128,512]{2,1,0:T(8,128)(2,1)S(1)} %get-tuple-element.89), channel_id=1, source_target_pairs={{4,0},{5,1},{6,2},{7,3},{8,4},{9,5},{10,6},{11,7},{12,8},{13,9},{1... | collective-permute-start | bytes 1572872 | tf_op jit(solution)/shard_map/ppermute | solution.py:318
  79.6 23.4 %collective-permute-start.23 = (bf16[4,128,512]{2,1,0:T(8,128)(2,1)S(1)}, bf16[4,128,512]{2,1,0:T(8,128)(2,1)S(1)}, u32[]{:S(2)}, u32[]{:S(2)}) collective-permute-start(bf16[4,128,512]{2,1,0:T(8,128)(2,1)S(1)} %add_convert_fusion.2), channel_id=1, source_target_pairs={{4,0},{5,1},{6,2},{7,3},{8,4},{9,5},{10,6},{11,7},{12,8},{13,9},{1... | collective-permute-start | bytes 1572872 | tf_op jit(solution)/shard_map/ppermute | solution.py:318
  80.9 12.2 %collective-permute-start.19 = (bf16[128,1024]{1,0:T(8,128)(2,1)S(1)}, bf16[128,1024]{1,0:T(8,128)(2,1)S(1)}, u32[]{:S(2)}, u32[]{:S(2)}) collective-permute-start(bf16[128,1024]{1,0:T(8,128)(2,1)S(1)} %get-tuple-element.79), channel_id=1, source_target_pairs={{0,1},{1,0},{2,3},{3,2},{4,5},{5,4},{6,7},{7,6},{8,9},{9,8},{10,11... | collective-permute-start | bytes 786440 | tf_op jit(solution)/shard_map/ppermute | solution.py:314
  81.6 11.6 %collective-permute-start.20 = (bf16[128,1024]{1,0:T(8,128)(2,1)S(1)}, bf16[128,1024]{1,0:T(8,128)(2,1)S(1)}, u32[]{:S(2)}, u32[]{:S(2)}) collective-permute-start(bf16[128,1024]{1,0:T(8,128)(2,1)S(1)} %get-tuple-element.80), channel_id=1, source_target_pairs={{0,2},{1,3},{2,0},{3,1},{4,6},{5,7},{6,4},{7,5},{8,10},{9,11},{10,... | collective-permute-start | bytes 786440 | tf_op jit(solution)/shard_map/ppermute | solution.py:314
  84.7 11.7 %collective-permute-start.21 = (bf16[128,1024]{1,0:T(8,128)(2,1)S(1)}, bf16[128,1024]{1,0:T(8,128)(2,1)S(1)}, u32[]{:S(2)}, u32[]{:S(2)}) collective-permute-start(bf16[128,1024]{1,0:T(8,128)(2,1)S(1)} %get-tuple-element.81), channel_id=1, source_target_pairs={{0,3},{1,2},{2,1},{3,0},{4,7},{5,6},{6,5},{7,4},{8,11},{9,10},{10,... | collective-permute-start | bytes 786440 | tf_op jit(solution)/shard_map/ppermute | solution.py:314
  96.4 10.2 %collective-permute-start.34 = (bf16[128,512]{1,0:T(8,128)(2,1)S(1)}, bf16[128,512]{1,0:T(8,128)(2,1)S(1)}, u32[]{:S(2)}, u32[]{:S(2)}) collective-permute-start(bf16[128,512]{1,0:T(8,128)(2,1)S(1)} %get-tuple-element.94), channel_id=1, source_target_pairs={{4,3},{5,2},{6,1},{7,0},{8,7},{9,6},{10,5},{11,4},{12,11},{13,10},... | collective-permute-start | bytes 393224 | tf_op jit(solution)/shard_map/ppermute | solution.py:326
  97.7 11.9 %collective-permute-start.33 = (bf16[128,512]{1,0:T(8,128)(2,1)S(1)}, bf16[128,512]{1,0:T(8,128)(2,1)S(1)}, u32[]{:S(2)}, u32[]{:S(2)}) collective-permute-start(bf16[128,512]{1,0:T(8,128)(2,1)S(1)} %get-tuple-element.95), channel_id=1, source_target_pairs={{4,2},{5,3},{6,0},{7,1},{8,6},{9,7},{10,4},{11,5},{12,10},{13,11},... | collective-permute-start | bytes 393224 | tf_op jit(solution)/shard_map/ppermute | solution.py:326
  99.0 13.0 %collective-permute-start.32 = (bf16[128,512]{1,0:T(8,128)(2,1)S(1)}, bf16[128,512]{1,0:T(8,128)(2,1)S(1)}, u32[]{:S(2)}, u32[]{:S(2)}) collective-permute-start(bf16[128,512]{1,0:T(8,128)(2,1)S(1)} %get-tuple-element.96), channel_id=1, source_target_pairs={{4,1},{5,0},{6,3},{7,2},{8,5},{9,4},{10,7},{11,6},{12,9},{13,8},{1... | collective-permute-start | bytes 393224 | tf_op jit(solution)/shard_map/ppermute | solution.py:326
  100.3 13.9 %collective-permute-start.31 = (bf16[128,512]{1,0:T(8,128)(2,1)S(1)}, bf16[128,512]{1,0:T(8,128)(2,1)S(1)}, u32[]{:S(2)}, u32[]{:S(2)}) collective-permute-start(bf16[128,512]{1,0:T(8,128)(2,1)S(1)} %get-tuple-element.97), channel_id=1, source_target_pairs={{4,0},{5,1},{6,2},{7,3},{8,4},{9,5},{10,6},{11,7},{12,8},{13,9},{1... | collective-permute-start | bytes 393224 | tf_op jit(solution)/shard_map/ppermute | solution.py:326
  103.3 11.0 %collective-permute-start.26 = (bf16[128,512]{1,0:T(8,128)(2,1)S(1)}, bf16[128,512]{1,0:T(8,128)(2,1)S(1)}, u32[]{:S(2)}, u32[]{:S(2)}) collective-permute-start(bf16[128,512]{1,0:T(8,128)(2,1)S(1)} %get-tuple-element.102), channel_id=1, source_target_pairs={{0,3},{1,2},{2,1},{3,0},{4,7},{5,6},{6,5},{7,4},{8,11},{9,10},{10,... | collective-permute-start | bytes 393224 | tf_op jit(solution)/shard_map/ppermute | solution.py:314
  (15 other events, 101.2 us)

commit v6 on v5

--- a/solution.py
+++ b/solution.py
@@ -17,7 +17,6 @@
 DIRECT_OUT = (1,)
 STEPS = ("kv0", "kv1", "z0", "q0", "q1", "z1", "att0", "o0", "r0", "dx0", "att1", "o1", "dx1", "r1")
 GATES = {
-    "kv1": ("kv0",),
     "pack": ("kv0",),
     "q1": ("q0",),
     "r11": ("o0",),

time: 117 us -> 117 us (level)
  no operation moved by 1% of the time
where the time goes in v6:
time: 117 us
  waiting for transfers between devices  49.4 us (42%)
  starting transfers between devices  41.1 us (35%)
  Pallas kernels  22.6 us (19%)
  local copies, waits for them, and re-layouts  2.2 us (2%)
    ppermute x24, waiting for transfers between devices, swap(): lax.ppermute(pieces[m], axes, pairs[m])  25.8 us
    ppermute x7, starting transfers between devices, hop(): return lax.ppermute(array, axes, pairs)  19.7 us
    ppermute x7, waiting for transfers between devices, hop(): return lax.ppermute(array, axes, pairs)  16.6 us
    pallas_call x2, Pallas kernels, attention(): pl.pallas_call(functools.partial(attention_kernel, members, planes - 1, g...  16.5 us
    ppermute x24, starting transfers between devices, swap(): lax.ppermute(pieces[m], axes, pairs[m])  16.3 us
    ppermute x4, waiting for transfers between devices, hop_across(): return [lax.ppermute(pieces[m], axes, pairs[m]) for m in range(members)]  7.05 us
    ppermute x4, starting transfers between devices, hop_across(): return [lax.ppermute(pieces[m], axes, pairs[m]) for m in range(members)]  5.17 us
    pallas_call x2, Pallas kernels, unpack(): pl.pallas_call(functools.partial(unpack_kernel, chunks, members, group, h...  4.14 us
  transfers between devices with their start and end apart: 35, of which 19 were waited for; matrix products, arithmetic and copies ran while one was open for 1% of the time, Pallas kernels for 17%

profile of v6, /device:TPU:0, one launch (start us, length us, event | category | flops | bytes accessed | tf_op | source)
XLA Modules:
  0.0 116.9 jit_solution(14873144793478733606)
XLA Ops:
  4.2 2.6 %collective-permute-start.1 = (bf16[128,512]{1,0:T(8,128)(2,1)S(1)}, bf16[128,512]{1,0:T(8,128)(2,1)S(1)}, u32[]{:S(2)}, u32[]{:S(2)}) collective-permute-start(bf16[128,512]{1,0:T(8,128)(2,1)S(1)} %get-tuple-element.47), channel_id=1, source_target_pairs={{0,2},{1,3},{2,0},{3,1},{4,6},{5,7},{6,4},{7,5},{8,10},{9,11},{10,... | collective-permute-start | bytes 393224 | tf_op jit(solution)/shard_map/ppermute | solution.py:313
  6.8 4.3 %collective-permute-done.1 = bf16[128,512]{1,0:T(8,128)(2,1)S(1)} collective-permute-done((bf16[128,512]{1,0:T(8,128)(2,1)S(1)}, bf16[128,512]{1,0:T(8,128)(2,1)S(1)}, u32[]{:S(2)}, u32[]{:S(2)}) %collective-permute-start.1) | collective-permute-done | bytes 131104 | tf_op jit(solution)/shard_map/ppermute | solution.py:313
  11.1 2.3 %collective-permute-done.2 = bf16[128,512]{1,0:T(8,128)(2,1)S(1)} collective-permute-done((bf16[128,512]{1,0:T(8,128)(2,1)S(1)}, bf16[128,512]{1,0:T(8,128)(2,1)S(1)}, u32[]{:S(2)}, u32[]{:S(2)}) %collective-permute-start.2) | collective-permute-done | bytes 131104 | tf_op jit(solution)/shard_map/ppermute | solution.py:313
  13.4 3.7 %collective-permute-start.3 = (bf16[4,128,512]{2,1,0:T(8,128)(2,1)S(1)}, bf16[4,128,512]{2,1,0:T(8,128)(2,1)S(1)}, u32[]{:S(2)}, u32[]{:S(2)}) collective-permute-start(bf16[4,128,512]{2,1,0:T(8,128)(2,1)S(1)} %pad_maximum_fusion.refs_2_), channel_id=1, source_target_pairs={{0,4},{1,5},{2,6},{3,7},{4,8},{5,9},{6,10},{7,11},{8,12},{9,13},{1... | collective-permute-start | bytes 1572872 | tf_op jit(solution)/shard_map/ppermute | solution.py:317
  19.1 4.5 %collective-permute-done.12 = bf16[128,512]{1,0:T(8,128)(2,1)S(1)} collective-permute-done((bf16[128,512]{1,0:T(8,128)(2,1)S(1)}, bf16[128,512]{1,0:T(8,128)(2,1)S(1)}, u32[]{:S(2)}, u32[]{:S(2)}) %collective-permute-start.12) | collective-permute-done | bytes 131104 | tf_op jit(solution)/shard_map/ppermute | solution.py:313
  23.6 1.9 %collective-permute-done.13 = bf16[128,512]{1,0:T(8,128)(2,1)S(1)} collective-permute-done((bf16[128,512]{1,0:T(8,128)(2,1)S(1)}, bf16[128,512]{1,0:T(8,128)(2,1)S(1)}, u32[]{:S(2)}, u32[]{:S(2)}) %collective-permute-start.13) | collective-permute-done | bytes 131104 | tf_op jit(solution)/shard_map/ppermute | solution.py:313
  25.6 3.5 %collective-permute-start.14 = (bf16[4,128,512]{2,1,0:T(8,128)(2,1)S(1)}, bf16[4,128,512]{2,1,0:T(8,128)(2,1)S(1)}, u32[]{:S(2)}, u32[]{:S(2)}) collective-permute-start(bf16[4,128,512]{2,1,0:T(8,128)(2,1)S(1)} %pad_maximum_fusion.1.refs_2_), channel_id=1, source_target_pairs={{0,4},{1,5},{2,6},{3,7},{4,8},{5,9},{6,10},{7,11},{8,12},{9,13},{1... | collective-permute-start | bytes 1572872 | tf_op jit(solution)/shard_map/ppermute | solution.py:317
  29.1 4.1 %collective-permute-start.4 = (bf16[4,128,512]{2,1,0:T(8,128)(2,1)S(1)}, bf16[4,128,512]{2,1,0:T(8,128)(2,1)S(1)}, u32[]{:S(2)}, u32[]{:S(2)}) collective-permute-start(bf16[4,128,512]{2,1,0:T(8,128)(2,1)S(1)} %collective-permute-done.3.refs_1_), channel_id=1, source_target_pairs={{0,4},{1,5},{2,6},{3,7},{4,8},{5,9},{6,10},{7,11},{8,12},{9,13},{1... | collective-permute-start | bytes 1572872 | tf_op jit(solution)/shard_map/ppermute | solution.py:317
  36.2 5.0 %collective-permute-done.14.refs_1_ = bf16[4,128,512]{2,1,0:T(8,128)(2,1)S(1)} collective-permute-done((bf16[4,128,512]{2,1,0:T(8,128)(2,1)S(1)}, bf16[4,128,512]{2,1,0:T(8,128)(2,1)S(1)}, u32[]{:S(2)}, u32[]{:S(2)}) %collective-permute-start.14) | collective-permute-done | bytes 524320 | tf_op jit(solution)/shard_map/ppermute | solution.py:317
  41.2 4.4 %collective-permute-start.15 = (bf16[4,128,512]{2,1,0:T(8,128)(2,1)S(1)}, bf16[4,128,512]{2,1,0:T(8,128)(2,1)S(1)}, u32[]{:S(2)}, u32[]{:S(2)}) collective-permute-start(bf16[4,128,512]{2,1,0:T(8,128)(2,1)S(1)} %collective-permute-done.14.refs_1_), channel_id=1, source_target_pairs={{0,4},{1,5},{2,6},{3,7},{4,8},{5,9},{6,10},{7,11},{8,12},{9,13},{1... | collective-permute-start | bytes 1572872 | tf_op jit(solution)/shard_map/ppermute | solution.py:317
  45.7 2.6 %collective-permute-done.7.refs_6_ = bf16[128,1024]{1,0:T(8,128)(2,1)S(1)} collective-permute-done((bf16[128,1024]{1,0:T(8,128)(2,1)S(1)}, bf16[128,1024]{1,0:T(8,128)(2,1)S(1)}, u32[]{:S(2)}, u32[]{:S(2)}) %collective-permute-start.7) | collective-permute-done | bytes 262176 | tf_op jit(solution)/shard_map/ppermute | solution.py:313
  50.1 2.4 %collective-permute-done.4.refs_0_ = bf16[4,128,512]{2,1,0:T(8,128)(2,1)S(1)} collective-permute-done((bf16[4,128,512]{2,1,0:T(8,128)(2,1)S(1)}, bf16[4,128,512]{2,1,0:T(8,128)(2,1)S(1)}, u32[]{:S(2)}, u32[]{:S(2)}) %collective-permute-start.4) | collective-permute-done | bytes 524320 | tf_op jit(solution)/shard_map/ppermute | solution.py:317
  52.5 8.2 %attention.2 = (bf16[128,1024]{1,0:T(8,128)(2,1)S(1)}, bf16[128,1024]{1,0:T(8,128)(2,1)S(1)}, bf16[128,1024]{1,0:T(8,128)(2,1)S(1)}, bf16[128,1024]{1,0:T(8,128)...) custom-call(s32[2]{0:T(128)S(1)} %pad_add_fusion.info, ...), custom_call_target="tpu_custom_call" | custom-call | flops 3623878656 | bytes 5242880 | tf_op jit(solution)/shard_map/attention/pallas_call | solution.py:265
  64.2 8.2 %attention.3 = (bf16[128,1024]{1,0:T(8,128)(2,1)S(1)}, bf16[128,1024]{1,0:T(8,128)(2,1)S(1)}, bf16[128,1024]{1,0:T(8,128)(2,1)S(1)}, bf16[128,1024]{1,0:T(8,128)...) custom-call(s32[2]{0:T(128)S(1)} %pad_add_fusion.info, ...), custom_call_target="tpu_custom_call" | custom-call | flops 3623878656 | bytes 5242880 | tf_op jit(solution)/shard_map/attention/pallas_call | solution.py:265
  72.4 2.2 %collective-permute-done.10.refs_3_ = bf16[128,1024]{1,0:T(8,128)(2,1)S(1)} collective-permute-done((bf16[128,1024]{1,0:T(8,128)(2,1)S(1)}, bf16[128,1024]{1,0:T(8,128)(2,1)S(1)}, u32[]{:S(2)}, u32[]{:S(2)}) %collective-permute-start.10) | collective-permute-done | bytes 262176 | tf_op jit(solution)/shard_map/ppermute | solution.py:313
  76.0 1.7 %collective-permute-start.29 = (bf16[128,512]{1,0:T(8,128)(2,1)S(1)}, bf16[128,512]{1,0:T(8,128)(2,1)S(1)}, u32[]{:S(2)}, u32[]{:S(2)}) collective-permute-start(bf16[128,512]{1,0:T(8,128)(2,1)S(1)} %get-tuple-element.90), channel_id=1, source_target_pairs={{0,3},{1,2},{2,1},{3,0},{4,7},{5,6},{6,5},{7,4},{8,11},{9,10},{10,... | collective-permute-start | bytes 393224 | tf_op jit(solution)/shard_map/ppermute | solution.py:313
  82.6 2.0 %collective-permute-done.28.refs_6_ = bf16[128,512]{1,0:T(8,128)(2,1)S(1)} collective-permute-done((bf16[128,512]{1,0:T(8,128)(2,1)S(1)}, bf16[128,512]{1,0:T(8,128)(2,1)S(1)}, u32[]{:S(2)}, u32[]{:S(2)}) %collective-permute-start.28) | collective-permute-done | bytes 131104 | tf_op jit(solution)/shard_map/ppermute | solution.py:313
  85.2 6.6 %collective-permute-done.30 = bf16[4,128,512]{2,1,0:T(8,128)(2,1)S(1)} collective-permute-done((bf16[4,128,512]{2,1,0:T(8,128)(2,1)S(1)}, bf16[4,128,512]{2,1,0:T(8,128)(2,1)S(1)}, u32[]{:S(2)}, u32[]{:S(2)}) %collective-permute-start.30) | collective-permute-done | bytes 524320 | tf_op jit(solution)/shard_map/ppermute | solution.py:317
  93.2 3.2 %collective-permute-done.21.refs_7_ = bf16[128,1024]{1,0:T(8,128)(2,1)S(1)} collective-permute-done((bf16[128,1024]{1,0:T(8,128)(2,1)S(1)}, bf16[128,1024]{1,0:T(8,128)(2,1)S(1)}, u32[]{:S(2)}, u32[]{:S(2)}) %collective-permute-start.21) | collective-permute-done | bytes 262176 | tf_op jit(solution)/shard_map/ppermute | solution.py:313
  104.3 2.3 %collective-permute-done.34.refs_11_ = bf16[128,512]{1,0:T(8,128)(2,1)S(1)} collective-permute-done((bf16[128,512]{1,0:T(8,128)(2,1)S(1)}, bf16[128,512]{1,0:T(8,128)(2,1)S(1)}, u32[]{:S(2)}, u32[]{:S(2)}) %collective-permute-start.34) | collective-permute-done | bytes 131104 | tf_op jit(solution)/shard_map/ppermute | solution.py:325
  107.1 2.5 %collective-permute-done.33.refs_10_ = bf16[128,512]{1,0:T(8,128)(2,1)S(1)} collective-permute-done((bf16[128,512]{1,0:T(8,128)(2,1)S(1)}, bf16[128,512]{1,0:T(8,128)(2,1)S(1)}, u32[]{:S(2)}, u32[]{:S(2)}) %collective-permute-start.33) | collective-permute-done | bytes 131104 | tf_op jit(solution)/shard_map/ppermute | solution.py:325
  109.7 2.4 %unpack.2 = (bf16[128,4096]{1,0:T(8,128)(2,1)}, bf16[128,4096]{1,0:T(8,128)(2,1)}) custom-call(s32[2]{0:T(128)S(1)} %pad_add_fusion.info, bf16[128,1024]{1,0:T(8,128)(2,1)S(1)} %get-tuple-element.54.refs_0_, bf16[128,1024]{1,0:T(8,128)(2,1)S(1)} %collective-permute-done.8.refs_1_, bf16[128,1024]{1,0:T(8,128)(2,1)S(1)} %collective-permute-done.9.refs_2_, ...), custom_call_target="tpu_custom_call" | custom-call | tf_op jit(solution)/shard_map/unpack/pallas_call | solution.py:109
  112.0 2.2 %collective-permute-done.31.refs_8_ = bf16[128,512]{1,0:T(8,128)(2,1)S(1)} collective-permute-done((bf16[128,512]{1,0:T(8,128)(2,1)S(1)}, bf16[128,512]{1,0:T(8,128)(2,1)S(1)}, u32[]{:S(2)}, u32[]{:S(2)}) %collective-permute-start.31) | collective-permute-done | bytes 131104 | tf_op jit(solution)/shard_map/ppermute | solution.py:325
  115.1 1.8 %unpack.3 = (bf16[128,2048]{1,0:T(8,128)(2,1)}, bf16[128,2048]{1,0:T(8,128)(2,1)}) custom-call(s32[2]{0:T(128)S(1)} %pad_add_fusion.info, bf16[128,512]{1,0:T(8,128)(2,1)S(1)} %get-tuple-element.97.refs_0_, bf16[128,512]{1,0:T(8,128)(2,1)S(1)} %collective-permute-done.24.refs_1_, bf16[128,512]{1,0:T(8,128)(2,1)S(1)} %collective-permute-done.25.refs_2_, ...), custom_call_target="tpu_custom_call" | custom-call | tf_op jit(solution)/shard_map/unpack/pallas_call | solution.py:109
  (69 shorter events, 31.3 us)
Async XLA Ops:
  13.4 15.6 %collective-permute-start.3 = (bf16[4,128,512]{2,1,0:T(8,128)(2,1)S(1)}, bf16[4,128,512]{2,1,0:T(8,128)(2,1)S(1)}, u32[]{:S(2)}, u32[]{:S(2)}) collective-permute-start(bf16[4,128,512]{2,1,0:T(8,128)(2,1)S(1)} %pad_maximum_fusion.refs_2_), channel_id=1, source_target_pairs={{0,4},{1,5},{2,6},{3,7},{4,8},{5,9},{6,10},{7,11},{8,12},{9,13},{1... | collective-permute-start | bytes 1572872 | tf_op jit(solution)/shard_map/ppermute | solution.py:317
  25.6 15.7 %collective-permute-start.14 = (bf16[4,128,512]{2,1,0:T(8,128)(2,1)S(1)}, bf16[4,128,512]{2,1,0:T(8,128)(2,1)S(1)}, u32[]{:S(2)}, u32[]{:S(2)}) collective-permute-start(bf16[4,128,512]{2,1,0:T(8,128)(2,1)S(1)} %pad_maximum_fusion.1.refs_2_), channel_id=1, source_target_pairs={{0,4},{1,5},{2,6},{3,7},{4,8},{5,9},{6,10},{7,11},{8,12},{9,13},{1... | collective-permute-start | bytes 1572872 | tf_op jit(solution)/shard_map/ppermute | solution.py:317
  29.1 23.4 %collective-permute-start.4 = (bf16[4,128,512]{2,1,0:T(8,128)(2,1)S(1)}, bf16[4,128,512]{2,1,0:T(8,128)(2,1)S(1)}, u32[]{:S(2)}, u32[]{:S(2)}) collective-permute-start(bf16[4,128,512]{2,1,0:T(8,128)(2,1)S(1)} %collective-permute-done.3.refs_1_), channel_id=1, source_target_pairs={{0,4},{1,5},{2,6},{3,7},{4,8},{5,9},{6,10},{7,11},{8,12},{9,13},{1... | collective-permute-start | bytes 1572872 | tf_op jit(solution)/shard_map/ppermute | solution.py:317
  34.3 11.4 %collective-permute-start.5 = (bf16[128,1024]{1,0:T(8,128)(2,1)S(1)}, bf16[128,1024]{1,0:T(8,128)(2,1)S(1)}, u32[]{:S(2)}, u32[]{:S(2)}) collective-permute-start(bf16[128,1024]{1,0:T(8,128)(2,1)S(1)} %get-tuple-element.51), channel_id=1, source_target_pairs={{0,1},{1,0},{2,3},{3,2},{4,5},{5,4},{6,7},{7,6},{8,9},{9,8},{10,11... | collective-permute-start | bytes 786440 | tf_op jit(solution)/shard_map/ppermute | solution.py:313
  34.4 11.3 %collective-permute-start.6 = (bf16[128,1024]{1,0:T(8,128)(2,1)S(1)}, bf16[128,1024]{1,0:T(8,128)(2,1)S(1)}, u32[]{:S(2)}, u32[]{:S(2)}) collective-permute-start(bf16[128,1024]{1,0:T(8,128)(2,1)S(1)} %get-tuple-element.52), channel_id=1, source_target_pairs={{0,2},{1,3},{2,0},{3,1},{4,6},{5,7},{6,4},{7,5},{8,10},{9,11},{10,... | collective-permute-start | bytes 786440 | tf_op jit(solution)/shard_map/ppermute | solution.py:313
  35.9 12.3 %collective-permute-start.7 = (bf16[128,1024]{1,0:T(8,128)(2,1)S(1)}, bf16[128,1024]{1,0:T(8,128)(2,1)S(1)}, u32[]{:S(2)}, u32[]{:S(2)}) collective-permute-start(bf16[128,1024]{1,0:T(8,128)(2,1)S(1)} %get-tuple-element.53), channel_id=1, source_target_pairs={{0,3},{1,2},{2,1},{3,0},{4,7},{5,6},{6,5},{7,4},{8,11},{9,10},{10,... | collective-permute-start | bytes 786440 | tf_op jit(solution)/shard_map/ppermute | solution.py:313
  41.2 22.9 %collective-permute-start.15 = (bf16[4,128,512]{2,1,0:T(8,128)(2,1)S(1)}, bf16[4,128,512]{2,1,0:T(8,128)(2,1)S(1)}, u32[]{:S(2)}, u32[]{:S(2)}) collective-permute-start(bf16[4,128,512]{2,1,0:T(8,128)(2,1)S(1)} %collective-permute-done.14.refs_1_), channel_id=1, source_target_pairs={{0,4},{1,5},{2,6},{3,7},{4,8},{5,9},{6,10},{7,11},{8,12},{9,13},{1... | collective-permute-start | bytes 1572872 | tf_op jit(solution)/shard_map/ppermute | solution.py:317
  48.3 12.5 %collective-permute-start.16 = (bf16[128,1024]{1,0:T(8,128)(2,1)S(1)}, bf16[128,1024]{1,0:T(8,128)(2,1)S(1)}, u32[]{:S(2)}, u32[]{:S(2)}) collective-permute-start(bf16[128,1024]{1,0:T(8,128)(2,1)S(1)} %get-tuple-element.67), channel_id=1, source_target_pairs={{0,1},{1,0},{2,3},{3,2},{4,5},{5,4},{6,7},{7,6},{8,9},{9,8},{10,11... | collective-permute-start | bytes 786440 | tf_op jit(solution)/shard_map/ppermute | solution.py:313
  48.5 13.8 %collective-permute-start.17 = (bf16[128,1024]{1,0:T(8,128)(2,1)S(1)}, bf16[128,1024]{1,0:T(8,128)(2,1)S(1)}, u32[]{:S(2)}, u32[]{:S(2)}) collective-permute-start(bf16[128,1024]{1,0:T(8,128)(2,1)S(1)} %get-tuple-element.68), channel_id=1, source_target_pairs={{0,2},{1,3},{2,0},{3,1},{4,6},{5,7},{6,4},{7,5},{8,10},{9,11},{10,... | collective-permute-start | bytes 786440 | tf_op jit(solution)/shard_map/ppermute | solution.py:313
  50.0 12.6 %collective-permute-start.18 = (bf16[128,1024]{1,0:T(8,128)(2,1)S(1)}, bf16[128,1024]{1,0:T(8,128)(2,1)S(1)}, u32[]{:S(2)}, u32[]{:S(2)}) collective-permute-start(bf16[128,1024]{1,0:T(8,128)(2,1)S(1)} %get-tuple-element.69), channel_id=1, source_target_pairs={{0,3},{1,2},{2,1},{3,0},{4,7},{5,6},{6,5},{7,4},{8,11},{9,10},{10,... | collective-permute-start | bytes 786440 | tf_op jit(solution)/shard_map/ppermute | solution.py:313
  60.7 11.7 %collective-permute-start.8 = (bf16[128,1024]{1,0:T(8,128)(2,1)S(1)}, bf16[128,1024]{1,0:T(8,128)(2,1)S(1)}, u32[]{:S(2)}, u32[]{:S(2)}) collective-permute-start(bf16[128,1024]{1,0:T(8,128)(2,1)S(1)} %get-tuple-element.55), channel_id=1, source_target_pairs={{0,1},{1,0},{2,3},{3,2},{4,5},{5,4},{6,7},{7,6},{8,9},{9,8},{10,11... | collective-permute-start | bytes 786440 | tf_op jit(solution)/shard_map/ppermute | solution.py:313
  60.8 11.6 %collective-permute-start.9 = (bf16[128,1024]{1,0:T(8,128)(2,1)S(1)}, bf16[128,1024]{1,0:T(8,128)(2,1)S(1)}, u32[]{:S(2)}, u32[]{:S(2)}) collective-permute-start(bf16[128,1024]{1,0:T(8,128)(2,1)S(1)} %get-tuple-element.56), channel_id=1, source_target_pairs={{0,2},{1,3},{2,0},{3,1},{4,6},{5,7},{6,4},{7,5},{8,10},{9,11},{10,... | collective-permute-start | bytes 786440 | tf_op jit(solution)/shard_map/ppermute | solution.py:313
  62.4 12.3 %collective-permute-start.10 = (bf16[128,1024]{1,0:T(8,128)(2,1)S(1)}, bf16[128,1024]{1,0:T(8,128)(2,1)S(1)}, u32[]{:S(2)}, u32[]{:S(2)}) collective-permute-start(bf16[128,1024]{1,0:T(8,128)(2,1)S(1)} %get-tuple-element.57), channel_id=1, source_target_pairs={{0,3},{1,2},{2,1},{3,0},{4,7},{5,6},{6,5},{7,4},{8,11},{9,10},{10,... | collective-permute-start | bytes 786440 | tf_op jit(solution)/shard_map/ppermute | solution.py:313
  62.7 16.8 %collective-permute-start.22 = (bf16[4,128,512]{2,1,0:T(8,128)(2,1)S(1)}, bf16[4,128,512]{2,1,0:T(8,128)(2,1)S(1)}, u32[]{:S(2)}, u32[]{:S(2)}) collective-permute-start(bf16[4,128,512]{2,1,0:T(8,128)(2,1)S(1)} %get-tuple-element.76), channel_id=1, source_target_pairs={{4,0},{5,1},{6,2},{7,3},{8,4},{9,5},{10,6},{11,7},{12,8},{13,9},{1... | collective-permute-start | bytes 1572872 | tf_op jit(solution)/shard_map/ppermute | solution.py:317
  74.7 17.1 %collective-permute-start.30 = (bf16[4,128,512]{2,1,0:T(8,128)(2,1)S(1)}, bf16[4,128,512]{2,1,0:T(8,128)(2,1)S(1)}, u32[]{:S(2)}, u32[]{:S(2)}) collective-permute-start(bf16[4,128,512]{2,1,0:T(8,128)(2,1)S(1)} %get-tuple-element.81), channel_id=1, source_target_pairs={{4,0},{5,1},{6,2},{7,3},{8,4},{9,5},{10,6},{11,7},{12,8},{13,9},{1... | collective-permute-start | bytes 1572872 | tf_op jit(solution)/shard_map/ppermute | solution.py:317
  79.6 23.4 %collective-permute-start.23 = (bf16[4,128,512]{2,1,0:T(8,128)(2,1)S(1)}, bf16[4,128,512]{2,1,0:T(8,128)(2,1)S(1)}, u32[]{:S(2)}, u32[]{:S(2)}) collective-permute-start(bf16[4,128,512]{2,1,0:T(8,128)(2,1)S(1)} %add_convert_fusion.2), channel_id=1, source_target_pairs={{4,0},{5,1},{6,2},{7,3},{8,4},{9,5},{10,6},{11,7},{12,8},{13,9},{1... | collective-permute-start | bytes 1572872 | tf_op jit(solution)/shard_map/ppermute | solution.py:317
  80.9 12.2 %collective-permute-start.19 = (bf16[128,1024]{1,0:T(8,128)(2,1)S(1)}, bf16[128,1024]{1,0:T(8,128)(2,1)S(1)}, u32[]{:S(2)}, u32[]{:S(2)}) collective-permute-start(bf16[128,1024]{1,0:T(8,128)(2,1)S(1)} %get-tuple-element.71), channel_id=1, source_target_pairs={{0,1},{1,0},{2,3},{3,2},{4,5},{5,4},{6,7},{7,6},{8,9},{9,8},{10,11... | collective-permute-start | bytes 786440 | tf_op jit(solution)/shard_map/ppermute | solution.py:313
  81.6 11.6 %collective-permute-start.20 = (bf16[128,1024]{1,0:T(8,128)(2,1)S(1)}, bf16[128,1024]{1,0:T(8,128)(2,1)S(1)}, u32[]{:S(2)}, u32[]{:S(2)}) collective-permute-start(bf16[128,1024]{1,0:T(8,128)(2,1)S(1)} %get-tuple-element.72), channel_id=1, source_target_pairs={{0,2},{1,3},{2,0},{3,1},{4,6},{5,7},{6,4},{7,5},{8,10},{9,11},{10,... | collective-permute-start | bytes 786440 | tf_op jit(solution)/shard_map/ppermute | solution.py:313
  84.7 11.7 %collective-permute-start.21 = (bf16[128,1024]{1,0:T(8,128)(2,1)S(1)}, bf16[128,1024]{1,0:T(8,128)(2,1)S(1)}, u32[]{:S(2)}, u32[]{:S(2)}) collective-permute-start(bf16[128,1024]{1,0:T(8,128)(2,1)S(1)} %get-tuple-element.73), channel_id=1, source_target_pairs={{0,3},{1,2},{2,1},{3,0},{4,7},{5,6},{6,5},{7,4},{8,11},{9,10},{10,... | collective-permute-start | bytes 786440 | tf_op jit(solution)/shard_map/ppermute | solution.py:313
  96.4 10.2 %collective-permute-start.34 = (bf16[128,512]{1,0:T(8,128)(2,1)S(1)}, bf16[128,512]{1,0:T(8,128)(2,1)S(1)}, u32[]{:S(2)}, u32[]{:S(2)}) collective-permute-start(bf16[128,512]{1,0:T(8,128)(2,1)S(1)} %get-tuple-element.86), channel_id=1, source_target_pairs={{4,3},{5,2},{6,1},{7,0},{8,7},{9,6},{10,5},{11,4},{12,11},{13,10},... | collective-permute-start | bytes 393224 | tf_op jit(solution)/shard_map/ppermute | solution.py:325
  97.7 11.9 %collective-permute-start.33 = (bf16[128,512]{1,0:T(8,128)(2,1)S(1)}, bf16[128,512]{1,0:T(8,128)(2,1)S(1)}, u32[]{:S(2)}, u32[]{:S(2)}) collective-permute-start(bf16[128,512]{1,0:T(8,128)(2,1)S(1)} %get-tuple-element.87), channel_id=1, source_target_pairs={{4,2},{5,3},{6,0},{7,1},{8,6},{9,7},{10,4},{11,5},{12,10},{13,11},... | collective-permute-start | bytes 393224 | tf_op jit(solution)/shard_map/ppermute | solution.py:325
  99.0 13.0 %collective-permute-start.32 = (bf16[128,512]{1,0:T(8,128)(2,1)S(1)}, bf16[128,512]{1,0:T(8,128)(2,1)S(1)}, u32[]{:S(2)}, u32[]{:S(2)}) collective-permute-start(bf16[128,512]{1,0:T(8,128)(2,1)S(1)} %get-tuple-element.88), channel_id=1, source_target_pairs={{4,1},{5,0},{6,3},{7,2},{8,5},{9,4},{10,7},{11,6},{12,9},{13,8},{1... | collective-permute-start | bytes 393224 | tf_op jit(solution)/shard_map/ppermute | solution.py:325
  100.3 13.9 %collective-permute-start.31 = (bf16[128,512]{1,0:T(8,128)(2,1)S(1)}, bf16[128,512]{1,0:T(8,128)(2,1)S(1)}, u32[]{:S(2)}, u32[]{:S(2)}) collective-permute-start(bf16[128,512]{1,0:T(8,128)(2,1)S(1)} %get-tuple-element.89), channel_id=1, source_target_pairs={{4,0},{5,1},{6,2},{7,3},{8,4},{9,5},{10,6},{11,7},{12,8},{13,9},{1... | collective-permute-start | bytes 393224 | tf_op jit(solution)/shard_map/ppermute | solution.py:325
  103.3 11.0 %collective-permute-start.26 = (bf16[128,512]{1,0:T(8,128)(2,1)S(1)}, bf16[128,512]{1,0:T(8,128)(2,1)S(1)}, u32[]{:S(2)}, u32[]{:S(2)}) collective-permute-start(bf16[128,512]{1,0:T(8,128)(2,1)S(1)} %get-tuple-element.94), channel_id=1, source_target_pairs={{0,3},{1,2},{2,1},{3,0},{4,7},{5,6},{6,5},{7,4},{8,11},{9,10},{10,... | collective-permute-start | bytes 393224 | tf_op jit(solution)/shard_map/ppermute | solution.py:313
  (15 other events, 101.2 us)
